TPU v7x, 32 devices: a whole 2x2x4 slice. The times are simulated.
32 devices in a mesh: section: 2 (over core), dp: 16 (over z, y, x).
Axes of the slice: x: 2, y: 2, z: 4, core: 2. Of those that a mesh axis runs over, the one named last changes fastest.
Arguments:
- token_ids: int32 [32, 224], P('dp'), may hold values from 0 to 50303
- seg_lengths: int32 [32, 5], P('dp'), may hold values from 1 to 112, 224 in all within a row
- rankings: int32 [32, 4], P('dp'), may hold values from 0 to 3, each once within a row
- table: float32 [1024, 50304], P('dp'), may hold values from -0.6 to 0.6
- table_m: float32 [1024, 50304], P('dp'), may hold values from -3.8146973e-06 to 3.8146973e-06
- table_v: float32 [1024, 50304], P('dp'), may hold values from 1.720838e-12 to 6.8572786e-12
- table_ema: float32 [1024, 50304], P('dp'), may hold values from -0.625 to 0.625
- in_w: float32 [2, 1024, 7168], P('section', 'dp'), may hold values from -0.1875 to 0.1875
- in_m: float32 [2, 1024, 7168], P('section', 'dp'), may hold values from -3.8146973e-06 to 3.8146973e-06
- in_v: float32 [2, 1024, 7168], P('section', 'dp'), may hold values from 1.720838e-12 to 6.8572786e-12
- in_ema: float32 [2, 1024, 7168], P('section', 'dp'), may hold values from -0.1875 to 0.1875
- out_w: float32 [2, 5120, 1024], P('section', 'dp'), may hold values from -0.75 to 0.75
- out_m: float32 [2, 5120, 1024], P('section', 'dp'), may hold values from -3.8146973e-06 to 3.8146973e-06
- out_v: float32 [2, 5120, 1024], P('section', 'dp'), may hold values from 1.720838e-12 to 6.8572786e-12
- out_ema: float32 [2, 5120, 1024], P('section', 'dp'), may hold values from -0.1875 to 0.1875
- layer_vec: float32 [2, 13312], P('section', 'dp'), may hold values from -1.2 to 2.6
- vec_m: float32 [2, 13312], P('section', 'dp'), may hold values from -1.5258789e-05 to 1.5258789e-05
- vec_v: float32 [2, 13312], P('section', 'dp'), may hold values from 2.7376967e-11 to 1.0950787e-10
- vec_ema: float32 [2, 13312], P('section', 'dp'), may hold values from -3 to 3
- final_vec: float32 [3072], P('dp'), may hold values from -1.5 to 1.5
- final_m: float32 [3072], P('dp'), may hold values from -1.9073486e-05 to 1.9073486e-05
- final_v: float32 [3072], P('dp'), may hold values from 5.21466045e-11 to 2.08586418e-10
- final_ema: float32 [3072], P('dp'), may hold values from -1.5 to 1.5
Outputs:
- loss_sum: float32 [], replicated
- grad_norm: float32 [], replicated
- table_new: float32 [1024, 50304], P('dp')
- table_m_new: float32 [1024, 50304], P('dp')
- table_v_new: float32 [1024, 50304], P('dp')
- table_ema_new: float32 [1024, 50304], P('dp')
- in_new: float32 [2, 1024, 7168], P('section', 'dp')
- in_m_new: float32 [2, 1024, 7168], P('section', 'dp')
- in_v_new: float32 [2, 1024, 7168], P('section', 'dp')
- in_ema_new: float32 [2, 1024, 7168], P('section', 'dp')
- out_new: float32 [2, 5120, 1024], P('section', 'dp')
- out_m_new: float32 [2, 5120, 1024], P('section', 'dp')
- out_v_new: float32 [2, 5120, 1024], P('section', 'dp')
- out_ema_new: float32 [2, 5120, 1024], P('section', 'dp')
- vec_new: float32 [2, 13312], P('section', 'dp')
- vec_m_new: float32 [2, 13312], P('section', 'dp')
- vec_v_new: float32 [2, 13312], P('section', 'dp')
- vec_ema_new: float32 [2, 13312], P('section', 'dp')
- final_new: float32 [3072], P('dp')
- final_m_new: float32 [3072], P('dp')
- final_v_new: float32 [3072], P('dp')
- final_ema_new: float32 [3072], P('dp')
Inputs may be any that keep to these rules, and one draw needn't show every extreme that they name: `seg_lengths`: row i holds the prompt length of list i and then its 4 continuation lengths, all at least 1; each row sums to 224, and its largest entry is 112. `rankings`: each row is a permutation of 0 to 3.
All inputs are finite; a program needn't handle non-finite values.
Results may differ from a plain program's by a relative error of at most 0.029.
The roundings to bfloat16 on the way count: a program that leaves them out, or rounds other values in their place, can miss the bound.
Values may be sent and summed in bfloat16 or wider, within the bound.
No kernel may reach another device: no remote copies, remote signals or barrier semaphores. Data moves between devices by JAX's collectives and lax.ppermute only.
A program may use at most 448 MiB of HBM per device.

v0:
```python
import jax
import jax.numpy as jnp
from jax import lax
from jax.sharding import PartitionSpec as P

D = 1024
HEADS = 16
HEAD_DIM = 64
FF = 4096
ROT = 16
STEP = 10


EPS_NORM = 1e-05
CLIP_NORM = 0.05
BETA_ONE = 0.9
BETA_TWO = 0.95
ADAM_EPS = 1e-08
RATE_MAT = 0.1
RATE_VEC = 0.3
WEIGHT_DECAY = 0.1
EMA_KEEP = 0.75
MASKED = -1e30


def shifted(value, axis, steps):
    count = lax.axis_size(axis)
    first, last = (max(0, -steps), min(count, count - steps))
    return lax.ppermute(value, axis, [(source, source + steps) for source in range(first, last)])


def matmul(left_operand, right_operand):
    return jnp.dot(left_operand, right_operand, preferred_element_type=jnp.float32)


def dot_rows(left_operand, right_operand):
    return lax.dot_general(
        left_operand, right_operand, (((0,), (0,)), ((), ())), preferred_element_type=jnp.float32
    )


def dot_cols(left_operand, right_operand):
    return lax.dot_general(
        left_operand, right_operand, (((1,), (1,)), ((), ())), preferred_element_type=jnp.float32
    )


def standard_deviation(value_rows):
    center = value_rows - jnp.mean(value_rows, -1, keepdims=True)
    scale_factor = lax.rsqrt(jnp.mean(center * center, -1, keepdims=True) + EPS_NORM)
    return (center * scale_factor, scale_factor)


def norm_gradient_pass(gradient_normalized, input_normalized, scale_factor):
    return scale_factor * (
        gradient_normalized
        - jnp.mean(gradient_normalized, -1, keepdims=True)
        - input_normalized * jnp.mean(gradient_normalized * input_normalized, -1, keepdims=True)
    )


def layout(lengths, width):
    bounds = jnp.cumsum(lengths)
    starts = bounds - lengths
    places = jnp.arange(width, dtype=jnp.int32)
    segment = jnp.sum((places[:, None] >= bounds[None, :]).astype(jnp.int32), 1)
    pieces_count = lengths.shape[0]
    owner = jnp.minimum(segment, pieces_count - 1)
    chosen = jnp.arange(pieces_count, dtype=jnp.int32)[None, :] == owner[:, None]
    begin = jnp.sum(jnp.where(chosen, starts[None, :], 0), 1)
    position = places - begin + jnp.where(segment > 0, lengths[0], 0)
    same = (segment[:, None] == segment[None, :]) & (places[None, :] <= places[:, None])
    prompt = (segment[None, :] == 0) & (segment[:, None] > 0) & (segment[:, None] < pieces_count)
    return (position, same | prompt, bounds[1:] - 1)


def angles(position):
    half = ROT // 2
    freqs = 10000.0 ** (-2.0 * jnp.arange(half, dtype=jnp.float32) / ROT)
    phase = position.astype(jnp.float32)[:, None] * freqs[None, :]
    return (jnp.cos(phase)[:, None, :], jnp.sin(phase)[:, None, :])


def turn(value_rows, cosine, sine, sign):
    half = cosine.shape[-1]
    first = value_rows[..., :half]
    second = value_rows[..., half : 2 * half]
    return jnp.concatenate(
        [
            first * cosine - sign * second * sine,
            second * cosine + sign * first * sine,
            value_rows[..., 2 * half :],
        ],
        -1,
    )


def pieces(vector):
    amounts = [D, D, D, D, 3 * D, D, FF, D]
    parts = []
    offset = 0
    for amount in amounts:
        parts.append(vector[offset : offset + amount])
        offset = offset + amount
    return parts


def gelu_slope(value_rows):
    cumulative = 0.5 * (1.0 + jax.scipy.special.erf(value_rows * 0.7071067811865476))
    return cumulative + value_rows * jnp.exp(-0.5 * value_rows * value_rows) * 0.3989422804014327


def scores_of(query_rows, key_rows, allowed):
    raw = jnp.einsum(
        "qhe,khe->hqk", query_rows, key_rows, preferred_element_type=jnp.float32
    ) * HEAD_DIM ** (-0.5)
    return jnp.where(allowed[None], raw, MASKED)


def layer_forward(residual_state, w_in, w_out, vector, cosine, sine, allowed):
    rows = residual_state.shape[0]
    first_gain, first_bias, second_gain, second_bias, bias_qkv, bias_attn, bias_up, bias_down = (
        pieces(vector.astype(jnp.float32))
    )
    input_normalized, scale_factor = standard_deviation(residual_state)
    left_operand = (input_normalized * first_gain + first_bias).astype(jnp.bfloat16)
    right_operand = (input_normalized * second_gain + second_bias).astype(jnp.bfloat16)
    joined = matmul(left_operand, w_in[:, : 3 * D]) + bias_qkv
    upper_projection = matmul(right_operand, w_in[:, 3 * D :]) + bias_up
    query_rows = turn(joined[:, :D].reshape(rows, HEADS, HEAD_DIM), cosine, sine, 1.0).astype(
        jnp.bfloat16
    )
    key_rows = turn(joined[:, D : 2 * D].reshape(rows, HEADS, HEAD_DIM), cosine, sine, 1.0).astype(
        jnp.bfloat16
    )
    value_rows = joined[:, 2 * D :].reshape(rows, HEADS, HEAD_DIM).astype(jnp.bfloat16)
    scores = scores_of(query_rows, key_rows, allowed)
    top_score = jnp.max(scores, -1, keepdims=True)
    powers = jnp.exp(scores - top_score)
    total_value = jnp.sum(powers, -1, keepdims=True)
    weights = (powers / total_value).astype(jnp.bfloat16)
    mixed_output = (
        jnp.einsum("hqk,khe->qhe", weights, value_rows, preferred_element_type=jnp.float32)
        .reshape(rows, D)
        .astype(jnp.bfloat16)
    )
    active_flags = jax.nn.gelu(upper_projection, approximate=False).astype(jnp.bfloat16)
    branch = (
        matmul(mixed_output, w_out[:D]) + bias_attn + (matmul(active_flags, w_out[D:]) + bias_down)
    )
    kept_entries = (
        input_normalized,
        scale_factor,
        upper_projection,
        query_rows,
        key_rows,
        value_rows,
        top_score + jnp.log(total_value),
        mixed_output,
        active_flags,
    )
    return (residual_state + branch, kept_entries)


def layer_backward(gradient_value, kept_entries, w_in, w_out, vector, cosine, sine, allowed):
    (
        input_normalized,
        scale_factor,
        upper_projection,
        query_rows,
        key_rows,
        value_rows,
        log_sum_exp,
        mixed_output,
        active_flags,
    ) = kept_entries
    rows = gradient_value.shape[0]
    first_gain, first_bias, second_gain, second_bias = pieces(vector.astype(jnp.float32))[:4]
    branch = gradient_value.astype(jnp.bfloat16)
    branch_sum = jnp.sum(branch.astype(jnp.float32), 0)
    grad_mixed = dot_cols(branch, w_out[:D]).astype(jnp.bfloat16).reshape(rows, HEADS, HEAD_DIM)
    grad_upper = (dot_cols(branch, w_out[D:]) * gelu_slope(upper_projection)).astype(jnp.bfloat16)
    weights = jnp.exp(scores_of(query_rows, key_rows, allowed) - log_sum_exp)
    grad_weights = jnp.einsum(
        "qhe,khe->hqk", grad_mixed, value_rows, preferred_element_type=jnp.float32
    )
    grad_scores = (
        weights * (grad_weights - jnp.sum(weights * grad_weights, -1, keepdims=True))
    ).astype(jnp.bfloat16)
    grad_values = jnp.einsum(
        "hqk,qhe->khe", weights.astype(jnp.bfloat16), grad_mixed, preferred_element_type=jnp.float32
    )
    factor = HEAD_DIM ** (-0.5)
    grad_query = (
        jnp.einsum("hqk,khe->qhe", grad_scores, key_rows, preferred_element_type=jnp.float32)
        * factor
    )
    grad_keys = (
        jnp.einsum("hqk,qhe->khe", grad_scores, query_rows, preferred_element_type=jnp.float32)
        * factor
    )
    grad_joined = jnp.concatenate(
        [
            turn(grad_query, cosine, sine, -1.0).reshape(rows, D),
            turn(grad_keys, cosine, sine, -1.0).reshape(rows, D),
            grad_values.reshape(rows, D),
        ],
        1,
    ).astype(jnp.bfloat16)
    left_operand = (input_normalized * first_gain + first_bias).astype(jnp.bfloat16)
    right_operand = (input_normalized * second_gain + second_bias).astype(jnp.bfloat16)
    gradient_left_side = dot_cols(grad_joined, w_in[:, : 3 * D])
    gradient_right_side = dot_cols(grad_upper, w_in[:, 3 * D :])
    grad_vector = jnp.concatenate(
        [
            jnp.sum(gradient_left_side * input_normalized, 0),
            jnp.sum(gradient_left_side, 0),
            jnp.sum(gradient_right_side * input_normalized, 0),
            jnp.sum(gradient_right_side, 0),
            jnp.sum(grad_joined.astype(jnp.float32), 0),
            branch_sum,
            jnp.sum(grad_upper.astype(jnp.float32), 0),
            branch_sum,
        ]
    )
    gradient_residual = gradient_value + norm_gradient_pass(
        gradient_left_side * first_gain + gradient_right_side * second_gain,
        input_normalized,
        scale_factor,
    )
    factors = (
        left_operand,
        grad_joined,
        right_operand,
        grad_upper,
        jnp.concatenate([mixed_output, active_flags], 1),
        branch,
    )
    return (gradient_residual, grad_vector, factors)


def plackett(scores, ranking):
    ordered = scores[ranking]
    count = ordered.shape[0]
    later = jnp.arange(count)[None, :] >= jnp.arange(count)[:, None]
    grid = jnp.where(later, ordered[None, :], MASKED)
    top_score = jnp.max(grid, 1, keepdims=True)
    tails = top_score[:, 0] + jnp.log(jnp.sum(jnp.exp(grid - top_score), 1))
    return jnp.sum(tails - ordered)


def head_backward(residual_state, final, ranking, final_position, valid):
    gain_vector, bias_vector, weight = (final[:D], final[D : 2 * D], final[2 * D :])
    input_normalized, scale_factor = standard_deviation(residual_state[final_position])
    selected_entries = (
        (input_normalized * gain_vector + bias_vector).astype(jnp.bfloat16).astype(jnp.float32)
    )
    scores = jnp.sum(selected_entries * weight, -1)
    loss, pull = jax.vjp(lambda given: plackett(given, ranking), scores)
    (grad_scores,) = pull(valid)
    gradient_selected = grad_scores[:, None] * weight
    grad_final = jnp.concatenate(
        [
            jnp.sum(gradient_selected * input_normalized, 0),
            jnp.sum(gradient_selected, 0),
            jnp.sum(grad_scores[:, None] * selected_entries, 0),
        ]
    )
    gradient_row_values = norm_gradient_pass(
        gradient_selected * gain_vector, input_normalized, scale_factor
    )
    gradient_residual = jnp.zeros_like(residual_state).at[final_position].add(gradient_row_values)
    return (loss * valid, gradient_residual, grad_final)


def pass_forward(value):
    return shifted(value, "section", 1)


def pass_backward(value):
    return shifted(value, "section", -1)


def adamw_update(weight, moment, second, average, gradient_value, rate, decay):
    moment_new = BETA_ONE * moment + (1.0 - BETA_ONE) * gradient_value
    second_new = BETA_TWO * second + (1.0 - BETA_TWO) * gradient_value * gradient_value
    moment_hat = moment_new / (1.0 - BETA_ONE**STEP)
    second_hat = second_new / (1.0 - BETA_TWO**STEP)
    weight_new = weight - rate * (moment_hat / (jnp.sqrt(second_hat) + ADAM_EPS) + decay * weight)
    average_new = EMA_KEEP * average + (1.0 - EMA_KEEP) * weight_new
    return (weight_new, moment_new, second_new, average_new)


def body(
    token_ids,
    seg_lengths,
    rankings,
    table,
    table_m,
    table_v,
    table_ema,
    in_w,
    in_m,
    in_v,
    in_ema,
    out_w,
    out_m,
    out_v,
    out_ema,
    layer_vec,
    vec_m,
    vec_v,
    vec_ema,
    final_vec,
    final_m,
    final_v,
    final_ema,
):
    micro = token_ids.shape[0]
    width = token_ids.shape[1]
    section_first = lax.axis_index("section") == 0
    first_section = section_first.astype(jnp.float32)
    later_section = 1.0 - first_section
    section_offset = 1 - section_first.astype(jnp.int32)
    w_in, w_out, vector, final = (
        lax.all_gather(in_w[0].astype(jnp.bfloat16), "dp", axis=0, tiled=True),
        lax.all_gather(out_w[0].astype(jnp.bfloat16), "dp", axis=0, tiled=True),
        lax.all_gather(layer_vec[0].astype(jnp.bfloat16), "dp", axis=0, tiled=True),
        lax.all_gather(final_vec.astype(jnp.bfloat16), "dp", axis=0, tiled=True),
    )
    final = final.astype(jnp.float32)
    every_ids = lax.all_gather(token_ids, "dp", axis=0, tiled=True).reshape(-1)
    selected_entries = jnp.take(table, every_ids, axis=1).astype(jnp.bfloat16)
    features = lax.all_to_all(selected_entries, "dp", split_axis=1, concat_axis=0, tiled=True)
    embedded = features.T.astype(jnp.float32).reshape(micro, width, D)
    received = jnp.zeros((width, D), jnp.float32)
    output = received
    caches = []
    geometry = []
    head_grads = []
    loss_local = jnp.zeros((), jnp.float32)
    grad_final = jnp.zeros((3 * D,), jnp.float32)
    for tick in range(micro + 1):
        if tick > 0:
            received = pass_forward(output.astype(jnp.bfloat16)).astype(jnp.float32)
        residual_state = received + first_section * embedded[tick] if tick < micro else received
        which = jnp.clip(tick - section_offset, 0, micro - 1)
        position, allowed, final_position = layout(seg_lengths[which], width)
        cosine, sine = angles(position)
        output, kept_entries = layer_forward(
            residual_state, w_in, w_out, vector, cosine, sine, allowed
        )
        valid = later_section * (1.0 if tick > 0 else 0.0)
        loss_term, grad_head, grad_fin = head_backward(
            output, final, rankings[which], final_position, valid
        )
        loss_local = loss_local + loss_term
        grad_final = grad_final + grad_fin
        caches.append(kept_entries)
        geometry.append((cosine, sine, allowed))
        head_grads.append(grad_head)
    incoming = jnp.zeros((width, D), jnp.float32)
    gradient_residual = incoming
    embed_grads = [None] * micro
    sum_in = jnp.zeros((D, 3 * D + FF), jnp.float32)
    sum_out = jnp.zeros((D + FF, D), jnp.float32)
    sum_vec = jnp.zeros((9 * D + FF,), jnp.float32)
    for sweep in range(micro + 1):
        index = micro - sweep
        if sweep > 0:
            incoming = pass_backward(gradient_residual.astype(jnp.bfloat16)).astype(jnp.float32)
        cosine, sine, allowed = geometry[index]
        gradient_residual, grad_vec, factors = layer_backward(
            incoming + head_grads[index], caches[index], w_in, w_out, vector, cosine, sine, allowed
        )
        sum_vec = sum_vec + grad_vec
        if index < micro:
            embed_grads[index] = gradient_residual * first_section
        left_operand, grad_joined, right_operand, grad_upper, acts, branch = factors
        sum_in = sum_in + jnp.concatenate(
            [dot_rows(left_operand, grad_joined), dot_rows(right_operand, grad_upper)], 1
        )
        sum_out = sum_out + dot_rows(acts, branch)
    shard_in, shard_out, shard_vec, shard_fin = (
        lax.psum_scatter(sum_in, "dp", scatter_dimension=0, tiled=True),
        lax.psum_scatter(sum_out, "dp", scatter_dimension=0, tiled=True),
        lax.psum_scatter(sum_vec, "dp", scatter_dimension=0, tiled=True),
        lax.psum_scatter(grad_final, "dp", scatter_dimension=0, tiled=True),
    )
    stacked = jnp.stack(embed_grads).reshape(micro * width, D).astype(jnp.bfloat16).T
    spread = lax.all_to_all(stacked, "dp", split_axis=0, concat_axis=1, tiled=True)
    table_grad = (
        jnp.zeros(table.shape, jnp.float32).at[:, every_ids].add(spread.astype(jnp.float32))
    )
    table_grad, shard_fin = (
        lax.psum(table_grad.astype(jnp.bfloat16), "section").astype(jnp.float32),
        lax.psum(shard_fin.astype(jnp.bfloat16), "section").astype(jnp.float32),
    )
    squares = (
        jnp.sum(shard_in * shard_in)
        + jnp.sum(shard_out * shard_out)
        + jnp.sum(shard_vec * shard_vec)
        + first_section * (jnp.sum(table_grad * table_grad) + jnp.sum(shard_fin * shard_fin))
    )
    total_squares, loss_sum = lax.psum((squares, loss_local), ("section", "dp"))
    grad_norm = jnp.sqrt(total_squares)
    factor = jnp.minimum(1.0, CLIP_NORM / (grad_norm + 1e-06))
    table_parts = adamw_update(
        table, table_m, table_v, table_ema, table_grad * factor, RATE_MAT, WEIGHT_DECAY
    )
    in_parts = adamw_update(
        in_w, in_m, in_v, in_ema, shard_in.reshape(in_w.shape) * factor, RATE_MAT, WEIGHT_DECAY
    )
    out_parts = adamw_update(
        out_w,
        out_m,
        out_v,
        out_ema,
        shard_out.reshape(out_w.shape) * factor,
        RATE_MAT,
        WEIGHT_DECAY,
    )
    vec_parts = adamw_update(
        layer_vec, vec_m, vec_v, vec_ema, shard_vec.reshape(layer_vec.shape) * factor, RATE_VEC, 0.0
    )
    final_parts = adamw_update(
        final_vec, final_m, final_v, final_ema, shard_fin * factor, RATE_VEC, 0.0
    )
    return (loss_sum, grad_norm) + table_parts + in_parts + out_parts + vec_parts + final_parts


def solution(mesh):
    in_specs = (
        P("dp", None),
        P("dp", None),
        P("dp", None),
        P("dp", None),
        P("dp", None),
        P("dp", None),
        P("dp", None),
        P("section", "dp", None),
        P("section", "dp", None),
        P("section", "dp", None),
        P("section", "dp", None),
        P("section", "dp", None),
        P("section", "dp", None),
        P("section", "dp", None),
        P("section", "dp", None),
        P("section", "dp"),
        P("section", "dp"),
        P("section", "dp"),
        P("section", "dp"),
        P("dp"),
        P("dp"),
        P("dp"),
        P("dp"),
    )
    out_specs = (
        P(),
        P(),
        P("dp", None),
        P("dp", None),
        P("dp", None),
        P("dp", None),
        P("section", "dp", None),
        P("section", "dp", None),
        P("section", "dp", None),
        P("section", "dp", None),
        P("section", "dp", None),
        P("section", "dp", None),
        P("section", "dp", None),
        P("section", "dp", None),
        P("section", "dp"),
        P("section", "dp"),
        P("section", "dp"),
        P("section", "dp"),
        P("dp"),
        P("dp"),
        P("dp"),
        P("dp"),
    )
    return jax.shard_map(body, mesh=mesh, in_specs=in_specs, out_specs=out_specs, check_vma=False)
```

profile of v0, /device:TPU:0, one launch (start us, length us, event | category | flops | bytes accessed | tf_op | source)
XLA Modules:
  0.0 1881.0 jit_solution(13620073719798781006)
XLA Ops:
  10.9 43.0 %all-gather.3 = s32[16,2,224]{2,1,0:T(2,128)S(1)} all-gather(s32[1,2,224]{2,1,0:T(2,128)S(1)} %bitcast.360), channel_id=1, replica_groups=mesh['section'=2,'dp'=16] {'dp'}, dimensions={0}, use_global_device_ids=true | all-gather | bytes 30464 | tf_op jit(solution)/shard_map/all_gather | solution.py:332
  54.2 15.9 copy.269
  70.1 25.5 %gather_fusion = bf16[7168,64]{1,0:T(8,128)(2,1)S(1)} fusion(bf16[64,50304]{0,1:T(8,128)(2,1)} %copy.269, s32[7168]{0:T(1024)S(1)} %broadcast_clamp_fusion), kind=kCustom, calls=%fused_computation | custom fusion | bytes 1863680 | tf_op jit(solution)/shard_map/jit(_take)/gather | solution.py:333
  107.2 100.6 %all-reduce.6 = (bf16[3072]{0:T(1024)(128)(2,1)S(1)}, bf16[13312]{0:T(1024)(128)(2,1)S(1)}) all-reduce(bf16[3072]{0:T(1024)(128)(2,1)S(1)} %dynamic-update-slice.1, bf16[13312]{0:T(1024)(128)(2,1)S(1)} %dynamic-update-slice), channel_id=1, replica_groups=mesh['section'=2,'dp'=16] {'dp'}, use_global_device_ids=true, to_apply=%add.1 | all-reduce | flops 16384 | bytes 65536
  233.2 14.7 fusion.12
  247.9 87.2 %all-gather.9.cloned.1.call-done = bf16[1,5120,1024]{2,1,0:T(8,128)(2,1)} async-done(((bf16[1,320,1024]{2,1,0:T(8,128)(2,1)}), bf16[1,5120,1024]{2,1,0:T(8,128)(2,1)}) %all-gather.9.cloned.1.call-update) | async-done | bytes 10485776 | tf_op jit(solution)/shard_map/all_gather | solution.py:327
  355.6 13.2 fusion.15
  421.3 14.0 fusion.18
  576.7 31.1 %all_to_all.23 = bf16[16,64,448]{2,1,0:T(8,128)(2,1)S(1)} all-to-all(bf16[16,64,448]{2,1,0:T(8,128)(2,1)S(1)} %bitcast.276), channel_id=1, replica_groups=mesh['section'=2,'dp'=16] {'dp'}, dimensions={0} | all-to-all | bytes 1835008 | tf_op jit(solution)/shard_map/all_to_all | solution.py:391
  615.4 49.0 %scatter_custom_fusion.6 = f32[64,50304]{0,1:T(8,128)} fusion(s32[7168]{0:T(1024)} %bitcast.347, f32[7168,64]{1,0:T(8,128)} %copy.301, f32[]{:T(128)} %constant.73.clone.1), kind=kCustom, calls=%fused_computation.26 | custom fusion | flops 458752 | bytes 12878336 | tf_op jit(solution)/shard_map/scatter-add | solution.py:393
  664.4 16.3 copy.302
  684.1 12.1 fusion.79
  696.3 10.6 fusion.83
  706.9 23.2 %add_add_fusion = f32[5120,1024]{1,0:T(8,128)} fusion(f32[5120,1024]{1,0:T(8,128)} %fusion.79, f32[5120,1024]{1,0:T(8,128)} %fusion.83, bf16[224,1024]{1,0:T(8,128)(2,1)S(1)} %copy-done.75, bf16[224,4096]{1,0:T(8,128)(2,1)S(1)} %copy-done.71, bf16[224,1024]{1,0:T(8,128)(2,1)S(1)} %copy-done.72), kind=kOutput, calls=%fused_computation.16 | convolution fusion | flops 2363883520 | bytes 65667072 | tf_op jit(solution)/shard_map/dot_general | solution.py:37
  731.5 7.2 fusion.271
  749.1 8.1 fusion.167
  764.1 8.6 fusion.165
  772.6 33.5 %fusion = f32[1024,7168]{1,0:T(8,128)} fusion(f32[1024,4096]{1,0:T(8,128)S(1)} %fusion.268, f32[1024,3072]{1,0:T(8,128)} %fusion.271, f32[1024,4096]{1,0:T(8,128)} %fusion.167, f32[1024,3072]{1,0:T(8,128)} %fusion.166, f32[1024,4096]{1,0:T(8,128)} %fusion.165, f32[1024,3072]{1,0:T(8,128)} %fusion.164), kind=kLoop, calls=%fused_computation.15 | loop fusion | flops 36700160 | bytes 117440512 | tf_op jit(solution)/shard_map/add | solution.py:380
  813.0 77.5 %all-reduce.5 = (f32[13312]{0:T(1024)S(1)}, bf16[3072]{0:T(1024)(128)(2,1)S(1)}) all-reduce(f32[13312]{0:T(1024)S(1)} %add_add_fusion.1, f32[3072]{0:T(1024)S(1)} %fusion.203), channel_id=7, replica_groups=mesh['section'=2,'dp'=16] {'dp'}, use_global_device_ids=true, to_apply=%region_93.94.clone | all-reduce | flops 16384 | bytes 124928
  894.4 6.9 fusion.3
  902.7 260.1 %reduce-scatter.5.cloned.1.call-done = f32[320,1024]{1,0:T(8,128)} async-done(((f32[5120,1024]{1,0:T(8,128)}), f32[320,1024]{1,0:T(8,128)}) %reduce-scatter.5.cloned.1.call-update) | async-done | bytes 1310736 | tf_op jit(solution)/shard_map/reduce_scatter | solution.py:386
  1165.1 607.7 %reduce-scatter.3.cloned.1.call-done = f32[64,7168]{1,0:T(8,128)} async-done(((f32[1024,7168]{1,0:T(8,128)}), f32[64,7168]{1,0:T(8,128)}) %reduce-scatter.3.cloned.1.call-update) | async-done | bytes 1835024 | tf_op jit(solution)/shard_map/reduce_scatter | solution.py:385
  1777.4 45.2 %all-reduce.4 = (f32[]{:T(128)}, f32[]{:T(128)}) all-reduce(f32[]{:T(128)S(6)} %add.682, f32[]{:T(128)S(6)} %add.715), channel_id=1, replica_groups=mesh['section'=2,'dp'=16] {'section','dp'}, use_global_device_ids=true, to_apply=%region_39.40 | all-reduce | flops 2 | bytes 16 | tf_op jit(solution)/shard_map/psum | solution.py:405
  1835.6 37.4 %multiply_add_fusion = (f32[64,50304]{1,0:T(8,128)}, f32[64,50304]{1,0:T(8,128)}, f32[64,50304]{1,0:T(8,128)}, f32[64,50304]{1,0:T(8,128)}) fusion(f32[64,50304]{1,0:T(8,128)} %param.29, f32[64,50304]{1,0:T(8,128)} %param.26, f32[]{:T(128)S(6)} %min.40, bf16[64,50304]{1,0:T(8,128)(2,1)} %all-reduce.9.cloned.1.call-done, f32[64,50304]{1,0:T(8,128)} %param.27, ...), kind=kLoop, calls=%fused_computation.24 | loop fusion | flops 64389120 | bytes 109461504 | tf_op jit(solution)/shard_map/add | solution.py:290
  (729 shorter events, 305.0 us)
Async XLA Ops:
  7.2 207.8 %all-gather.7.cloned.1.call-start = ((), (), s32[]{:S(2)}) async-start(), calls=%async_computation.7 | async-start | bytes 15597568 | tf_op jit(solution)/shard_map/all_gather | solution.py:326
  9.9 325.2 %all-gather.9.cloned.1.call-start = ((), (), s32[]{:S(2)}) async-start(), calls=%async_computation.8 | async-start | bytes 11141120 | tf_op jit(solution)/shard_map/all_gather | solution.py:327
  97.7 113.3 %all-to-all-start = ((bf16[64,16,448]{2,0,1:T(8,128)(2,1)}), bf16[64,16,448]{2,0,1:T(8,128)(2,1)S(1)}, u32[]{:S(2)}, u32[]{:S(2)}) async-start(bf16[64,16,448]{2,0,1:T(8,128)(2,1)} %select_convert_fusion), calls=%async_computation | async-start | bytes 2097152 | tf_op jit(solution)/shard_map/all_to_all | solution.py:334
  101.4 793.0 %all-reduce.9.cloned.1.call-start = ((), (), s32[]{:S(2)}) async-start(), calls=%async_computation.6 | async-start | bytes 12877824 | tf_op jit(solution)/shard_map/psum | solution.py:396
  208.6 188.6 %copy-start.85 = (f32[1,1024]{1,0:T(1,128)}, f32[1,1024]{1,0:T(1,128)S(1)}, u32[]{:S(2)}) copy-start(f32[1,1024]{1,0:T(1,128)S(1)} %get-tuple-element.266) | copy-start | bytes 12292
  208.6 212.7 %copy-start.87 = (f32[1,1024]{1,0:T(1,128)}, f32[1,1024]{1,0:T(1,128)S(1)}, u32[]{:S(2)}) copy-start(f32[1,1024]{1,0:T(1,128)S(1)} %get-tuple-element.264) | copy-start | bytes 12292
  214.5 359.3 %copy-start = (f32[1024,448]{0,1:T(8,128)}, f32[1024,448]{0,1:T(8,128)S(1)}, u32[]{:S(2)}) copy-start(f32[1024,448]{0,1:T(8,128)S(1)} %copy.271) | copy-start | bytes 5505028
  344.3 4.0 collective-permute-start
  392.4 4.3 collective-permute-start.1
  396.8 333.6 %copy-start.8 = (bf16[224,1024]{1,0:T(8,128)(2,1)}, bf16[224,1024]{1,0:T(8,128)(2,1)S(1)}, u32[]{:S(2)}) copy-start(bf16[224,1024]{1,0:T(8,128)(2,1)S(1)} %collective-permute-done.1) | copy-start | bytes 1376260
  487.3 3.7 collective-permute-start.2
  530.0 3.7 collective-permute-start.3
  680.7 482.1 %reduce-scatter.5.cloned.1.call-start = ((), (), s32[]{:S(2)}) async-start(), calls=%async_computation.5 | async-start | bytes 22282240 | tf_op jit(solution)/shard_map/reduce_scatter | solution.py:386
  730.1 1042.7 %reduce-scatter.3.cloned.1.call-start = ((), (), s32[]{:S(2)}) async-start(), calls=%async_computation.4 | async-start | bytes 31195136 | tf_op jit(solution)/shard_map/reduce_scatter | solution.py:385
  894.3 929.0 %copy-start.184 = (f32[192]{0:T(256)S(1)}, f32[192]{0:T(256)}, u32[]{:S(2)}) copy-start(f32[192]{0:T(256)} %param.42) | copy-start | bytes 2308
  894.3 929.0 %copy-start.185 = (f32[192]{0:T(256)S(1)}, f32[192]{0:T(256)}, u32[]{:S(2)}) copy-start(f32[192]{0:T(256)} %param.45) | copy-start | bytes 2308
  894.4 929.0 %copy-start.186 = (f32[192]{0:T(256)S(1)}, f32[192]{0:T(256)}, u32[]{:S(2)}) copy-start(f32[192]{0:T(256)} %param.43) | copy-start | bytes 2308
  894.4 929.0 %copy-start.187 = (f32[192]{0:T(256)S(1)}, f32[192]{0:T(256)}, u32[]{:S(2)}) copy-start(f32[192]{0:T(256)} %param.44) | copy-start | bytes 2308
  894.4 929.6 %copy-start.147 = (f32[1,832]{1,0:T(1,128)S(1)}, f32[1,832]{1,0:T(1,128)}, u32[]{:S(2)}) copy-start(f32[1,832]{1,0:T(1,128)} %param.38) | copy-start | bytes 9988
  894.4 929.6 %copy-start.167 = (f32[1,832]{1,0:T(1,128)S(1)}, f32[1,832]{1,0:T(1,128)}, u32[]{:S(2)}) copy-start(f32[1,832]{1,0:T(1,128)} %param.41) | copy-start | bytes 9988
  894.4 929.6 %copy-start.168 = (f32[1,832]{1,0:T(1,128)S(1)}, f32[1,832]{1,0:T(1,128)}, u32[]{:S(2)}) copy-start(f32[1,832]{1,0:T(1,128)} %param.39) | copy-start | bytes 9988
  894.4 929.6 %copy-start.169 = (f32[1,832]{1,0:T(1,128)S(1)}, f32[1,832]{1,0:T(1,128)}, u32[]{:S(2)}) copy-start(f32[1,832]{1,0:T(1,128)} %param.40) | copy-start | bytes 9988
  894.4 930.2 %copy-start.16 = (f32[1,320,1024]{2,1,0:T(8,128)S(1)}, f32[1,320,1024]{2,1,0:T(8,128)}, u32[]{:S(2)}) copy-start(f32[1,320,1024]{2,1,0:T(8,128)} %param.34) | copy-start | bytes 3932164
  1162.8 661.8 %copy-start.14 = (f32[320,1024]{1,0:T(8,128)S(1)}, f32[320,1024]{1,0:T(8,128)}, u32[]{:S(2)}) copy-start(f32[320,1024]{1,0:T(8,128)} %reduce-scatter.5.cloned.1.call-done) | copy-start | bytes 3932164
  (198 other events, 1574.1 us)
Sparse Core Ops, SparseCore 0:
  11.4 188.8 all-gather.6
  203.6 131.4 all-gather.8
  680.8 30.5 all-reduce.8
  730.3 432.4 reduce-scatter.4
  1164.9 607.8 reduce-scatter.2
where the time goes:
time: 1890 us; the launch traced here: 1880 us
  waiting for transfers between devices  960 us (51%)
  blocking collectives  300 us (16%)
  matrix products  248 us (13%)
  other arithmetic  198 us (10%)
  local copies, waits for them, and re-layouts  139 us (7%)
  between operations  27.3 us (1%)
    reduce_scatter x1, waiting for transfers between devices, body(): lax.psum_scatter(sum_in, 'dp', scatter_dimension=0, tiled=True)  608 us
    reduce_scatter x1, waiting for transfers between devices, body(): lax.psum_scatter(sum_out, 'dp', scatter_dimension=0, tiled=True)  260 us
    unnamed x2, blocking collectives  178 us
    all_gather x1, waiting for transfers between devices, body(): lax.all_gather(out_w[0].astype(jnp.bfloat16), 'dp', axis=0, tiled=True)  87.2 us
    dot_general x9, matrix products, dot_rows(): lax.dot_general(left_operand, right_operand, (((0,), (0,)), ((), ())), pr...  87 us
    dot_general x12, matrix products, matmul(): jnp.dot(left_operand, right_operand, preferred_element_type=jnp.float32)  72.4 us
    dot_general x12, matrix products, dot_cols(): lax.dot_general(left_operand, right_operand, (((1,), (1,)), ((), ())), pr...  62.8 us
    scatter-add x1, other arithmetic, body(): jnp.zeros(table.shape, jnp.float32).at[:, every_ids]  49 us
  transfers between devices with their start and end apart: 10, of which 5 were waited for; matrix products, arithmetic and copies ran while one was open for 12% of the time, Pallas kernels for 0%

commit v1 on v0

v1 whole, which is shorter than its diff:
```python
import jax
import jax.numpy as jnp
from jax import lax
from jax.sharding import PartitionSpec as P

D = 1024
HEADS = 16
HEAD_DIM = 64
FF = 4096
ROT = 16
STEP = 10


EPS_NORM = 1e-05
CLIP_NORM = 0.05
BETA_ONE = 0.9
BETA_TWO = 0.95
ADAM_EPS = 1e-08
RATE_MAT = 0.1
RATE_VEC = 0.3
WEIGHT_DECAY = 0.1
EMA_KEEP = 0.75
MASKED = -1e30


def matmul(left_operand, right_operand):
    return jnp.dot(left_operand, right_operand, preferred_element_type=jnp.float32)


def dot_rows(left_operand, right_operand):
    return lax.dot_general(
        left_operand, right_operand, (((0,), (0,)), ((), ())), preferred_element_type=jnp.float32
    )


def dot_cols(left_operand, right_operand):
    return lax.dot_general(
        left_operand, right_operand, (((1,), (1,)), ((), ())), preferred_element_type=jnp.float32
    )


def standard_deviation(value_rows):
    center = value_rows - jnp.mean(value_rows, -1, keepdims=True)
    scale_factor = lax.rsqrt(jnp.mean(center * center, -1, keepdims=True) + EPS_NORM)
    return (center * scale_factor, scale_factor)


def norm_gradient_pass(gradient_normalized, input_normalized, scale_factor):
    return scale_factor * (
        gradient_normalized
        - jnp.mean(gradient_normalized, -1, keepdims=True)
        - input_normalized * jnp.mean(gradient_normalized * input_normalized, -1, keepdims=True)
    )


def layout(lengths, width):
    bounds = jnp.cumsum(lengths)
    starts = bounds - lengths
    places = jnp.arange(width, dtype=jnp.int32)
    segment = jnp.sum((places[:, None] >= bounds[None, :]).astype(jnp.int32), 1)
    pieces_count = lengths.shape[0]
    owner = jnp.minimum(segment, pieces_count - 1)
    chosen = jnp.arange(pieces_count, dtype=jnp.int32)[None, :] == owner[:, None]
    begin = jnp.sum(jnp.where(chosen, starts[None, :], 0), 1)
    position = places - begin + jnp.where(segment > 0, lengths[0], 0)
    same = (segment[:, None] == segment[None, :]) & (places[None, :] <= places[:, None])
    prompt = (segment[None, :] == 0) & (segment[:, None] > 0) & (segment[:, None] < pieces_count)
    return (position, same | prompt, bounds[1:] - 1)


def angles(position):
    half = ROT // 2
    freqs = 10000.0 ** (-2.0 * jnp.arange(half, dtype=jnp.float32) / ROT)
    phase = position.astype(jnp.float32)[:, None] * freqs[None, :]
    return (jnp.cos(phase)[:, None, :], jnp.sin(phase)[:, None, :])


def turn(value_rows, cosine, sine, sign):
    half = cosine.shape[-1]
    first = value_rows[..., :half]
    second = value_rows[..., half : 2 * half]
    return jnp.concatenate(
        [
            first * cosine - sign * second * sine,
            second * cosine + sign * first * sine,
            value_rows[..., 2 * half :],
        ],
        -1,
    )


def pieces(vector):
    amounts = [D, D, D, D, 3 * D, D, FF, D]
    parts = []
    offset = 0
    for amount in amounts:
        parts.append(vector[offset : offset + amount])
        offset = offset + amount
    return parts


def gelu_slope(value_rows):
    cumulative = 0.5 * (1.0 + jax.scipy.special.erf(value_rows * 0.7071067811865476))
    return cumulative + value_rows * jnp.exp(-0.5 * value_rows * value_rows) * 0.3989422804014327


def scores_of(query_rows, key_rows, allowed):
    raw = jnp.einsum(
        "qhe,khe->hqk", query_rows, key_rows, preferred_element_type=jnp.float32
    ) * HEAD_DIM ** (-0.5)
    return jnp.where(allowed[None], raw, MASKED)


def grid(count):
    return {16: (4, 2, 2), 128: (8, 4, 4)}.get(count, (count, 1, 1))


class Links:
    def __init__(self):
        self.count = lax.axis_size("dp")
        self.sizes = grid(self.count)
        self.nz, self.n1, self.n2 = self.sizes
        self.core = lax.axis_index("section")
        self.dp = lax.axis_index("dp")
        self.z = self.dp // (self.n1 * self.n2)
        self.i1 = self.dp // self.n2 % self.n1
        self.i2 = self.dp % self.n2
        self.twist = self.n1 == self.n2
        self.na, self.nb = self.n2, self.n1

    def axis_of(self, kind, core):
        if kind == "z":
            return 0
        if kind == "a":
            return 1 if core == 1 and self.twist else 2
        if kind == "b":
            return 2 if core == 1 and self.twist else 1
        return kind

    def pairs(self, kind, target):
        result = []
        for core in range(2):
            axis = self.axis_of(kind, core)
            for place in range(self.count):
                spot = [place // (self.n1 * self.n2), place // self.n2 % self.n1, place % self.n2]
                spot[axis] = target(spot[axis], self.sizes[axis])
                to = (spot[0] * self.n1 + spot[1]) * self.n2 + spot[2]
                result.append((core * self.count + place, core * self.count + to))
        return result

    def shift(self, value, kind, steps=1):
        pairs = self.pairs(kind, lambda place, size: (place + steps) % size)
        return lax.ppermute(value, ("section", "dp"), pairs)

    def flip(self, value, kind, bit):
        return lax.ppermute(value, ("section", "dp"), self.pairs(kind, lambda place, size: place ^ bit))

    def swap(self, value):
        return lax.ppermute(value, "section", [(0, 1), (1, 0)])

    def plane(self, back_a, back_b, core):
        first = (self.i1 - back_b) % self.n1
        second = (self.i2 - back_a) % self.n2
        usual = first * self.n2 + second
        if not self.twist:
            return usual
        other = (self.i1 - back_a) % self.n1 * self.n2 + (self.i2 - back_b) % self.n2
        return jnp.where(core == 0, usual, other)


def update(whole, part, starts):
    starts = [jnp.asarray(start, jnp.int32) for start in starts]
    starts = starts + [jnp.zeros((), jnp.int32)] * (whole.ndim - len(starts))
    return lax.dynamic_update_slice(whole, part, starts)


def collect_layers_first(links, shard):
    rows, width = shard.shape
    nz, na, nb = links.nz, links.na, links.nb
    column = jnp.zeros((nz, rows, width), shard.dtype)
    piece = shard
    for step in range(nz):
        if step > 0:
            piece = links.shift(piece, "z")
        column = update(column, piece[None], [(links.z - step) % nz])
    whole = jnp.zeros((nz, na * nb, 2, rows, width), shard.dtype)
    along = column
    for back_a in range(na):
        if back_a > 0:
            along = links.shift(along, "a")
        across = along
        for back_b in range(nb):
            if back_b > 0:
                across = links.shift(across, "b")
            sibling = links.swap(across)
            mine = links.plane(back_a, back_b, links.core)
            theirs = links.plane(back_a, back_b, 1 - links.core)
            whole = update(whole, across[:, None, None], [0, mine, links.core])
            whole = update(whole, sibling[:, None, None], [0, theirs, 1 - links.core])
    return whole.reshape(nz * na * nb * 2 * rows, width)


def collect_layers_last(links, shard):
    rows, width = shard.shape
    nz, na, nb = links.nz, links.na, links.nb
    layer = jnp.zeros((na * nb, rows, width), shard.dtype)
    along = shard
    for back_a in range(na):
        if back_a > 0:
            along = links.shift(along, "a")
        across = along
        for back_b in range(nb):
            if back_b > 0:
                across = links.shift(across, "b")
            layer = update(layer, across[None], [links.plane(back_a, back_b, links.core)])
    whole = jnp.zeros((nz, na * nb, 2, rows, width), shard.dtype)
    for step in range(nz):
        if step > 0:
            layer = links.shift(layer, "z")
        sibling = links.swap(layer)
        place = (links.z - step) % nz
        whole = update(whole, layer[None, :, None], [place, 0, links.core])
        whole = update(whole, sibling[None, :, None], [place, 0, 1 - links.core])
    return whole.reshape(nz * na * nb * 2 * rows, width)


def collect_small(links, row):
    pieces = [row]
    for _ in range(links.nz - 1):
        pieces.append(links.shift(pieces[-1], "z"))
    stack = jnp.stack(pieces)
    parts, places = [], []
    along = stack
    for back_a in range(links.na):
        if back_a > 0:
            along = links.shift(along, "a")
        across = along
        for back_b in range(links.nb):
            if back_b > 0:
                across = links.shift(across, "b")
            parts.append(across)
            plane = links.plane(back_a, back_b, links.core)
            for step in range(links.nz):
                places.append((links.z - step) % links.nz * (links.n1 * links.n2) + plane)
    found = jnp.concatenate(parts)
    return place_rows(found, jnp.stack(places))


def place_rows(found, places):
    count = found.shape[0]
    result = jnp.zeros_like(found)
    spots = jnp.arange(count, dtype=jnp.int32)
    for index in range(count):
        chosen = spots == places[index]
        result = jnp.where(chosen[(slice(None),) + (None,) * (found.ndim - 1)], found[index][None], result)
    return result


def roll_to(value, axis, first):
    size = value.shape[axis]
    if size == 1:
        return value
    doubled = jnp.concatenate([value, value], axis)
    return lax.dynamic_slice_in_dim(doubled, first, size, axis)


def relative_rows(links, left):
    features = left.shape[1]
    nz, n1, n2 = links.sizes
    half = features // (links.count * 2)
    turned = left.T.reshape(nz, n1, n2, 2, half, left.shape[0])
    turned = roll_to(roll_to(roll_to(turned, 0, links.z), 1, links.i1), 2, links.i2)
    turned = roll_to(turned, 3, links.core)
    ordinary = turned.transpose(3, 2, 1, 0, 4, 5)
    if not links.twist:
        return ordinary
    other = turned.transpose(3, 1, 2, 0, 4, 5)
    return jnp.stack(
        [jnp.where(links.core == 0, ordinary[0], other[0]), jnp.where(links.core == 0, other[1], ordinary[1])]
    )


def reduce_layers_first(links, left, right):
    nz, na, nb = links.nz, links.na, links.nb
    half, width = left.shape[4], right.shape[1]
    rows = left.shape[5]
    give = matmul(left[1].reshape(-1, rows), right).astype(jnp.bfloat16)
    got = links.swap(give)
    total = matmul(left[0].reshape(-1, rows), right) + got.astype(jnp.float32)
    total = total.astype(jnp.bfloat16).reshape(na, nb, nz, half, width)
    lines = []
    for at_a in range(na):
        moving = total[at_a, nb - 1]
        for at_b in range(nb - 2, -1, -1):
            moving = add_low(total[at_a, at_b], links.shift(moving, "b"))
        lines.append(moving)
    moving = lines[na - 1]
    for at_a in range(na - 2, -1, -1):
        moving = add_low(lines[at_a], links.shift(moving, "a"))
    column = moving
    moving = column[nz - 1]
    for at_z in range(nz - 2, -1, -1):
        moved = links.shift(moving, "z")
        moving = column[at_z].astype(jnp.float32) + moved.astype(jnp.float32)
        if at_z > 0:
            moving = moving.astype(jnp.bfloat16)
    return moving.astype(jnp.float32)


def reduce_layers_last(links, left, right):
    nz, na, nb = links.nz, links.na, links.nb
    half, width = left.shape[4], right.shape[1]
    rows = left.shape[5]
    left = left.transpose(0, 3, 1, 2, 4, 5)
    give = matmul(left[1].reshape(-1, rows), right).astype(jnp.bfloat16)
    got = links.swap(give)
    total = matmul(left[0].reshape(-1, rows), right) + got.astype(jnp.float32)
    total = total.astype(jnp.bfloat16).reshape(nz, na, nb, half, width)
    moving = total[nz - 1]
    for at_z in range(nz - 2, -1, -1):
        moving = add_low(total[at_z], links.shift(moving, "z"))
    layer = moving
    lines = []
    for at_a in range(na):
        moving = layer[at_a, nb - 1]
        for at_b in range(nb - 2, -1, -1):
            moving = add_low(layer[at_a, at_b], links.shift(moving, "b"))
        lines.append(moving)
    moving = lines[na - 1]
    for at_a in range(na - 2, -1, -1):
        moved = links.shift(moving, "a")
        moving = lines[at_a].astype(jnp.float32) + moved.astype(jnp.float32)
        if at_a > 0:
            moving = moving.astype(jnp.bfloat16)
    return moving.astype(jnp.float32)


def add_low(first, second):
    return (first.astype(jnp.float32) + second.astype(jnp.float32)).astype(jnp.bfloat16)


def exchange(links, blocks):
    nz, n1, n2 = links.sizes
    blocks = blocks.reshape((nz, n1, n2) + blocks.shape[1:])
    for axis, here in ((2, links.i2), (1, links.i1), (0, links.z)):
        size = links.sizes[axis]
        fresh = blocks
        for steps in range(1, size):
            part = lax.dynamic_slice_in_dim(blocks, (here + steps) % size, 1, axis)
            moved = links.shift(part, axis, steps)
            fresh = lax.dynamic_update_slice_in_dim(fresh, moved, (here - steps) % size, axis)
        blocks = fresh
    return blocks.reshape((nz * n1 * n2,) + blocks.shape[3:])


def all_sum(links, value):
    value = value + links.swap(value)
    for axis in (2, 1, 0):
        bit = 1
        while bit < links.sizes[axis]:
            value = value + links.flip(value, axis, bit)
            bit = bit * 2
    return value


def softmax_parts(scores):
    top_score = jnp.max(scores, -1, keepdims=True)
    powers = jnp.exp(scores - top_score)
    return powers / jnp.sum(powers, -1, keepdims=True)


def first_layer_forward(state, w_qkv, w_up, w_out, vector, cosine, sine, allowed):
    rows = state.shape[0]
    first_gain, first_bias, second_gain, second_bias, bias_qkv, bias_attn, bias_up, bias_down = pieces(vector)
    normal, scale = standard_deviation(state)
    left = (normal * first_gain + first_bias).astype(jnp.bfloat16)
    right = (normal * second_gain + second_bias).astype(jnp.bfloat16)
    joined = matmul(left, w_qkv) + bias_qkv
    upper = matmul(right, w_up) + bias_up
    query = turn(joined[:, :D].reshape(rows, HEADS, HEAD_DIM), cosine, sine, 1.0).astype(jnp.bfloat16)
    keys = turn(joined[:, D : 2 * D].reshape(rows, HEADS, HEAD_DIM), cosine, sine, 1.0).astype(jnp.bfloat16)
    values = joined[:, 2 * D :].reshape(rows, HEADS, HEAD_DIM).astype(jnp.bfloat16)
    weights = softmax_parts(scores_of(query, keys, allowed))
    mixed = (
        jnp.einsum("hqk,khe->qhe", weights.astype(jnp.bfloat16), values, preferred_element_type=jnp.float32)
        .reshape(rows, D)
        .astype(jnp.bfloat16)
    )
    active = jax.nn.gelu(upper, approximate=False).astype(jnp.bfloat16)
    acts = jnp.concatenate([mixed, active], 1)
    branch = matmul(mixed, w_out[:D]) + bias_attn + (matmul(active, w_out[D:]) + bias_down)
    kept = (normal, scale, left, right, upper, query, keys, values, weights, acts)
    return (state + branch, kept)


def attention_backward(query, keys, values, weights, grad_mixed):
    factor = HEAD_DIM ** (-0.5)
    grad_weights = jnp.einsum("qhe,khe->hqk", grad_mixed, values, preferred_element_type=jnp.float32)
    grad_scores = (weights * (grad_weights - jnp.sum(weights * grad_weights, -1, keepdims=True))).astype(jnp.bfloat16)
    grad_values = jnp.einsum(
        "hqk,qhe->khe", weights.astype(jnp.bfloat16), grad_mixed, preferred_element_type=jnp.float32
    )
    grad_query = jnp.einsum("hqk,khe->qhe", grad_scores, keys, preferred_element_type=jnp.float32) * factor
    grad_keys = jnp.einsum("hqk,qhe->khe", grad_scores, query, preferred_element_type=jnp.float32) * factor
    return (grad_query, grad_keys, grad_values)


def total_rows(value):
    return jnp.sum(value.astype(jnp.float32), 0)


def plackett(scores, ranking):
    ordered = scores[ranking]
    count = ordered.shape[0]
    later = jnp.arange(count)[None, :] >= jnp.arange(count)[:, None]
    grid = jnp.where(later, ordered[None, :], MASKED)
    top_score = jnp.max(grid, 1, keepdims=True)
    tails = top_score[:, 0] + jnp.log(jnp.sum(jnp.exp(grid - top_score), 1))
    return jnp.sum(tails - ordered)


def head_pass(state, final, ranking):
    gain_vector, bias_vector, weight = (final[:D], final[D : 2 * D], final[2 * D :])
    normal, scale = standard_deviation(state)
    chosen = lax.reduce_precision(normal * gain_vector + bias_vector, 8, 7)
    scores = jnp.sum(chosen * weight, -1)
    loss, pull = jax.vjp(lambda given: plackett(given, ranking), scores)
    (grad_scores,) = pull(jnp.ones((), jnp.float32))
    grad_chosen = grad_scores[:, None] * weight
    grad_final = jnp.concatenate(
        [
            jnp.sum(grad_chosen * normal, 0),
            jnp.sum(grad_chosen, 0),
            jnp.sum(grad_scores[:, None] * chosen, 0),
        ]
    )
    return (loss, norm_gradient_pass(grad_chosen * gain_vector, normal, scale), grad_final)


def adamw_update(weight, moment, second, average, gradient_value, rate, decay):
    moment_new = BETA_ONE * moment + (1.0 - BETA_ONE) * gradient_value
    second_new = BETA_TWO * second + (1.0 - BETA_TWO) * gradient_value * gradient_value
    moment_hat = moment_new / (1.0 - BETA_ONE**STEP)
    second_hat = second_new / (1.0 - BETA_TWO**STEP)
    weight_new = weight - rate * (moment_hat / (jnp.sqrt(second_hat) + ADAM_EPS) + decay * weight)
    average_new = EMA_KEEP * average + (1.0 - EMA_KEEP) * weight_new
    return (weight_new, moment_new, second_new, average_new)


def body(
    token_ids,
    seg_lengths,
    rankings,
    table,
    table_m,
    table_v,
    table_ema,
    in_w,
    in_m,
    in_v,
    in_ema,
    out_w,
    out_m,
    out_v,
    out_ema,
    layer_vec,
    vec_m,
    vec_v,
    vec_ema,
    final_vec,
    final_m,
    final_v,
    final_ema,
):
    links = Links()
    core, place, count = links.core, links.dp, links.count
    micro, width = token_ids.shape
    mine_first = core == 0

    own_vec, own_final = lax.reduce_precision(layer_vec[0], 8, 7), lax.reduce_precision(final_vec, 8, 7)
    vec_part, final_part = own_vec.shape[0], own_final.shape[0]
    small = collect_small(
        links, jnp.concatenate([own_vec, own_final, token_ids.astype(jnp.float32).reshape(-1)])
    )
    small_other = links.swap(small[:, :vec_part])
    own_layer, other_layer = small[:, :vec_part].reshape(-1), small_other.reshape(-1)
    vector_0 = jnp.where(mine_first, own_layer, other_layer)
    vector_1 = jnp.where(mine_first, other_layer, own_layer)
    final = small[:, vec_part : vec_part + final_part].reshape(-1)
    every_ids = small[:, vec_part + final_part :].astype(jnp.int32).reshape(count, micro, width)

    low_in, low_out = in_w[0].astype(jnp.bfloat16), out_w[0].astype(jnp.bfloat16)

    def halves(shard):
        rows = shard.shape[0] // 2
        keep = lax.dynamic_slice_in_dim(shard, core * rows, rows, 0)
        give = lax.dynamic_slice_in_dim(shard, (1 - core) * rows, rows, 0)
        got = links.swap(give)
        return (jnp.where(mine_first, keep, got), jnp.where(mine_first, got, keep))

    in_0, in_1 = halves(low_in)
    out_0, out_1 = halves(low_out)
    w_qkv_0 = collect_layers_first(links, in_0[:, : 3 * D])
    w_up_0 = collect_layers_first(links, in_0[:, 3 * D :])
    w_out_0 = collect_layers_first(links, out_0)
    w_qkv_1 = collect_layers_first(links, in_1[:, : 3 * D])
    w_out_1 = collect_layers_last(links, out_1)
    w_up_1 = collect_layers_first(links, in_1[:, 3 * D :])

    ids_here = lax.dynamic_slice_in_dim(every_ids, core, 1, 1).reshape(-1)
    picked = jnp.take(table, ids_here, axis=1).astype(jnp.bfloat16)
    features = picked.shape[0]
    blocks = picked.reshape(features, count, width).transpose(1, 0, 2)
    state = exchange(links, blocks).reshape(D, width).T.astype(jnp.float32)

    lengths = lax.dynamic_slice_in_dim(seg_lengths, core, 1, 0)[0]
    ranking = lax.dynamic_slice_in_dim(rankings, core, 1, 0)[0]
    position, allowed, last = layout(lengths, width)
    cosine, sine = angles(position)

    state_1, kept = first_layer_forward(state, w_qkv_0, w_up_0, w_out_0, vector_0, cosine, sine, allowed)
    state_1 = lax.reduce_precision(state_1, 8, 7)

    ends = last.shape[0]
    first_gain, first_bias, second_gain, second_bias, bias_qkv, bias_attn, bias_up, bias_down = pieces(vector_1)
    normal, scale = standard_deviation(state_1)
    left = (normal * first_gain + first_bias).astype(jnp.bfloat16)
    pairs = matmul(left, w_qkv_1[:, D:]) + bias_qkv[D:]
    keys = turn(pairs[:, :D].reshape(width, HEADS, HEAD_DIM), cosine, sine, 1.0).astype(jnp.bfloat16)
    values = pairs[:, D:].reshape(width, HEADS, HEAD_DIM).astype(jnp.bfloat16)
    normal_end, scale_end, state_end = normal[last], scale[last], state_1[last]
    cosine_end, sine_end, allowed_end = cosine[last], sine[last], allowed[last]
    left_end = (normal_end * first_gain + first_bias).astype(jnp.bfloat16)
    right_end = (normal_end * second_gain + second_bias).astype(jnp.bfloat16)
    query = matmul(left_end, w_qkv_1[:, :D]) + bias_qkv[:D]
    query = turn(query.reshape(ends, HEADS, HEAD_DIM), cosine_end, sine_end, 1.0).astype(jnp.bfloat16)
    upper = matmul(right_end, w_up_1) + bias_up
    weights = softmax_parts(scores_of(query, keys, allowed_end))
    mixed = (
        jnp.einsum("hqk,khe->qhe", weights.astype(jnp.bfloat16), values, preferred_element_type=jnp.float32)
        .reshape(ends, D)
        .astype(jnp.bfloat16)
    )
    active = jax.nn.gelu(upper, approximate=False).astype(jnp.bfloat16)
    branch = matmul(mixed, w_out_1[:D]) + bias_attn + (matmul(active, w_out_1[D:]) + bias_down)
    loss, grad_end, grad_final = head_pass(state_end + branch, final, ranking)

    low_end = grad_end.astype(jnp.bfloat16)
    grad_mixed = dot_cols(low_end, w_out_1[:D]).astype(jnp.bfloat16).reshape(ends, HEADS, HEAD_DIM)
    grad_upper = (dot_cols(low_end, w_out_1[D:]) * gelu_slope(upper)).astype(jnp.bfloat16)
    grad_query, grad_keys, grad_values = attention_backward(query, keys, values, weights, grad_mixed)
    grad_query = turn(grad_query, cosine_end, sine_end, -1.0).reshape(ends, D).astype(jnp.bfloat16)
    grad_pairs = jnp.concatenate(
        [turn(grad_keys, cosine, sine, -1.0).reshape(width, D), grad_values.reshape(width, D)], 1
    ).astype(jnp.bfloat16)
    back_left = dot_cols(grad_pairs, w_qkv_1[:, D:])
    back_left_end = dot_cols(grad_query, w_qkv_1[:, :D])
    back_right_end = dot_cols(grad_upper, w_up_1)
    sum_end = total_rows(low_end)
    sum_vec_1 = jnp.concatenate(
        [
            jnp.sum(back_left * normal, 0) + jnp.sum(back_left_end * normal_end, 0),
            jnp.sum(back_left, 0) + jnp.sum(back_left_end, 0),
            jnp.sum(back_right_end * normal_end, 0),
            jnp.sum(back_right_end, 0),
            total_rows(grad_query),
            total_rows(grad_pairs),
            sum_end,
            total_rows(grad_upper),
            sum_end,
        ]
    )
    row_index = jnp.arange(width, dtype=jnp.int32)
    extra = back_left_end * first_gain + back_right_end * second_gain
    pulled = back_left * first_gain
    landed = jnp.zeros_like(pulled)
    for end in range(ends):
        here = (row_index == last[end])[:, None]
        pulled = pulled + jnp.where(here, extra[end][None], 0.0)
        landed = landed + jnp.where(here, grad_end[end][None], 0.0)
    grad_state = landed + norm_gradient_pass(pulled, normal, scale)
    grad_state = lax.reduce_precision(grad_state, 8, 7).astype(jnp.bfloat16)

    pair_half = reduce_layers_first(links, relative_rows(links, left), grad_pairs)
    factors = jnp.concatenate([left_end, right_end, mixed, active, grad_query, grad_upper, low_end], 1)
    every_factor = collect_layers_first(links, factors)
    in_rows, out_rows = in_w.shape[1], out_w.shape[1]

    def factor_part(begin, size):
        return every_factor[:, begin : begin + size]

    left_own = lax.dynamic_slice_in_dim(factor_part(0, D), place * in_rows, in_rows, 1)
    right_own = lax.dynamic_slice_in_dim(factor_part(D, D), place * in_rows, in_rows, 1)
    acts_own = lax.dynamic_slice_in_dim(factor_part(2 * D, D + FF), place * out_rows, out_rows, 1)
    query_part = factor_part(3 * D + FF, D)
    upper_part = factor_part(4 * D + FF, FF)
    end_part = factor_part(4 * D + 2 * FF, D)
    grad_in_query = dot_rows(left_own, query_part)
    grad_in_upper = dot_rows(right_own, upper_part)
    grad_out_1 = dot_rows(acts_own, end_part)

    normal, scale, left, right, upper, query, keys, values, weights, acts = kept
    first_gain, first_bias, second_gain, second_bias = pieces(vector_0)[:4]
    low_state = grad_state
    acts_relative = relative_rows(links, acts)
    out_half = jnp.concatenate(
        [
            reduce_layers_last(links, acts_relative, low_state[:, : D // 2]),
            reduce_layers_first(links, acts_relative, low_state[:, D // 2 :]),
        ],
        1,
    )
    grad_mixed = dot_cols(low_state, w_out_0[:D]).astype(jnp.bfloat16).reshape(width, HEADS, HEAD_DIM)
    grad_upper = (dot_cols(low_state, w_out_0[D:]) * gelu_slope(upper)).astype(jnp.bfloat16)
    up_half = reduce_layers_first(links, relative_rows(links, right), grad_upper)
    grad_query, grad_keys, grad_values = attention_backward(query, keys, values, weights, grad_mixed)
    grad_joined = jnp.concatenate(
        [
            turn(grad_query, cosine, sine, -1.0).reshape(width, D),
            turn(grad_keys, cosine, sine, -1.0).reshape(width, D),
            grad_values.reshape(width, D),
        ],
        1,
    ).astype(jnp.bfloat16)
    back_left = dot_cols(grad_joined, w_qkv_0)
    back_right = dot_cols(grad_upper, w_up_0)
    sum_state = total_rows(low_state)
    sum_vec_0 = jnp.concatenate(
        [
            jnp.sum(back_left * normal, 0),
            jnp.sum(back_left, 0),
            jnp.sum(back_right * normal, 0),
            jnp.sum(back_right, 0),
            total_rows(grad_joined),
            sum_state,
            total_rows(grad_upper),
            sum_state,
        ]
    )
    grad_embedded = low_state.astype(jnp.float32) + norm_gradient_pass(
        back_left * first_gain + back_right * second_gain, normal, scale
    )
    qkv_half = reduce_layers_first(links, relative_rows(links, left), grad_joined)

    blocks = grad_embedded.astype(jnp.bfloat16).T.reshape(count, features, width)
    spread_mine = exchange(links, blocks).transpose(1, 0, 2)
    spread_other = links.swap(spread_mine)
    spread = jnp.stack(
        [jnp.where(mine_first, spread_mine, spread_other), jnp.where(mine_first, spread_other, spread_mine)], 2
    ).reshape(features, count * micro * width)
    table_grad = jnp.zeros(table.shape, jnp.float32).at[:, every_ids.reshape(-1)].add(spread.astype(jnp.float32))

    packed = jnp.concatenate([sum_vec_0, sum_vec_1, grad_final, loss[None], jnp.zeros((127,), jnp.float32)])
    packed = all_sum(links, packed.reshape(-1, 128)).reshape(-1)
    vec_size = sum_vec_0.shape[0]
    shard_vec = lax.dynamic_slice_in_dim(packed, core * vec_size + place * vec_part, vec_part, 0)
    shard_fin = lax.dynamic_slice_in_dim(packed, 2 * vec_size + place * final_part, final_part, 0)
    loss_sum = packed[2 * vec_size + 3 * D]

    in_half = jnp.concatenate([qkv_half, up_half], 1)
    in_other, out_other, pair_other = links.swap(in_half), links.swap(out_half), links.swap(pair_half)
    grad_in_0 = jnp.concatenate([in_half, in_other], 0)
    grad_out_0 = jnp.concatenate([out_half, out_other], 0)
    grad_in_1 = jnp.concatenate(
        [grad_in_query, jnp.concatenate([pair_other, pair_half], 0), grad_in_upper], 1
    )
    shard_in = jnp.where(mine_first, grad_in_0, grad_in_1)
    shard_out = jnp.where(mine_first, grad_out_0, grad_out_1)

    squares = (
        jnp.sum(shard_in * shard_in)
        + jnp.sum(shard_out * shard_out)
        + jnp.sum(shard_vec * shard_vec)
        + jnp.where(mine_first, jnp.sum(table_grad * table_grad) + jnp.sum(shard_fin * shard_fin), 0.0)
    )
    total_squares = all_sum(links, jnp.broadcast_to(squares, (8, 128)))[0, 0]
    grad_norm = jnp.sqrt(total_squares)
    factor = jnp.minimum(1.0, CLIP_NORM / (grad_norm + 1e-06))
    table_parts = adamw_update(table, table_m, table_v, table_ema, table_grad * factor, RATE_MAT, WEIGHT_DECAY)
    in_parts = adamw_update(
        in_w, in_m, in_v, in_ema, shard_in.reshape(in_w.shape) * factor, RATE_MAT, WEIGHT_DECAY
    )
    out_parts = adamw_update(
        out_w, out_m, out_v, out_ema, shard_out.reshape(out_w.shape) * factor, RATE_MAT, WEIGHT_DECAY
    )
    vec_parts = adamw_update(
        layer_vec, vec_m, vec_v, vec_ema, shard_vec.reshape(layer_vec.shape) * factor, RATE_VEC, 0.0
    )
    final_parts = adamw_update(final_vec, final_m, final_v, final_ema, shard_fin * factor, RATE_VEC, 0.0)
    return (loss_sum, grad_norm) + table_parts + in_parts + out_parts + vec_parts + final_parts


def solution(mesh):
    in_specs = (
        P("dp", None),
        P("dp", None),
        P("dp", None),
        P("dp", None),
        P("dp", None),
        P("dp", None),
        P("dp", None),
        P("section", "dp", None),
        P("section", "dp", None),
        P("section", "dp", None),
        P("section", "dp", None),
        P("section", "dp", None),
        P("section", "dp", None),
        P("section", "dp", None),
        P("section", "dp", None),
        P("section", "dp"),
        P("section", "dp"),
        P("section", "dp"),
        P("section", "dp"),
        P("dp"),
        P("dp"),
        P("dp"),
        P("dp"),
    )
    out_specs = (
        P(),
        P(),
        P("dp", None),
        P("dp", None),
        P("dp", None),
        P("dp", None),
        P("section", "dp", None),
        P("section", "dp", None),
        P("section", "dp", None),
        P("section", "dp", None),
        P("section", "dp", None),
        P("section", "dp", None),
        P("section", "dp", None),
        P("section", "dp", None),
        P("section", "dp"),
        P("section", "dp"),
        P("section", "dp"),
        P("section", "dp"),
        P("dp"),
        P("dp"),
        P("dp"),
        P("dp"),
    )
    return jax.shard_map(body, mesh=mesh, in_specs=in_specs, out_specs=out_specs, check_vma=False)
```

time: 1890 us -> 1080 us (0.57)
  waiting for transfers between devices: 960 us -> 431 us
  blocking collectives: 300 us -> 0 us
  matrix products: 248 us -> 132 us
  local copies, waits for them, and re-layouts: 139 us -> 223 us
  starting transfers between devices: 9.67 us -> 89.9 us
    reduce_scatter x2 -> x0, waiting for transfers between devices: 868 us -> none  [the longest x1 608 us: body(): lax.psum_scatter(sum_in, 'dp', scatter_dimension=0, tiled=True)]
    ppermute x4 -> x138, waiting for transfers between devices: 4.7 us -> 431 us  [the longest x88 398 us: shift(): return lax.ppermute(value, ('section', 'dp'), pairs)]
    unnamed x2 -> x0, blocking collectives: 178 us -> none
    all_gather x2 -> x0, waiting for transfers between devices: 87.2 us -> none  [the longest x1 87.2 us: body(): lax.all_gather(out_w[0].astype(jnp.bfloat16), 'dp', axis=0, tiled=True)]
    ppermute x4 -> x138, starting transfers between devices: 5.63 us -> 89.9 us  [the longest x88 77.7 us: shift(): return lax.ppermute(value, ('section', 'dp'), pairs)]
    dot_general x9 -> x3, matrix products: 87 us -> 2.78 us  [dot_rows(): lax.dot_general(left_operand, right_operand, (((0,), (0,)), ((), ())), pr...]
    dynamic_update_slice x0 -> x90, local copies, waits for them, and re-layouts: none -> 82.9 us  [the longest x82 82.8 us: update(): return lax.dynamic_update_slice(whole, part, starts)]
    psum x2 -> x0, blocking collectives: 47.6 us -> none  [the longest x1 45.2 us: body(): total_squares, loss_sum = lax.psum((squares, loss_local), ('section', 'dp'))]
  transfers between devices with their start and end apart: 10 -> 138, of which waited for: 5 -> 58; matrix products, arithmetic and copies ran while one was open for 12% -> 38% of each run, Pallas kernels for 0% -> 0%
where the time goes in v1:
time: 1080 us; the launch traced here: 1070 us
  waiting for transfers between devices  431 us (40%)
  local copies, waits for them, and re-layouts  223 us (21%)
  other arithmetic  181 us (17%)
  matrix products  132 us (12%)
  starting transfers between devices  89.9 us (8%)
    ppermute x88, waiting for transfers between devices, shift(): return lax.ppermute(value, ('section', 'dp'), pairs)  398 us
    dynamic_update_slice x82, local copies, waits for them, and re-layouts, update(): return lax.dynamic_update_slice(whole, part, starts)  82.8 us
    ppermute x88, starting transfers between devices, shift(): return lax.ppermute(value, ('section', 'dp'), pairs)  77.7 us
    dot_general x19, matrix products, matmul(): jnp.dot(left_operand, right_operand, preferred_element_type=jnp.float32)  64.6 us
    add x5, other arithmetic, adamw_update(): average_new = EMA_KEEP * average + (1.0 - EMA_KEEP) * weight_new  54.8 us
    scatter-add x1, other arithmetic, body(): jnp.zeros(table.shape, jnp.float32).at[:, every_ids.reshape(-1)]  49 us
    dot_general x9, matrix products, dot_cols(): lax.dot_general(left_operand, right_operand, (((1,), (1,)), ((), ())), pr...  42.3 us
    unnamed x371, local copies, waits for them, and re-layouts  26.1 us
  transfers between devices with their start and end apart: 138, of which 58 were waited for; matrix products, arithmetic and copies ran while one was open for 38% of the time, Pallas kernels for 0%

profile of v1, /device:TPU:0, one launch (start us, length us, event | category | flops | bytes accessed | tf_op | source)
XLA Modules:
  0.0 1066.3 jit_solution(13630978492632124624)
XLA Ops:
  34.3 15.9 %copy.297 = bf16[64,50304]{0,1:T(8,128)(2,1)} copy(f32[64,50304]{1,0:T(8,128)} %param.26) | data formatting | bytes 19316736 | tf_op args[3]
  57.8 12.1 %gather_fusion = bf16[3584,64]{1,0:T(8,128)(2,1)S(1)} fusion(bf16[64,50304]{0,1:T(8,128)(2,1)} %copy.297, s32[4096]{0:T(1024)S(1)} %pad_clamp_fusion), kind=kCustom, calls=%fused_computation | custom fusion | bytes 931840 | tf_op jit(solution)/shard_map/jit(_take)/gather | solution.py:511
  89.4 12.1 %collective-permute-done.8 = bf16[1,2,2,64,224]{4,3,2,1,0:T(8,128)(2,1)S(1)} collective-permute-done((bf16[1,2,2,64,224]{4,3,2,1,0:T(8,128)(2,1)S(1)}, bf16[1,2,2,64,224]{4,3,2,1,0:T(8,128)(2,1)S(1)}, u32[]{:S(2)}, u32[]{:S(2)}) %collective-permute-start.8) | collective-permute-done | bytes 114720 | tf_op jit(solution)/shard_map/ppermute | solution.py:153
  102.6 8.4 collective-permute-done.44
  122.1 20.3 %collective-permute-done.9 = bf16[1,2,2,64,224]{4,3,2,1,0:T(8,128)(2,1)S(1)} collective-permute-done((bf16[1,2,2,64,224]{4,3,2,1,0:T(8,128)(2,1)S(1)}, bf16[1,2,2,64,224]{4,3,2,1,0:T(8,128)(2,1)S(1)}, u32[]{:S(2)}, u32[]{:S(2)}) %collective-permute-start.9) | collective-permute-done | bytes 114720 | tf_op jit(solution)/shard_map/ppermute | solution.py:153
  177.5 28.2 %collective-permute-done.36 = bf16[32,4096]{1,0:T(8,128)(2,1)S(1)} collective-permute-done((bf16[32,4096]{1,0:T(8,128)(2,1)}, bf16[32,4096]{1,0:T(8,128)(2,1)S(1)}, u32[]{:S(2)}, u32[]{:S(2)}) %collective-permute-start.36) | collective-permute-done | bytes 262176 | tf_op jit(solution)/shard_map/ppermute | solution.py:153
  245.1 12.0 %collective-permute-done.38 = bf16[4,32,4096]{2,1,0:T(8,128)(2,1)S(1)} collective-permute-done((bf16[4,32,4096]{2,1,0:T(8,128)(2,1)S(1)}, bf16[4,32,4096]{2,1,0:T(8,128)(2,1)S(1)}, u32[]{:S(2)}, u32[]{:S(2)}) %collective-permute-start.38) | collective-permute-done | bytes 1048608 | tf_op jit(solution)/shard_map/ppermute | solution.py:153
  261.3 17.3 %collective-permute-done.68 = bf16[4,32,4096]{2,1,0:T(8,128)(2,1)S(1)} collective-permute-done((bf16[4,32,4096]{2,1,0:T(8,128)(2,1)S(1)}, bf16[4,32,4096]{2,1,0:T(8,128)(2,1)S(1)}, u32[]{:S(2)}, u32[]{:S(2)}) %collective-permute-start.68) | collective-permute-done | bytes 1048608 | tf_op jit(solution)/shard_map/ppermute | solution.py:153
  291.5 36.3 %collective-permute-done.21 = bf16[4,32,3072]{2,1,0:T(8,128)(2,1)S(1)} collective-permute-done((bf16[4,32,3072]{2,1,0:T(8,128)(2,1)S(1)}, bf16[4,32,3072]{2,1,0:T(8,128)(2,1)S(1)}, u32[]{:S(2)}, u32[]{:S(2)}) %collective-permute-start.21) | collective-permute-done | bytes 786464 | tf_op jit(solution)/shard_map/ppermute | solution.py:153
  355.0 21.7 %collective-permute-done.42 = bf16[4,32,4096]{2,1,0:T(8,128)(2,1)S(1)} collective-permute-done((bf16[4,32,4096]{2,1,0:T(8,128)(2,1)S(1)}, bf16[4,32,4096]{2,1,0:T(8,128)(2,1)S(1)}, u32[]{:S(2)}, u32[]{:S(2)}) %collective-permute-start.42) | collective-permute-done | bytes 1048608 | tf_op jit(solution)/shard_map/ppermute | solution.py:153
  420.2 13.6 %fusion.31 = (bf16[224,4096]{1,0:T(8,128)(2,1)S(1)}, f32[224,4096]{1,0:T(8,128)}) fusion(f32[4096]{0:T(1024)S(1)} %slice-done.11, bf16[1024,4096]{1,0:T(8,128)(2,1)} %bitcast.80, f32[1024,224]{0,1:T(8,128)S(1)} %copy.299, f32[1024]{0:T(1024)S(1)} %copy-done.161, f32[1024]{0:T(1024)S(1)} %copy-done.156, f32[224]{0:T(256)S(1)} %copy-done.138, ...), kind=kOutput, calls=%fused_computation.59 | convolution fusion | flops 1940750336 | bytes 14837504 | tf_op jit(solution)/shard_map/dot_general | solution.py:27
  663.1 8.9 collective-permute-done.98
  679.4 49.0 %scatter_custom_fusion.1 = f32[64,50304]{0,1:T(8,128)} fusion(s32[7168]{0:T(1024)} %bitcast.789, f32[7168,64]{1,0:T(8,128)} %bitcast.736, f32[]{:T(128)} %constant.885.clone.1), kind=kCustom, calls=%fused_computation.17 | custom fusion | flops 458752 | bytes 12878336 | tf_op jit(solution)/shard_map/scatter-add | solution.py:651
  728.4 13.2 %multiply_reduce_fusion = f32[]{:T(128)} fusion(f32[64,50304]{0,1:T(8,128)} %scatter_custom_fusion.1), kind=kLoop, calls=%fused_computation.11 | loop fusion | flops 6438911 | bytes 12877828 | tf_op jit(solution)/shard_map/reduce_sum | solution.py:674
  792.1 16.5 %collective-permute-done.108 = bf16[32,2048]{1,0:T(8,128)(2,1)S(1)} collective-permute-done((bf16[32,2048]{1,0:T(8,128)(2,1)S(1)}, bf16[32,2048]{1,0:T(8,128)(2,1)S(1)}, u32[]{:S(2)}, u32[]{:S(2)}) %collective-permute-start.108) | collective-permute-done | bytes 131104 | tf_op jit(solution)/shard_map/ppermute | solution.py:153
  818.9 19.7 %collective-permute-done.81 = bf16[4,32,3072]{2,1,0:T(8,128)(2,1)S(1)} collective-permute-done((bf16[4,32,3072]{2,1,0:T(8,128)(2,1)S(1)}, bf16[4,32,3072]{2,1,0:T(8,128)(2,1)S(1)}, u32[]{:S(2)}, u32[]{:S(2)}) %collective-permute-start.81) | collective-permute-done | bytes 786464 | tf_op jit(solution)/shard_map/ppermute | solution.py:153
  839.8 12.9 %collective-permute-done.114 = bf16[2,2,160,512]{3,2,1,0:T(8,128)(2,1)S(1)} collective-permute-done((bf16[2,2,160,512]{3,2,1,0:T(8,128)(2,1)S(1)}, bf16[2,2,160,512]{3,2,1,0:T(8,128)(2,1)S(1)}, u32[]{:S(2)}, u32[]{:S(2)}) %collective-permute-start.114) | collective-permute-done | bytes 655392 | tf_op jit(solution)/shard_map/ppermute | solution.py:153
  852.9 8.7 collective-permute-done.123
  865.3 12.3 %collective-permute-done.124 = bf16[160,512]{1,0:T(8,128)(2,1)S(1)} collective-permute-done((bf16[160,512]{1,0:T(8,128)(2,1)S(1)}, bf16[160,512]{1,0:T(8,128)(2,1)S(1)}, u32[]{:S(2)}, u32[]{:S(2)}) %collective-permute-start.124) | collective-permute-done | bytes 163872 | tf_op jit(solution)/shard_map/ppermute | solution.py:153
  889.8 34.9 %collective-permute-done.117 = bf16[160,512]{1,0:T(8,128)(2,1)S(1)} collective-permute-done((bf16[160,512]{1,0:T(8,128)(2,1)S(1)}, bf16[160,512]{1,0:T(8,128)(2,1)S(1)}, u32[]{:S(2)}, u32[]{:S(2)}) %collective-permute-start.117) | collective-permute-done | bytes 163872 | tf_op jit(solution)/shard_map/ppermute | solution.py:153
  930.3 11.0 %collective-permute-done.89 = bf16[4,32,4096]{2,1,0:T(8,128)(2,1)S(1)} collective-permute-done((bf16[4,32,4096]{2,1,0:T(8,128)(2,1)S(1)}, bf16[4,32,4096]{2,1,0:T(8,128)(2,1)S(1)}, u32[]{:S(2)}, u32[]{:S(2)}) %collective-permute-start.89) | collective-permute-done | bytes 1048608 | tf_op jit(solution)/shard_map/ppermute | solution.py:153
  942.0 9.1 collective-permute-done.90
  984.0 20.3 %copy.389 = f32[64,50304]{1,0:T(8,128)} copy(f32[64,50304]{0,1:T(8,128)} %scatter_custom_fusion.1) | data formatting | bytes 25755648 | tf_op jit(solution)/shard_map/scatter-add | solution.py:651
  1016.7 40.2 %multiply_add_fusion = (f32[64,50304]{1,0:T(8,128)}, f32[64,50304]{1,0:T(8,128)}, f32[64,50304]{1,0:T(8,128)}, f32[64,50304]{1,0:T(8,128)}) fusion(f32[64,50304]{1,0:T(8,128)} %param.29, f32[64,50304]{1,0:T(8,128)} %param.26, f32[64,50304]{1,0:T(8,128)} %copy.389, f32[]{:T(128)S(6)} %min.15, f32[64,50304]{1,0:T(8,128)} %param.27, f32[64,50304]{1,0:T(8,128)} %param.28), kind=kLoop, calls=%fused_computation.14 | loop fusion | flops 61169664 | bytes 115900416 | tf_op jit(solution)/shard_map/add | solution.py:446
  (1071 shorter events, 601.8 us)
Async XLA Ops:
  8.3 72.1 %collective-permute-start.23 = (bf16[160,1024]{1,0:T(8,128)(2,1)}, bf16[160,1024]{1,0:T(8,128)(2,1)}, u32[]{:S(2)}, u32[]{:S(2)}) collective-permute-start(bf16[160,1024]{1,0:T(8,128)(2,1)} %dynamic-slice_bitcast_fusion.1), channel_id=1, source_target_pairs={{0,16},{16,0},{1,17},{17,1},{2,18},{18,2},{3,19},{19,3},{4,20},{20... | collective-permute-start | bytes 983048 | tf_op jit(solution)/shard_map/ppermute | solution.py:159
  9.3 75.8 %collective-permute-start.12 = (bf16[32,7168]{1,0:T(8,128)(2,1)}, bf16[32,7168]{1,0:T(8,128)(2,1)}, u32[]{:S(2)}, u32[]{:S(2)}) collective-permute-start(bf16[32,7168]{1,0:T(8,128)(2,1)} %dynamic-slice_bitcast_fusion), channel_id=1, source_target_pairs={{0,16},{16,0},{1,17},{17,1},{2,18},{18,2},{3,19},{19,3},{4,20},{20... | collective-permute-start | bytes 1376264 | tf_op jit(solution)/shard_map/ppermute | solution.py:159
  122.1 49.2 %collective-permute-start.25 = (bf16[160,1024]{1,0:T(8,128)(2,1)}, bf16[160,1024]{1,0:T(8,128)(2,1)}, u32[]{:S(2)}, u32[]{:S(2)}) collective-permute-start(bf16[160,1024]{1,0:T(8,128)(2,1)} %collective-permute-done.24), channel_id=1, source_target_pairs={{0,4},{1,5},{2,6},{3,7},{4,8},{5,9},{6,10},{7,11},{8,12},{9,13},{1... | collective-permute-start | bytes 983048 | tf_op jit(solution)/shard_map/ppermute | solution.py:153
  160.6 123.1 %collective-permute-start.58 = (bf16[4,160,1024]{2,1,0:T(8,128)(2,1)S(1)}, bf16[4,160,1024]{2,1,0:T(8,128)(2,1)}, u32[]{:S(2)}, u32[]{:S(2)}) collective-permute-start(bf16[4,160,1024]{2,1,0:T(8,128)(2,1)S(1)} %bitcast_dynamic-update-slice_fusion.56), channel_id=1, source_target_pairs={{0,4},{1,5},{2,6},{3,7},{4,8},{5,9},{6,10},{7,11},{8,12},{9,13},{1... | collective-permute-start | bytes 3932168 | tf_op jit(solution)/shard_map/ppermute | solution.py:153
  163.7 116.0 %collective-permute-start.57 = (bf16[4,160,1024]{2,1,0:T(8,128)(2,1)S(1)}, bf16[4,160,1024]{2,1,0:T(8,128)(2,1)}, u32[]{:S(2)}, u32[]{:S(2)}) collective-permute-start(bf16[4,160,1024]{2,1,0:T(8,128)(2,1)S(1)} %bitcast_dynamic-update-slice_fusion.56), channel_id=1, source_target_pairs={{0,16},{16,0},{1,17},{17,1},{2,18},{18,2},{3,19},{19,3},{4,20},{20... | collective-permute-start | bytes 3932168 | tf_op jit(solution)/shard_map/ppermute | solution.py:159
  205.7 83.5 %collective-permute-start.50 = (bf16[4,32,3072]{2,1,0:T(8,128)(2,1)S(1)}, bf16[4,32,3072]{2,1,0:T(8,128)(2,1)S(1)}, u32[]{:S(2)}, u32[]{:S(2)}) collective-permute-start(bf16[4,32,3072]{2,1,0:T(8,128)(2,1)S(1)} %bitcast_dynamic-update-slice_fusion.72), channel_id=1, source_target_pairs={{0,1},{1,0},{2,3},{3,2},{4,5},{5,4},{6,7},{7,6},{8,9},{9,8},{10,11... | collective-permute-start | bytes 2359304 | tf_op jit(solution)/shard_map/ppermute | solution.py:153
  279.7 52.5 %collective-permute-start.70 = (bf16[4,32,4096]{2,1,0:T(8,128)(2,1)S(1)}, bf16[4,32,4096]{2,1,0:T(8,128)(2,1)S(1)}, u32[]{:S(2)}, u32[]{:S(2)}) collective-permute-start(bf16[4,32,4096]{2,1,0:T(8,128)(2,1)S(1)} %bitcast_dynamic-update-slice_fusion.64), channel_id=1, source_target_pairs={{0,1},{1,0},{2,3},{3,2},{4,5},{5,4},{6,7},{7,6},{8,9},{9,8},{10,11... | collective-permute-start | bytes 3145736 | tf_op jit(solution)/shard_map/ppermute | solution.py:153
  283.7 62.9 %collective-permute-start.40 = (bf16[4,32,4096]{2,1,0:T(8,128)(2,1)S(1)}, bf16[4,32,4096]{2,1,0:T(8,128)(2,1)S(1)}, u32[]{:S(2)}, u32[]{:S(2)}) collective-permute-start(bf16[4,32,4096]{2,1,0:T(8,128)(2,1)S(1)} %bitcast_dynamic-update-slice_fusion.68), channel_id=1, source_target_pairs={{0,1},{1,0},{2,3},{3,2},{4,5},{5,4},{6,7},{7,6},{8,9},{9,8},{10,11... | collective-permute-start | bytes 3145736 | tf_op jit(solution)/shard_map/ppermute | solution.py:153
  286.8 47.0 %collective-permute-start.28 = (bf16[4,160,1024]{2,1,0:T(8,128)(2,1)S(1)}, bf16[4,160,1024]{2,1,0:T(8,128)(2,1)}, u32[]{:S(2)}, u32[]{:S(2)}) collective-permute-start(bf16[4,160,1024]{2,1,0:T(8,128)(2,1)S(1)} %bitcast_dynamic-update-slice_fusion.60), channel_id=1, source_target_pairs={{0,2},{1,3},{2,0},{3,1},{4,6},{5,7},{6,4},{7,5},{8,10},{9,11},{10,... | collective-permute-start | bytes 3932168 | tf_op jit(solution)/shard_map/ppermute | solution.py:153
  332.2 47.1 %collective-permute-start.30 = (bf16[4,160,1024]{2,1,0:T(8,128)(2,1)S(1)}, bf16[4,160,1024]{2,1,0:T(8,128)(2,1)}, u32[]{:S(2)}, u32[]{:S(2)}) collective-permute-start(bf16[4,160,1024]{2,1,0:T(8,128)(2,1)S(1)} %bitcast_dynamic-update-slice_fusion.60), channel_id=1, source_target_pairs={{0,1},{1,0},{2,3},{3,2},{4,5},{5,4},{6,7},{7,6},{8,9},{9,8},{10,11... | collective-permute-start | bytes 3932168 | tf_op jit(solution)/shard_map/ppermute | solution.py:153
  333.8 45.7 %collective-permute-start.72 = (bf16[4,32,4096]{2,1,0:T(8,128)(2,1)S(1)}, bf16[4,32,4096]{2,1,0:T(8,128)(2,1)}, u32[]{:S(2)}, u32[]{:S(2)}) collective-permute-start(bf16[4,32,4096]{2,1,0:T(8,128)(2,1)S(1)} %collective-permute-done.70), channel_id=1, source_target_pairs={{0,2},{1,3},{2,0},{3,1},{4,6},{5,7},{6,4},{7,5},{8,10},{9,11},{10,... | collective-permute-start | bytes 3145736 | tf_op jit(solution)/shard_map/ppermute | solution.py:153
  353.5 52.4 %collective-permute-start.60 = (bf16[4,160,1024]{2,1,0:T(8,128)(2,1)}, bf16[4,160,1024]{2,1,0:T(8,128)(2,1)}, u32[]{:S(2)}, u32[]{:S(2)}) collective-permute-start(bf16[4,160,1024]{2,1,0:T(8,128)(2,1)} %collective-permute-done.58), channel_id=1, source_target_pairs={{0,4},{1,5},{2,6},{3,7},{4,8},{5,9},{6,10},{7,11},{8,12},{9,13},{1... | collective-permute-start | bytes 3932168 | tf_op jit(solution)/shard_map/ppermute | solution.py:153
  403.1 46.8 %collective-permute-start.73 = (bf16[4,32,4096]{2,1,0:T(8,128)(2,1)}, bf16[4,32,4096]{2,1,0:T(8,128)(2,1)}, u32[]{:S(2)}, u32[]{:S(2)}) collective-permute-start(bf16[4,32,4096]{2,1,0:T(8,128)(2,1)} %collective-permute-done.72), channel_id=1, source_target_pairs={{0,16},{16,0},{1,17},{17,1},{2,18},{18,2},{3,19},{19,3},{4,20},{20... | collective-permute-start | bytes 3145736 | tf_op jit(solution)/shard_map/ppermute | solution.py:159
  452.6 50.3 %collective-permute-start.63 = (bf16[4,160,1024]{2,1,0:T(8,128)(2,1)}, bf16[4,160,1024]{2,1,0:T(8,128)(2,1)}, u32[]{:S(2)}, u32[]{:S(2)}) collective-permute-start(bf16[4,160,1024]{2,1,0:T(8,128)(2,1)} %collective-permute-done.62), channel_id=1, source_target_pairs={{0,16},{16,0},{1,17},{17,1},{2,18},{18,2},{3,19},{19,3},{4,20},{20... | collective-permute-start | bytes 3932168 | tf_op jit(solution)/shard_map/ppermute | solution.py:159
  587.2 170.7 %collective-permute-start.104 = (bf16[512,2048]{1,0:T(8,128)(2,1)}, bf16[512,2048]{1,0:T(8,128)(2,1)}, u32[]{:S(2)}, u32[]{:S(2)}) collective-permute-start(bf16[512,2048]{1,0:T(8,128)(2,1)} %convolution_convert_fusion.4), channel_id=1, source_target_pairs={{0,16},{16,0},{1,17},{17,1},{2,18},{18,2},{3,19},{19,3},{4,20},{20... | collective-permute-start | bytes 6291464 | tf_op jit(solution)/shard_map/ppermute | solution.py:159
  592.2 184.5 %collective-permute-start.119 = (bf16[2560,512]{1,0:T(8,128)(2,1)}, bf16[2560,512]{1,0:T(8,128)(2,1)}, u32[]{:S(2)}, u32[]{:S(2)}) collective-permute-start(bf16[2560,512]{1,0:T(8,128)(2,1)} %convolution_convert_fusion.1), channel_id=1, source_target_pairs={{0,16},{16,0},{1,17},{17,1},{2,18},{18,2},{3,19},{19,3},{4,20},{20... | collective-permute-start | bytes 7864328 | tf_op jit(solution)/shard_map/ppermute | solution.py:159
  592.6 188.1 %collective-permute-start.112 = (bf16[2560,512]{1,0:T(8,128)(2,1)}, bf16[2560,512]{1,0:T(8,128)(2,1)}, u32[]{:S(2)}, u32[]{:S(2)}) collective-permute-start(bf16[2560,512]{1,0:T(8,128)(2,1)} %convolution_convert_fusion.2), channel_id=1, source_target_pairs={{0,16},{16,0},{1,17},{17,1},{2,18},{18,2},{3,19},{19,3},{4,20},{20... | collective-permute-start | bytes 7864328 | tf_op jit(solution)/shard_map/ppermute | solution.py:159
  660.9 82.1 %collective-permute-start.100 = (bf16[4,4,13312]{2,1,0:T(4,128)(2,1)}, bf16[4,4,13312]{2,1,0:T(4,128)(2,1)}, u32[]{:S(2)}, u32[]{:S(2)}) collective-permute-start(bf16[4,4,13312]{2,1,0:T(4,128)(2,1)} %bitcast_dynamic-update-slice_fusion.80), channel_id=1, source_target_pairs={{0,1},{1,0},{2,3},{3,2},{4,5},{5,4},{6,7},{7,6},{8,9},{9,8},{10,11... | collective-permute-start | bytes 1277960 | tf_op jit(solution)/shard_map/ppermute | solution.py:153
  673.9 69.5 %collective-permute-start.99 = (bf16[4,4,13312]{2,1,0:T(4,128)(2,1)}, bf16[4,4,13312]{2,1,0:T(4,128)(2,1)}, u32[]{:S(2)}, u32[]{:S(2)}) collective-permute-start(bf16[4,4,13312]{2,1,0:T(4,128)(2,1)} %collective-permute-done.98), channel_id=1, source_target_pairs={{0,16},{16,0},{1,17},{17,1},{2,18},{18,2},{3,19},{19,3},{4,20},{20... | collective-permute-start | bytes 1277960 | tf_op jit(solution)/shard_map/ppermute | solution.py:159
  757.7 104.0 %collective-permute-start.86 = (bf16[512,4096]{1,0:T(8,128)(2,1)}, bf16[512,4096]{1,0:T(8,128)(2,1)}, u32[]{:S(2)}, u32[]{:S(2)}) collective-permute-start(bf16[512,4096]{1,0:T(8,128)(2,1)} %convolution_convert_fusion), channel_id=1, source_target_pairs={{0,16},{16,0},{1,17},{17,1},{2,18},{18,2},{3,19},{19,3},{4,20},{20... | collective-permute-start | bytes 12582920 | tf_op jit(solution)/shard_map/ppermute | solution.py:159
  780.6 58.1 %collective-permute-start.120 = (bf16[4,160,512]{2,1,0:T(8,128)(2,1)S(1)}, bf16[4,160,512]{2,1,0:T(8,128)(2,1)S(1)}, u32[]{:S(2)}, u32[]{:S(2)}) collective-permute-start(bf16[4,160,512]{2,1,0:T(8,128)(2,1)S(1)} %get-tuple-element.178), channel_id=1, source_target_pairs={{0,2},{1,3},{2,0},{3,1},{4,6},{5,7},{6,4},{7,5},{8,10},{9,11},{10,... | collective-permute-start | bytes 1966088 | tf_op jit(solution)/shard_map/ppermute | solution.py:153
  808.6 78.7 %collective-permute-start.80 = (bf16[4,32,3072]{2,1,0:T(8,128)(2,1)S(1)}, bf16[4,32,3072]{2,1,0:T(8,128)(2,1)S(1)}, u32[]{:S(2)}, u32[]{:S(2)}) collective-permute-start(bf16[4,32,3072]{2,1,0:T(8,128)(2,1)S(1)} %get-tuple-element.168), channel_id=1, source_target_pairs={{0,2},{1,3},{2,0},{3,1},{4,6},{5,7},{6,4},{7,5},{8,10},{9,11},{10,... | collective-permute-start | bytes 2359304 | tf_op jit(solution)/shard_map/ppermute | solution.py:153
  838.8 130.4 %collective-permute-start.110 = (bf16[32,2048]{1,0:T(8,128)(2,1)S(1)}, bf16[32,2048]{1,0:T(8,128)(2,1)S(1)}, u32[]{:S(2)}, u32[]{:S(2)}) collective-permute-start(bf16[32,2048]{1,0:T(8,128)(2,1)S(1)} %fusion.179), channel_id=1, source_target_pairs={{0,4},{1,5},{2,6},{3,7},{4,8},{5,9},{6,10},{7,11},{8,12},{9,13},{1... | collective-permute-start | bytes 393224 | tf_op jit(solution)/shard_map/ppermute | solution.py:153
  838.9 49.6 %collective-permute-start.82 = (bf16[4,32,3072]{2,1,0:T(8,128)(2,1)S(1)}, bf16[4,32,3072]{2,1,0:T(8,128)(2,1)S(1)}, u32[]{:S(2)}, u32[]{:S(2)}) collective-permute-start(bf16[4,32,3072]{2,1,0:T(8,128)(2,1)S(1)} %fusion.72), channel_id=1, source_target_pairs={{0,1},{1,0},{2,3},{3,2},{4,5},{5,4},{6,7},{7,6},{8,9},{9,8},{10,11... | collective-permute-start | bytes 2359304 | tf_op jit(solution)/shard_map/ppermute | solution.py:153
  (302 other events, 4007.1 us)

commit v2 on v1

--- a/solution.py
+++ b/solution.py
@@ -1,6 +1,8 @@
 import jax
 import jax.numpy as jnp
 from jax import lax
+from jax.experimental import pallas as pl
+from jax.experimental.pallas import tpu as pltpu
 from jax.sharding import PartitionSpec as P
 
 D = 1024
@@ -168,82 +170,224 @@
         return jnp.where(core == 0, usual, other)
 
 
+def nothing(*refs):
+    pass
+
+
+def blank(shape, kind, after):
+    return pl.pallas_call(
+        nothing,
+        out_shape=jax.ShapeDtypeStruct(shape, kind),
+        in_specs=[pl.BlockSpec(memory_space=pl.ANY)] * len(after),
+        out_specs=pl.BlockSpec(memory_space=pl.ANY),
+        name="blank",
+    )(*after)
+
+
+def behind(value, *after):
+    return pl.pallas_call(
+        nothing,
+        out_shape=jax.ShapeDtypeStruct(value.shape, value.dtype),
+        in_specs=[pl.BlockSpec(memory_space=pl.ANY)] * (1 + len(after)),
+        out_specs=pl.BlockSpec(memory_space=pl.ANY),
+        input_output_aliases={0: 0},
+        name="behind",
+    )(value, *after)
+
+
 def update(whole, part, starts):
     starts = [jnp.asarray(start, jnp.int32) for start in starts]
     starts = starts + [jnp.zeros((), jnp.int32)] * (whole.ndim - len(starts))
     return lax.dynamic_update_slice(whole, part, starts)
 
 
-def collect_layers_first(links, shard):
-    rows, width = shard.shape
-    nz, na, nb = links.nz, links.na, links.nb
-    column = jnp.zeros((nz, rows, width), shard.dtype)
-    piece = shard
-    for step in range(nz):
-        if step > 0:
-            piece = links.shift(piece, "z")
-        column = update(column, piece[None], [(links.z - step) % nz])
-    whole = jnp.zeros((nz, na * nb, 2, rows, width), shard.dtype)
-    along = column
-    for back_a in range(na):
-        if back_a > 0:
-            along = links.shift(along, "a")
-        across = along
-        for back_b in range(nb):
-            if back_b > 0:
-                across = links.shift(across, "b")
-            sibling = links.swap(across)
-            mine = links.plane(back_a, back_b, links.core)
-            theirs = links.plane(back_a, back_b, 1 - links.core)
-            whole = update(whole, across[:, None, None], [0, mine, links.core])
-            whole = update(whole, sibling[:, None, None], [0, theirs, 1 - links.core])
-    return whole.reshape(nz * na * nb * 2 * rows, width)
-
-
-def collect_layers_last(links, shard):
-    rows, width = shard.shape
-    nz, na, nb = links.nz, links.na, links.nb
-    layer = jnp.zeros((na * nb, rows, width), shard.dtype)
-    along = shard
-    for back_a in range(na):
-        if back_a > 0:
-            along = links.shift(along, "a")
-        across = along
-        for back_b in range(nb):
-            if back_b > 0:
-                across = links.shift(across, "b")
-            layer = update(layer, across[None], [links.plane(back_a, back_b, links.core)])
-    whole = jnp.zeros((nz, na * nb, 2, rows, width), shard.dtype)
-    for step in range(nz):
-        if step > 0:
-            layer = links.shift(layer, "z")
-        sibling = links.swap(layer)
-        place = (links.z - step) % nz
-        whole = update(whole, layer[None, :, None], [place, 0, links.core])
-        whole = update(whole, sibling[None, :, None], [place, 0, 1 - links.core])
-    return whole.reshape(nz * na * nb * 2 * rows, width)
-
-
-def collect_small(links, row):
-    pieces = [row]
-    for _ in range(links.nz - 1):
-        pieces.append(links.shift(pieces[-1], "z"))
-    stack = jnp.stack(pieces)
-    parts, places = [], []
-    along = stack
-    for back_a in range(links.na):
-        if back_a > 0:
-            along = links.shift(along, "a")
-        across = along
-        for back_b in range(links.nb):
-            if back_b > 0:
-                across = links.shift(across, "b")
-            parts.append(across)
+def place(whole, parts, axis):
+    count = len(parts)
+    spots = jnp.stack([jnp.asarray(spot, jnp.int32) for _, *pair in parts for spot in pair])
+    fresh = isinstance(whole, tuple)
+    kind, shape = parts[0][0].dtype, whole if fresh else whole.shape
+
+    def kernel(spots_ref, *refs):
+        sources, target, arrived, left = refs[:count], refs[-3 - count], refs[-2], refs[-1]
+        buffers = refs[-2 - count : -2]
+        loads = [
+            pltpu.make_async_copy(sources[at], buffers[at], arrived.at[at]) for at in range(count)
+        ]
+        stores = []
+        for at in range(count):
+            spot, half = spots_ref[2 * at], spots_ref[2 * at + 1]
+            into = target.at[:, spot, half] if axis == 1 else target.at[spot, :, half]
+            stores.append(pltpu.make_async_copy(buffers[at], into, left.at[at]))
+        for load in loads:
+            load.start()
+        for load, store in zip(loads, stores):
+            load.wait()
+            store.start()
+        for store in stores:
+            store.wait()
+
+    return pl.pallas_call(
+        kernel,
+        out_shape=jax.ShapeDtypeStruct(shape, kind),
+        grid_spec=pltpu.PrefetchScalarGridSpec(
+            num_scalar_prefetch=1,
+            grid=(1,),
+            in_specs=[pl.BlockSpec(memory_space=pl.ANY)] * (count + (0 if fresh else 1)),
+            out_specs=pl.BlockSpec(memory_space=pl.ANY),
+            scratch_shapes=[pltpu.VMEM(part.shape, kind) for part, *_ in parts]
+            + [pltpu.SemaphoreType.DMA((count,)), pltpu.SemaphoreType.DMA((count,))],
+        ),
+        input_output_aliases={} if fresh else {1 + count: 0},
+        compiler_params=pltpu.CompilerParams(vmem_limit_bytes=40 * 1024 * 1024),
+        name="place",
+    )(spots, *[part for part, *_ in parts], *([] if fresh else [whole]))
+
+
+def peek(value):
+    ends = [min(size, limit) for size, limit in zip(value.shape[-2:], (8, 128))]
+    return lax.slice(value, (0,) * value.ndim, (1,) * (value.ndim - 2) + tuple(ends))
+
+
+class Pace:
+    def __init__(self):
+        self.token = None
+
+    def tie(self, value):
+        return value if self.token is None else behind(value, self.token)
+
+    def close(self, *values, hold=()):
+        hold = [gather for gather in hold if gather.write() is not None]
+        held = [gather.buffer for gather in hold]
+        taken = len(values) + len(held)
+
+        def kernel(*refs):
+            refs[taken][...] = jnp.zeros_like(refs[taken])
+
+        outs = pl.pallas_call(
+            kernel,
+            out_shape=[jax.ShapeDtypeStruct((8, 128), jnp.float32)]
+            + [jax.ShapeDtypeStruct(value.shape, value.dtype) for value in held],
+            in_specs=[pl.BlockSpec(memory_space=pl.ANY)] * taken,
+            out_specs=[pl.BlockSpec(memory_space=pltpu.VMEM)]
+            + [pl.BlockSpec(memory_space=pl.ANY)] * len(held),
+            input_output_aliases={len(values) + at: 1 + at for at in range(len(held))},
+            name="close",
+        )(*values, *held)
+        self.token = outs[0]
+        for gather, value in zip(hold, outs[1:]):
+            gather.buffer = value
+
+
+class Gather:
+    def __init__(self, links, shard):
+        self.links, self.piece, self.step, self.level = links, shard, 0, 0
+        self.column = blank((links.nz,) + shard.shape, shard.dtype, (shard,))
+        self.column = update(self.column, shard[None], [links.z])
+        self.found, self.sibling, self.buffer, self.written = None, {}, None, set()
+
+    def along(self, pace, steps=None):
+        links, fresh = self.links, []
+        self.piece = pace.tie(self.piece)
+        while self.step < links.nz - 1 and (steps is None or steps > 0):
+            self.step = self.step + 1
+            self.piece = links.shift(self.piece, "z")
+            self.column = update(self.column, self.piece[None], [(links.z - self.step) % links.nz])
+            fresh.append(self.piece)
+            steps = None if steps is None else steps - 1
+        return fresh
+
+    def wave(self, pace, siblings=True):
+        links, fresh = self.links, []
+        if self.found is None:
+            fresh = self.along(pace)
+            self.found = {(0, 0): self.column}
+        for key in [key for key in self.found if sum(key) == self.level]:
+            self.found[key] = pace.tie(self.found[key])
+            if siblings:
+                self.sibling[key] = links.swap(self.found[key])
+                fresh.append(self.sibling[key])
+        self.level = self.level + 1
+        for back_a in range(links.na):
+            back_b = self.level - back_a
+            if 0 <= back_b < links.nb:
+                if back_b > 0:
+                    value = links.shift(self.found[back_a, back_b - 1], "b")
+                else:
+                    value = links.shift(self.found[back_a - 1, 0], "a")
+                self.found[back_a, back_b] = value
+                fresh.append(value)
+        return fresh
+
+    def last(self, pace):
+        links, fresh = self.links, []
+        while self.level < links.na + links.nb - 2:
+            fresh = fresh + self.wave(pace)
+        for key in self.found:
+            if key not in self.sibling:
+                self.found[key] = pace.tie(self.found[key])
+                self.sibling[key] = links.swap(self.found[key])
+                fresh.append(self.sibling[key])
+        return fresh
+
+    def write(self):
+        links, parts = self.links, []
+        nz, rows, width = self.column.shape
+        for key in self.sibling:
+            if key not in self.written:
+                self.written.add(key)
+                mine = links.plane(key[0], key[1], links.core)
+                theirs = links.plane(key[0], key[1], 1 - links.core)
+                parts.append((self.found[key], mine, links.core))
+                parts.append((self.sibling[key], theirs, 1 - links.core))
+        if parts:
+            shape = (nz, links.na * links.nb, 2, rows, width)
+            self.buffer = place(shape if self.buffer is None else self.buffer, parts, 1)
+        return self.buffer
+
+    def whole(self):
+        return self.write().reshape(-1, self.column.shape[2])
+
+
+class Small:
+    def __init__(self, links, row):
+        self.links, self.pieces, self.level, self.found = links, [row], 0, None
+
+    def along(self, pace, steps=1):
+        while len(self.pieces) < self.links.nz and steps > 0:
+            self.pieces.append(self.links.shift(pace.tie(self.pieces[-1]), "z"))
+            steps = steps - 1
+        return self.pieces[-1:]
+
+    def wave(self, pace):
+        links, fresh = self.links, []
+        if self.found is None:
+            self.along(pace, links.nz)
+            self.found = {(0, 0): jnp.stack(self.pieces)}
+        for key in [key for key in self.found if sum(key) == self.level]:
+            self.found[key] = pace.tie(self.found[key])
+        self.level = self.level + 1
+        for back_a in range(links.na):
+            back_b = self.level - back_a
+            if 0 <= back_b < links.nb:
+                if back_b > 0:
+                    value = links.shift(self.found[back_a, back_b - 1], "b")
+                else:
+                    value = links.shift(self.found[back_a - 1, 0], "a")
+                self.found[back_a, back_b] = value
+                fresh.append(value)
+        return fresh
+
+    def whole(self, pace):
+        links = self.links
+        while self.found is None or self.level < links.na + links.nb - 2:
+            self.wave(pace)
+        parts, places = [], []
+        for (back_a, back_b), value in self.found.items():
+            parts.append(value)
             plane = links.plane(back_a, back_b, links.core)
             for step in range(links.nz):
                 places.append((links.z - step) % links.nz * (links.n1 * links.n2) + plane)
-    found = jnp.concatenate(parts)
-    return place_rows(found, jnp.stack(places))
+        return place_rows(jnp.concatenate(parts), jnp.stack(places))
 
 
 def place_rows(found, places):
@@ -271,86 +415,87 @@
     turned = left.T.reshape(nz, n1, n2, 2, half, left.shape[0])
     turned = roll_to(roll_to(roll_to(turned, 0, links.z), 1, links.i1), 2, links.i2)
     turned = roll_to(turned, 3, links.core)
-    ordinary = turned.transpose(3, 2, 1, 0, 4, 5)
+    ordinary = turned.transpose(3, 1, 2, 0, 4, 5)
     if not links.twist:
         return ordinary
-    other = turned.transpose(3, 1, 2, 0, 4, 5)
+    other = turned.transpose(3, 2, 1, 0, 4, 5)
     return jnp.stack(
         [jnp.where(links.core == 0, ordinary[0], other[0]), jnp.where(links.core == 0, other[1], ordinary[1])]
     )
 
 
-def reduce_layers_first(links, left, right):
-    nz, na, nb = links.nz, links.na, links.nb
-    half, width = left.shape[4], right.shape[1]
-    rows = left.shape[5]
-    give = matmul(left[1].reshape(-1, rows), right).astype(jnp.bfloat16)
-    got = links.swap(give)
-    total = matmul(left[0].reshape(-1, rows), right) + got.astype(jnp.float32)
-    total = total.astype(jnp.bfloat16).reshape(na, nb, nz, half, width)
-    lines = []
-    for at_a in range(na):
-        moving = total[at_a, nb - 1]
-        for at_b in range(nb - 2, -1, -1):
-            moving = add_low(total[at_a, at_b], links.shift(moving, "b"))
-        lines.append(moving)
-    moving = lines[na - 1]
-    for at_a in range(na - 2, -1, -1):
-        moving = add_low(lines[at_a], links.shift(moving, "a"))
-    column = moving
-    moving = column[nz - 1]
-    for at_z in range(nz - 2, -1, -1):
-        moved = links.shift(moving, "z")
-        moving = column[at_z].astype(jnp.float32) + moved.astype(jnp.float32)
-        if at_z > 0:
-            moving = moving.astype(jnp.bfloat16)
-    return moving.astype(jnp.float32)
-
-
-def reduce_layers_last(links, left, right):
-    nz, na, nb = links.nz, links.na, links.nb
-    half, width = left.shape[4], right.shape[1]
-    rows = left.shape[5]
-    left = left.transpose(0, 3, 1, 2, 4, 5)
-    give = matmul(left[1].reshape(-1, rows), right).astype(jnp.bfloat16)
-    got = links.swap(give)
-    total = matmul(left[0].reshape(-1, rows), right) + got.astype(jnp.float32)
-    total = total.astype(jnp.bfloat16).reshape(nz, na, nb, half, width)
-    moving = total[nz - 1]
-    for at_z in range(nz - 2, -1, -1):
-        moving = add_low(total[at_z], links.shift(moving, "z"))
-    layer = moving
-    lines = []
-    for at_a in range(na):
-        moving = layer[at_a, nb - 1]
-        for at_b in range(nb - 2, -1, -1):
-            moving = add_low(layer[at_a, at_b], links.shift(moving, "b"))
-        lines.append(moving)
-    moving = lines[na - 1]
-    for at_a in range(na - 2, -1, -1):
-        moved = links.shift(moving, "a")
-        moving = lines[at_a].astype(jnp.float32) + moved.astype(jnp.float32)
-        if at_a > 0:
-            moving = moving.astype(jnp.bfloat16)
-    return moving.astype(jnp.float32)
-
-
-def add_low(first, second):
-    return (first.astype(jnp.float32) + second.astype(jnp.float32)).astype(jnp.bfloat16)
-
-
-def exchange(links, blocks):
-    nz, n1, n2 = links.sizes
-    blocks = blocks.reshape((nz, n1, n2) + blocks.shape[1:])
-    for axis, here in ((2, links.i2), (1, links.i1), (0, links.z)):
-        size = links.sizes[axis]
-        fresh = blocks
-        for steps in range(1, size):
-            part = lax.dynamic_slice_in_dim(blocks, (here + steps) % size, 1, axis)
-            moved = links.shift(part, axis, steps)
-            fresh = lax.dynamic_update_slice_in_dim(fresh, moved, (here - steps) % size, axis)
-        blocks = fresh
-    return blocks.reshape((nz * n1 * n2,) + blocks.shape[3:])
+def both_rows(links, left):
+    return jnp.concatenate([left[0], links.swap(left[1])], 4)
+
+
+def halves_total(left, right):
+    total = matmul(left.reshape(-1, left.shape[4]), right).astype(jnp.bfloat16)
+    return total.reshape(left.shape[:4] + (right.shape[1],))
+
+
+class Reduce:
+    def __init__(self, links, value, kinds):
+        self.links, self.value, self.kinds = links, value, list(kinds)
+        self.spot, self.moving = value.shape[0] - 1, value[value.shape[0] - 1]
+
+    def step(self, pace, steps=1):
+        if not self.kinds:
+            return []
+        if self.spot == 0:
+            self.kinds = self.kinds[1:]
+            if not self.kinds:
+                return []
+            self.value = self.moving
+            self.spot, self.moving = self.value.shape[0] - 1, self.value[self.value.shape[0] - 1]
+        self.moving = pace.tie(self.moving)
+        while self.spot > 0 and steps > 0:
+            moved = self.links.shift(self.moving, self.kinds[0])
+            self.spot, steps = self.spot - 1, steps - 1
+            self.moving = self.value[self.spot].astype(jnp.float32) + moved.astype(jnp.float32)
+            if self.spot > 0 or len(self.kinds) > 1:
+                self.moving = self.moving.astype(jnp.bfloat16)
+        return [self.moving]
+
+    def ring(self, pace):
+        return self.step(pace, 1000)
+
+    def done(self, pace):
+        while len(self.kinds) > 1 or (self.kinds and self.spot > 0):
+            self.ring(pace)
+        return self.moving.astype(jnp.float32)
+
+
+def exchange_along(links, blocks, axis):
+    here = (links.z, links.i1, links.i2)[axis]
+    size, fresh = links.sizes[axis], blocks
+    for steps in range(1, size):
+        part = lax.dynamic_slice_in_dim(blocks, (here + steps) % size, 1, axis)
+        moved = links.shift(part, axis, steps)
+        fresh = lax.dynamic_update_slice_in_dim(fresh, moved, (here - steps) % size, axis)
+    return fresh
+
+
+class Total:
+    def __init__(self, links, value):
+        self.links, self.value, self.ways = links, value, [None]
+        for axis in (2, 1, 0):
+            bit = 1
+            while bit < links.sizes[axis]:
+                self.ways.append((axis, bit))
+                bit = bit * 2
+
+    def step(self, pace):
+        if self.ways:
+            way, self.ways = self.ways[0], self.ways[1:]
+            self.value = pace.tie(self.value)
+            moved = self.links.swap(self.value) if way is None else self.links.flip(self.value, *way)
+            self.value = self.value + moved
+        return [self.value]
+
+    def done(self, pace):
+        while self.ways:
+            self.step(pace)
+        return self.value
 
 
 def all_sum(links, value):
@@ -367,30 +512,6 @@
     top_score = jnp.max(scores, -1, keepdims=True)
     powers = jnp.exp(scores - top_score)
     return powers / jnp.sum(powers, -1, keepdims=True)
-
-
-def first_layer_forward(state, w_qkv, w_up, w_out, vector, cosine, sine, allowed):
-    rows = state.shape[0]
-    first_gain, first_bias, second_gain, second_bias, bias_qkv, bias_attn, bias_up, bias_down = pieces(vector)
-    normal, scale = standard_deviation(state)
-    left = (normal * first_gain + first_bias).astype(jnp.bfloat16)
-    right = (normal * second_gain + second_bias).astype(jnp.bfloat16)
-    joined = matmul(left, w_qkv) + bias_qkv
-    upper = matmul(right, w_up) + bias_up
-    query = turn(joined[:, :D].reshape(rows, HEADS, HEAD_DIM), cosine, sine, 1.0).astype(jnp.bfloat16)
-    keys = turn(joined[:, D : 2 * D].reshape(rows, HEADS, HEAD_DIM), cosine, sine, 1.0).astype(jnp.bfloat16)
-    values = joined[:, 2 * D :].reshape(rows, HEADS, HEAD_DIM).astype(jnp.bfloat16)
-    weights = softmax_parts(scores_of(query, keys, allowed))
-    mixed = (
-        jnp.einsum("hqk,khe->qhe", weights.astype(jnp.bfloat16), values, preferred_element_type=jnp.float32)
-        .reshape(rows, D)
-        .astype(jnp.bfloat16)
-    )
-    active = jax.nn.gelu(upper, approximate=False).astype(jnp.bfloat16)
-    acts = jnp.concatenate([mixed, active], 1)
-    branch = matmul(mixed, w_out[:D]) + bias_attn + (matmul(active, w_out[D:]) + bias_down)
-    kept = (normal, scale, left, right, upper, query, keys, values, weights, acts)
-    return (state + branch, kept)
 
 
 def attention_backward(query, keys, values, weights, grad_mixed):
@@ -445,6 +566,103 @@
     weight_new = weight - rate * (moment_hat / (jnp.sqrt(second_hat) + ADAM_EPS) + decay * weight)
     average_new = EMA_KEEP * average + (1.0 - EMA_KEEP) * weight_new
     return (weight_new, moment_new, second_new, average_new)
+
+
+def low_rows(table, token):
+    features, vocabulary = table.shape
+    block = 4096
+
+    def kernel(table_ref, token_ref, out_ref):
+        out_ref[...] = table_ref[...].T.astype(jnp.bfloat16)
+
+    return pl.pallas_call(
+        kernel,
+        grid=(pl.cdiv(vocabulary, block),),
+        out_shape=jax.ShapeDtypeStruct((vocabulary, features), jnp.bfloat16),
+        in_specs=[
+            pl.BlockSpec((features, block), lambda at: (0, at)),
+            pl.BlockSpec(memory_space=pl.ANY),
+        ],
+        out_specs=pl.BlockSpec((block, features), lambda at: (at, 0)),
+        compiler_params=pltpu.CompilerParams(vmem_limit_bytes=48 * 1024 * 1024),
+        name="low_rows",
+    )(table, token)
+
+
+def sum_rows(ids, rows, count):
+    tokens, features = rows.shape
+    unroll, block = 32, 64
+
+    def kernel(ids_ref, rows_ref, out_ref, squares_ref):
+        def clear(at, carry):
+            out_ref[pl.ds(at * block, block), :] = jnp.zeros((block, features), jnp.float32)
+            return carry
+
+        lax.fori_loop(0, count // block, clear, 0)
+
+        def add(at, carry):
+            for step in range(unroll):
+                token = at * unroll + step
+                spot = ids_ref[token]
+                out_ref[pl.ds(spot, 1), :] = out_ref[pl.ds(spot, 1), :] + rows_ref[pl.ds(token, 1), :]
+            return carry
+
+        lax.fori_loop(0, tokens // unroll, add, 0)
+
+        def square(at, total):
+            value = out_ref[pl.ds(at * block, block), :]
+            return total + jnp.sum((value * value).reshape(block // 8, 8, features), 0)
+
+        total = lax.fori_loop(0, count // block, square, jnp.zeros((8, features), jnp.float32))
+        squares_ref[0, 0] = jnp.sum(total)
+
+    summed, squares = pl.pallas_call(
+        kernel,
+        out_shape=(
+            jax.ShapeDtypeStruct((count, features), jnp.float32),
+            jax.ShapeDtypeStruct((1, 1), jnp.float32),
+        ),
+        grid_spec=pltpu.PrefetchScalarGridSpec(
+            num_scalar_prefetch=1,
+            grid=(1,),
+            in_specs=[pl.BlockSpec((tokens, features), lambda at, ids: (0, 0))],
+            out_specs=[
+                pl.BlockSpec((count, features), lambda at, ids: (0, 0), pipeline_mode=pl.Buffered(1)),
+                pl.BlockSpec(memory_space=pltpu.SMEM),
+            ],
+        ),
+        compiler_params=pltpu.CompilerParams(vmem_limit_bytes=58 * 1024 * 1024),
+        name="sum_rows",
+    )(ids, rows)
+    return (summed, squares[0, 0])
+
+
+def table_update(table, moment, second, average, grad_rows, factor):
+    features, vocabulary = table.shape
+    block = 2048
+
+    def kernel(factor_ref, table_ref, moment_ref, second_ref, average_ref, grad_ref, *outs):
+        grad = grad_ref[...].T * factor_ref[0, 0]
+        parts = adamw_update(
+            table_ref[...], moment_ref[...], second_ref[...], average_ref[...], grad, RATE_MAT, WEIGHT_DECAY
+        )
+        for out, part in zip(outs, parts):
+            out[...] = part
+
+    wide = pl.BlockSpec((features, block), lambda at: (0, at))
+    return tuple(
+        pl.pallas_call(
+            kernel,
+            grid=(pl.cdiv(vocabulary, block),),
+            out_shape=[jax.ShapeDtypeStruct(table.shape, jnp.float32)] * 4,
+            in_specs=[pl.BlockSpec(memory_space=pltpu.SMEM)]
+            + [wide] * 4
+            + [pl.BlockSpec((block, features), lambda at: (at, 0))],
+            out_specs=[wide] * 4,
+            compiler_params=pltpu.CompilerParams(vmem_limit_bytes=48 * 1024 * 1024),
+            name="table_update",
+        )(factor.reshape(1, 1), table, moment, second, average, grad_rows)
+    )
 
 
 def body(
@@ -477,11 +695,33 @@
     micro, width = token_ids.shape
     mine_first = core == 0
 
+    pace = Pace()
+    low_in, low_out = in_w[0].astype(jnp.bfloat16), out_w[0].astype(jnp.bfloat16)
+
+    def halves(shard):
+        rows = shard.shape[0] // 2
+        keep = lax.dynamic_slice_in_dim(shard, core * rows, rows, 0)
+        give = lax.dynamic_slice_in_dim(shard, (1 - core) * rows, rows, 0)
+        got = links.swap(give)
+        return (jnp.where(mine_first, keep, got), jnp.where(mine_first, got, keep))
+
+    in_0, in_1 = halves(low_in)
+    out_0, out_1 = halves(low_out)
     own_vec, own_final = lax.reduce_precision(layer_vec[0], 8, 7), lax.reduce_precision(final_vec, 8, 7)
     vec_part, final_part = own_vec.shape[0], own_final.shape[0]
-    small = collect_small(
-        links, jnp.concatenate([own_vec, own_final, token_ids.astype(jnp.float32).reshape(-1)])
-    )
+    small = Small(links, jnp.concatenate([own_vec, own_final, token_ids.astype(jnp.float32).reshape(-1)]))
+    pace.close(in_0, out_0, *small.along(pace))
+    w_in_0 = lax.all_gather(in_0, ("dp", "section"), axis=0, tiled=True)
+    w_up_1 = lax.all_gather(in_1[:, 3 * D :], ("dp", "section"), axis=0, tiled=True)
+    w_out_1 = lax.all_gather(out_1, ("dp", "section"), axis=0, tiled=True)
+    out_0, qkv_1 = Gather(links, out_0), Gather(links, in_1[:, : 3 * D])
+    pace.close(*small.along(pace))
+    table_rows = low_rows(table, pace.token)
+    pace.close(*small.along(pace), peek(table_rows))
+    pace.close(*small.wave(pace))
+    pace.close(*small.wave(pace))
+    lengths = lax.dynamic_slice_in_dim(seg_lengths, core, 1, 0)[0]
+    small = small.whole(pace)
     small_other = links.swap(small[:, :vec_part])
     own_layer, other_layer = small[:, :vec_part].reshape(-1), small_other.reshape(-1)
     vector_0 = jnp.where(mine_first, own_layer, other_layer)
@@ -489,37 +729,56 @@
     final = small[:, vec_part : vec_part + final_part].reshape(-1)
     every_ids = small[:, vec_part + final_part :].astype(jnp.int32).reshape(count, micro, width)
 
-    low_in, low_out = in_w[0].astype(jnp.bfloat16), out_w[0].astype(jnp.bfloat16)
-
-    def halves(shard):
-        rows = shard.shape[0] // 2
-        keep = lax.dynamic_slice_in_dim(shard, core * rows, rows, 0)
-        give = lax.dynamic_slice_in_dim(shard, (1 - core) * rows, rows, 0)
-        got = links.swap(give)
-        return (jnp.where(mine_first, keep, got), jnp.where(mine_first, got, keep))
-
-    in_0, in_1 = halves(low_in)
-    out_0, out_1 = halves(low_out)
-    w_qkv_0 = collect_layers_first(links, in_0[:, : 3 * D])
-    w_up_0 = collect_layers_first(links, in_0[:, 3 * D :])
-    w_out_0 = collect_layers_first(links, out_0)
-    w_qkv_1 = collect_layers_first(links, in_1[:, : 3 * D])
-    w_out_1 = collect_layers_last(links, out_1)
-    w_up_1 = collect_layers_first(links, in_1[:, 3 * D :])
-
     ids_here = lax.dynamic_slice_in_dim(every_ids, core, 1, 1).reshape(-1)
-    picked = jnp.take(table, ids_here, axis=1).astype(jnp.bfloat16)
-    features = picked.shape[0]
-    blocks = picked.reshape(features, count, width).transpose(1, 0, 2)
-    state = exchange(links, blocks).reshape(D, width).T.astype(jnp.float32)
-
-    lengths = lax.dynamic_slice_in_dim(seg_lengths, core, 1, 0)[0]
+    picked = jnp.take(table_rows, pace.tie(ids_here), axis=0, mode="clip")
+    features = picked.shape[1]
+    blocks = picked.reshape(links.sizes + (width, features)).transpose(0, 1, 2, 4, 3)
+    pace.close(peek(blocks), *out_0.along(pace, 1))
+    blocks = exchange_along(links, pace.tie(blocks), 2)
+    pace.close(peek(blocks), *out_0.along(pace, 1))
+    blocks = exchange_along(links, pace.tie(blocks), 1)
+    pace.close(peek(blocks), *out_0.along(pace))
+    blocks = exchange_along(links, pace.tie(blocks), 0)
+    pace.close(peek(blocks))
+    state = blocks.reshape(D, width).T.astype(jnp.float32)
+
     ranking = lax.dynamic_slice_in_dim(rankings, core, 1, 0)[0]
     position, allowed, last = layout(lengths, width)
     cosine, sine = angles(position)
 
-    state_1, kept = first_layer_forward(state, w_qkv_0, w_up_0, w_out_0, vector_0, cosine, sine, allowed)
+    first_gain, first_bias, second_gain, second_bias, bias_qkv, bias_attn, bias_up, bias_down = pieces(vector_0)
+    normal, scale = standard_deviation(state)
+    left = (normal * first_gain + first_bias).astype(jnp.bfloat16)
+    right = (normal * second_gain + second_bias).astype(jnp.bfloat16)
+    joined = matmul(pace.tie(left), w_in_0[:, : 3 * D]) + bias_qkv
+    query = turn(joined[:, :D].reshape(width, HEADS, HEAD_DIM), cosine, sine, 1.0).astype(jnp.bfloat16)
+    keys = turn(joined[:, D : 2 * D].reshape(width, HEADS, HEAD_DIM), cosine, sine, 1.0).astype(jnp.bfloat16)
+    values = joined[:, 2 * D :].reshape(width, HEADS, HEAD_DIM).astype(jnp.bfloat16)
+    weights = softmax_parts(scores_of(query, keys, allowed))
+    mixed = (
+        jnp.einsum("hqk,khe->qhe", weights.astype(jnp.bfloat16), values, preferred_element_type=jnp.float32)
+        .reshape(width, D)
+        .astype(jnp.bfloat16)
+    )
+    pace.close(*out_0.wave(pace), *qkv_1.along(pace, 1), peek(mixed))
+    upper = matmul(pace.tie(right), w_in_0[:, 3 * D :]) + bias_up
+    active = jax.nn.gelu(upper, approximate=False).astype(jnp.bfloat16)
+    pace.close(*out_0.wave(pace), *qkv_1.along(pace, 1), peek(active))
+    left_both = both_rows(links, relative_rows(links, left))
+    right_both = both_rows(links, relative_rows(links, right))
+    pace.close(*out_0.last(pace), *qkv_1.along(pace), peek(left_both), peek(right_both))
+    w_out_0 = out_0.whole()
+    acts = jnp.concatenate([mixed, active], 1)
+    state_1 = (
+        state + matmul(mixed, w_out_0[:D]) + bias_attn + (matmul(pace.tie(active), w_out_0[D:]) + bias_down)
+    )
     state_1 = lax.reduce_precision(state_1, 8, 7)
+    kept = (normal, scale, left, right, upper, query, keys, values, weights, acts)
+    pace.close(*qkv_1.wave(pace), peek(state_1))
+    pace.close(*qkv_1.wave(pace))
+    pace.close(*qkv_1.last(pace))
+    w_qkv_1 = qkv_1.whole()
+    state_1 = pace.tie(state_1)
 
     ends = last.shape[0]
     first_gain, first_bias, second_gain, second_bias, bias_qkv, bias_attn, bias_up, bias_down = pieces(vector_1)
@@ -581,39 +840,26 @@
     grad_state = landed + norm_gradient_pass(pulled, normal, scale)
     grad_state = lax.reduce_precision(grad_state, 8, 7).astype(jnp.bfloat16)
 
-    pair_half = reduce_layers_first(links, relative_rows(links, left), grad_pairs)
+    pairs_both = both_rows(links, relative_rows(links, left))
+    pairs_grad = jnp.concatenate([grad_pairs, links.swap(grad_pairs)])
     factors = jnp.concatenate([left_end, right_end, mixed, active, grad_query, grad_upper, low_end], 1)
-    every_factor = collect_layers_first(links, factors)
+    every_factor = lax.all_gather(factors, ("dp", "section"), axis=0, tiled=True)
     in_rows, out_rows = in_w.shape[1], out_w.shape[1]
-
-    def factor_part(begin, size):
-        return every_factor[:, begin : begin + size]
-
-    left_own = lax.dynamic_slice_in_dim(factor_part(0, D), place * in_rows, in_rows, 1)
-    right_own = lax.dynamic_slice_in_dim(factor_part(D, D), place * in_rows, in_rows, 1)
-    acts_own = lax.dynamic_slice_in_dim(factor_part(2 * D, D + FF), place * out_rows, out_rows, 1)
-    query_part = factor_part(3 * D + FF, D)
-    upper_part = factor_part(4 * D + FF, FF)
-    end_part = factor_part(4 * D + 2 * FF, D)
-    grad_in_query = dot_rows(left_own, query_part)
-    grad_in_upper = dot_rows(right_own, upper_part)
-    grad_out_1 = dot_rows(acts_own, end_part)
 
     normal, scale, left, right, upper, query, keys, values, weights, acts = kept
     first_gain, first_bias, second_gain, second_bias = pieces(vector_0)[:4]
     low_state = grad_state
-    acts_relative = relative_rows(links, acts)
-    out_half = jnp.concatenate(
-        [
-            reduce_layers_last(links, acts_relative, low_state[:, : D // 2]),
-            reduce_layers_first(links, acts_relative, low_state[:, D // 2 :]),
-        ],
-        1,
-    )
+    pair_sum = Reduce(links, halves_total(pairs_both, pairs_grad), "baz")
+    pace.close(peek(pair_sum.moving), peek(low_state))
+    low_state = pace.tie(low_state)
+    out_half = dot_rows(acts, low_state).astype(jnp.bfloat16)
+    out_half = lax.psum_scatter(out_half, ("dp", "section"), scatter_dimension=0, tiled=True)
     grad_mixed = dot_cols(low_state, w_out_0[:D]).astype(jnp.bfloat16).reshape(width, HEADS, HEAD_DIM)
     grad_upper = (dot_cols(low_state, w_out_0[D:]) * gelu_slope(upper)).astype(jnp.bfloat16)
-    up_half = reduce_layers_first(links, relative_rows(links, right), grad_upper)
-    grad_query, grad_keys, grad_values = attention_backward(query, keys, values, weights, grad_mixed)
+    upper_both = jnp.concatenate([grad_upper, links.swap(grad_upper)])
+    pace.close(*map(peek, pair_sum.ring(pace)), peek(grad_mixed), peek(upper_both))
+    up_sum = halves_total(right_both, pace.tie(upper_both))
+    grad_query, grad_keys, grad_values = attention_backward(query, keys, values, weights, pace.tie(grad_mixed))
     grad_joined = jnp.concatenate(
         [
             turn(grad_query, cosine, sine, -1.0).reshape(width, D),
@@ -622,8 +868,23 @@
         ],
         1,
     ).astype(jnp.bfloat16)
-    back_left = dot_cols(grad_joined, w_qkv_0)
-    back_right = dot_cols(grad_upper, w_up_0)
+    pace.close(*map(peek, pair_sum.ring(pace)), peek(up_sum), peek(grad_joined))
+    up_sum = Reduce(links, up_sum, "baz")
+    grad_joined = pace.tie(grad_joined)
+    back_left = dot_cols(grad_joined, w_in_0[:, : 3 * D])
+    back_right = dot_cols(grad_upper, w_in_0[:, 3 * D :])
+    grad_embedded = low_state.astype(jnp.float32) + norm_gradient_pass(
+        back_left * first_gain + back_right * second_gain, normal, scale
+    )
+    joined_both = jnp.concatenate([grad_joined, links.swap(grad_joined)])
+    blocks = grad_embedded.astype(jnp.bfloat16).T.reshape(links.sizes + (features, width))
+    pace.close(*map(peek, up_sum.ring(pace) + pair_sum.step(pace)), peek(joined_both), peek(blocks))
+    blocks = exchange_along(links, pace.tie(blocks), 2)
+    qkv_sum = halves_total(left_both, pace.tie(joined_both))
+    pace.close(*map(peek, pair_sum.step(pace)), peek(blocks), peek(qkv_sum))
+    qkv_sum = Reduce(links, qkv_sum, "baz")
+    blocks = exchange_along(links, pace.tie(blocks), 1)
+    back_left, back_right = pace.tie(back_left), pace.tie(back_right)
     sum_state = total_rows(low_state)
     sum_vec_0 = jnp.concatenate(
         [
@@ -637,21 +898,39 @@
             sum_state,
         ]
     )
-    grad_embedded = low_state.astype(jnp.float32) + norm_gradient_pass(
-        back_left * first_gain + back_right * second_gain, normal, scale
-    )
-    qkv_half = reduce_layers_first(links, relative_rows(links, left), grad_joined)
-
-    blocks = grad_embedded.astype(jnp.bfloat16).T.reshape(count, features, width)
-    spread_mine = exchange(links, blocks).transpose(1, 0, 2)
+    packed = jnp.concatenate([sum_vec_0, sum_vec_1, grad_final, loss[None], jnp.zeros((127,), jnp.float32)])
+    packed = Total(links, packed.reshape(-1, 128))
+    pace.close(*map(peek, pair_sum.step(pace)), peek(blocks), packed.value)
+    blocks = exchange_along(links, pace.tie(blocks), 0)
+    pace.close(*map(peek, up_sum.ring(pace)), peek(blocks), *packed.step(pace))
+    blocks = pace.tie(blocks)
+    spread_mine = blocks.reshape(count, features, width).transpose(0, 2, 1)
     spread_other = links.swap(spread_mine)
     spread = jnp.stack(
-        [jnp.where(mine_first, spread_mine, spread_other), jnp.where(mine_first, spread_other, spread_mine)], 2
-    ).reshape(features, count * micro * width)
-    table_grad = jnp.zeros(table.shape, jnp.float32).at[:, every_ids.reshape(-1)].add(spread.astype(jnp.float32))
-
-    packed = jnp.concatenate([sum_vec_0, sum_vec_1, grad_final, loss[None], jnp.zeros((127,), jnp.float32)])
-    packed = all_sum(links, packed.reshape(-1, 128)).reshape(-1)
+        [jnp.where(mine_first, spread_mine, spread_other), jnp.where(mine_first, spread_other, spread_mine)], 1
+    ).reshape(count * micro * width, features)
+    table_grad, table_squares = sum_rows(every_ids.reshape(-1), spread.astype(jnp.float32), table.shape[1])
+    pace.close(*map(peek, up_sum.step(pace) + qkv_sum.ring(pace)), peek(table_grad))
+    pace.close(*map(peek, up_sum.step(pace) + qkv_sum.ring(pace)), *packed.step(pace))
+    pace.close(*map(peek, up_sum.ring(pace) + qkv_sum.step(pace)), *packed.step(pace))
+    pace.close(*map(peek, qkv_sum.step(pace)), *packed.step(pace))
+    pace.close(*map(peek, qkv_sum.ring(pace)), *packed.step(pace))
+    up_half, pair_half, qkv_half = up_sum.done(pace), pair_sum.done(pace), qkv_sum.done(pace)
+    def factor_part(begin, size):
+        return every_factor[:, begin : begin + size]
+
+    left_own = lax.dynamic_slice_in_dim(factor_part(0, D), place * in_rows, in_rows, 1)
+    right_own = lax.dynamic_slice_in_dim(factor_part(D, D), place * in_rows, in_rows, 1)
+    acts_own = lax.dynamic_slice_in_dim(factor_part(2 * D, D + FF), place * out_rows, out_rows, 1)
+    query_part = factor_part(3 * D + FF, D)
+    upper_part = factor_part(4 * D + FF, FF)
+    end_part = factor_part(4 * D + 2 * FF, D)
+    grad_in_query = dot_rows(left_own, query_part)
+    grad_in_upper = dot_rows(right_own, upper_part)
+    grad_out_1 = dot_rows(acts_own, end_part)
+
+
+    packed = packed.done(pace).reshape(-1)
     vec_size = sum_vec_0.shape[0]
     shard_vec = lax.dynamic_slice_in_dim(packed, core * vec_size + place * vec_part, vec_part, 0)
     shard_fin = lax.dynamic_slice_in_dim(packed, 2 * vec_size + place * final_part, final_part, 0)
@@ -660,7 +939,8 @@
     in_half = jnp.concatenate([qkv_half, up_half], 1)
     in_other, out_other, pair_other = links.swap(in_half), links.swap(out_half), links.swap(pair_half)
     grad_in_0 = jnp.concatenate([in_half, in_other], 0)
-    grad_out_0 = jnp.concatenate([out_half, out_other], 0)
+    out_half = out_half.astype(jnp.float32)
+    grad_out_0 = jnp.concatenate([out_half, out_other.astype(jnp.float32)], 0)
     grad_in_1 = jnp.concatenate(
         [grad_in_query, jnp.concatenate([pair_other, pair_half], 0), grad_in_upper], 1
     )
@@ -671,12 +951,12 @@
         jnp.sum(shard_in * shard_in)
         + jnp.sum(shard_out * shard_out)
         + jnp.sum(shard_vec * shard_vec)
-        + jnp.where(mine_first, jnp.sum(table_grad * table_grad) + jnp.sum(shard_fin * shard_fin), 0.0)
+        + jnp.where(mine_first, table_squares + jnp.sum(shard_fin * shard_fin), 0.0)
     )
     total_squares = all_sum(links, jnp.broadcast_to(squares, (8, 128)))[0, 0]
     grad_norm = jnp.sqrt(total_squares)
     factor = jnp.minimum(1.0, CLIP_NORM / (grad_norm + 1e-06))
-    table_parts = adamw_update(table, table_m, table_v, table_ema, table_grad * factor, RATE_MAT, WEIGHT_DECAY)
+    table_parts = table_update(table, table_m, table_v, table_ema, table_grad, factor)
     in_parts = adamw_update(
         in_w, in_m, in_v, in_ema, shard_in.reshape(in_w.shape) * factor, RATE_MAT, WEIGHT_DECAY
     )

time: 1080 us -> 822 us (0.76)
  waiting for transfers between devices: 431 us -> 133 us
  Pallas kernels: 0 us -> 134 us
  other arithmetic: 181 us -> 108 us
  local copies, waits for them, and re-layouts: 223 us -> 177 us
  starting transfers between devices: 89.9 us -> 111 us
  between operations: 9.89 us -> 22 us
    ppermute x88 -> x43, waiting for transfers between devices: 398 us -> 111 us  [shift(): return lax.ppermute(value, ('section', 'dp'), pairs)]
    pallas_call x0 -> x91, Pallas kernels: none -> 134 us  [the longest x1 52.2 us: table_update(): pl.pallas_call(kernel, grid=(pl.cdiv(vocabulary, block),), out_shape=[jax...]
    dynamic_update_slice x82 -> x8, local copies, waits for them, and re-layouts: 82.8 us -> 6.38 us  [update(): return lax.dynamic_update_slice(whole, part, starts)]
    scatter-add x1 -> x0, other arithmetic: 49 us -> none  [body(): jnp.zeros(table.shape, jnp.float32).at[:, every_ids.reshape(-1)]]
    add x5 -> x4, other arithmetic: 54.8 us -> 9.74 us  [adamw_update(): average_new = EMA_KEEP * average + (1.0 - EMA_KEEP) * weight_new]
    slice x11 -> x48, local copies, waits for them, and re-layouts: 5.74 us -> 47.8 us  [the longest x37 29.2 us: peek(): lax.slice(value, (0,) * value.ndim, (1,) * (value.ndim - 2) + tuple(ends))]
    ppermute x42 -> x23, starting transfers between devices: 8.1 us -> 44.8 us  [swap(): return lax.ppermute(value, 'section', [(0, 1), (1, 0)])]
    another operation x16 -> x5, local copies, waits for them, and re-layouts: 22 us -> 0.81 us  [the longest x4 0.72 us: wave(): self.found = {(0, 0): jnp.stack(self.pieces)}]
  transfers between devices with their start and end apart: 138 -> 79, of which waited for: 58 -> 33; matrix products, arithmetic and copies ran while one was open for 38% -> 42% of each run, Pallas kernels for 0% -> 10%
where the time goes in v2:
time: 822 us; the launch traced here: 811 us
  local copies, waits for them, and re-layouts  177 us (22%)
  Pallas kernels  134 us (16%)
  waiting for transfers between devices  133 us (16%)
  matrix products  125 us (15%)
  starting transfers between devices  111 us (14%)
  other arithmetic  108 us (13%)
  between operations  22 us (3%)
    ppermute x43, waiting for transfers between devices, shift(): return lax.ppermute(value, ('section', 'dp'), pairs)  111 us
    ppermute x43, starting transfers between devices, shift(): return lax.ppermute(value, ('section', 'dp'), pairs)  63.2 us
    pallas_call x1, Pallas kernels, table_update(): pl.pallas_call(kernel, grid=(pl.cdiv(vocabulary, block),), out_shape=[jax...  52.2 us
    dot_general x12, matrix products, matmul(): jnp.dot(left_operand, right_operand, preferred_element_type=jnp.float32)  51 us
    ppermute x23, starting transfers between devices, swap(): return lax.ppermute(value, 'section', [(0, 1), (1, 0)])  44.8 us
    pallas_call x1, Pallas kernels, sum_rows(): pl.pallas_call(kernel, out_shape=(jax.ShapeDtypeStruct((count, features),...  42.9 us
    dot_general x9, matrix products, dot_cols(): lax.dot_general(left_operand, right_operand, (((1,), (1,)), ((), ())), pr...  42.8 us
    unnamed x348, local copies, waits for them, and re-layouts  42.1 us
  transfers between devices with their start and end apart: 79, of which 33 were waited for; matrix products, arithmetic and copies ran while one was open for 42% of the time, Pallas kernels for 10%

profile of v2, /device:TPU:0, one launch (start us, length us, event | category | flops | bytes accessed | tf_op | source)
XLA Modules:
  0.0 811.0 jit_solution(9163857255498817576)
XLA Ops:
  30.9 15.6 %low_rows.1 = bf16[50304,64]{1,0:T(8,128)(2,1)} custom-call(f32[64,50304]{1,0:T(8,128)} %table_ref.3, f32[8,128]{1,0:T(8,128)S(1)} %copy-done.27), custom_call_target="tpu_custom_call" | custom-call | tf_op jit(solution)/shard_map/low_rows/pallas_call | solution.py:578
  65.8 12.1 %gather_fusion = bf16[3584,64]{1,0:T(8,128)(2,1)S(1)} fusion(bf16[50304,64]{1,0:T(8,128)(2,1)} %low_rows.1, s32[4096]{0:T(1024)S(1)} %pad_clamp_fusion), kind=kCustom, calls=%fused_computation | custom fusion | bytes 931840 | tf_op jit(solution)/shard_map/jit(_take)/gather | solution.py:733
  84.9 11.1 %collective-permute-done.9 = bf16[4,2,1,64,224]{4,3,2,1,0:T(8,128)(2,1)S(1)} collective-permute-done((bf16[4,2,1,64,224]{4,3,2,1,0:T(8,128)(2,1)S(1)}, bf16[4,2,1,64,224]{4,3,2,1,0:T(8,128)(2,1)S(1)}, u32[]{:S(2)}, u32[]{:S(2)}) %collective-permute-start.9) | collective-permute-done | bytes 229408 | tf_op jit(solution)/shard_map/ppermute | solution.py:155
  107.1 7.0 collective-permute-start.12
  118.5 12.0 %collective-permute-done.12.refs_1_ = bf16[160,1024]{1,0:T(8,128)(2,1)S(1)} collective-permute-done((bf16[160,1024]{1,0:T(8,128)(2,1)}, bf16[160,1024]{1,0:T(8,128)(2,1)S(1)}, u32[]{:S(2)}, u32[]{:S(2)}) %collective-permute-start.12) | collective-permute-done | bytes 327712 | tf_op jit(solution)/shard_map/ppermute | solution.py:155
  132.7 5.5 collective-permute-start.13
  221.3 13.1 %fusion.43 = (bf16[224,4096]{1,0:T(8,128)(2,1)S(1)}, f32[224,4096]{1,0:T(8,128)}) fusion(f32[4096]{0:T(1024)S(1)} %slice-done.3, bf16[224,1024]{1,0:T(8,128)(2,1)} %behind.76, bf16[1024,7168]{1,0:T(8,128)(2,1)} %all-gather.6.cloned.1.call-done), kind=kOutput, calls=%fused_computation.46 | convolution fusion | flops 1939603456 | bytes 14368768 | tf_op jit(solution)/shard_map/dot_general | solution.py:29
  260.6 5.6 place.2
  266.3 5.5 fusion.107
  274.8 6.0 collective-permute-done.27.refs_2_.refs_0_
  350.6 6.3 convert_reduce_fusion.5
  360.9 6.4 fusion.238
  379.4 8.1 %convert_reduce_fusion = (f32[4096]{0:T(1024)}, bf16[224,4096]{1,0:T(8,128)(2,1)}) fusion(f32[224,4096]{1,0:T(8,128)} %get-tuple-element.215, bf16[224,1024]{1,0:T(8,128)(2,1)} %behind.85, bf16[5120,1024]{1,0:T(8,128)(2,1)} %bitcast.318), kind=kOutput, calls=%fused_computation.52 | convolution fusion | flops 1890054144 | bytes 14368768 | tf_op jit(solution)/shard_map/dot_general | solution.py:39
  395.4 7.6 convolution_convert_fusion
  449.3 8.1 fusion.237
  466.7 15.3 %collective-permute-done.41 = bf16[2,4,32,4096]{3,2,1,0:T(8,128)(2,1)} collective-permute-done((bf16[2,4,32,4096]{3,2,1,0:T(8,128)(2,1)}, bf16[2,4,32,4096]{3,2,1,0:T(8,128)(2,1)}, u32[]{:S(2)}, u32[]{:S(2)}) %collective-permute-start.41) | collective-permute-done | bytes 2097184 | tf_op jit(solution)/shard_map/ppermute | solution.py:155
  499.5 6.6 collective-permute-done.43
  524.6 35.8 %collective-permute-start.48 = (f32[233,128]{1,0:T(8,128)}, f32[233,128]{1,0:T(8,128)S(1)}, u32[]{:S(2)}, u32[]{:S(2)}) collective-permute-start(f32[233,128]{1,0:T(8,128)} %behind.100), channel_id=1, source_target_pairs={{0,16},{16,0},{1,17},{17,1},{2,18},{18,2},{3,19},{19,3},{4,20},{20... | collective-permute-start | bytes 357896 | tf_op jit(solution)/shard_map/ppermute | solution.py:161
  578.0 5.4 collective-permute-start.53
  597.4 42.9 %sum_rows.1 = (f32[50304,64]{1,0:T(8,128)}, f32[1,1]{1,0:T(1,128)}) custom-call(s32[7168]{0:T(1024)} %reshape_reshape.3.ids_ref, f32[7168,64]{1,0:T(8,128)} %bitcast.320), custom_call_target="tpu_custom_call" | custom-call | tf_op jit(solution)/shard_map/sum_rows/pallas_call | solution.py:619
  672.7 6.9 collective-permute-done.60
  685.5 6.5 collective-permute-done.62
  698.5 5.6 collective-permute-done.65
  741.0 52.2 %table_update.1 = (f32[64,50304]{1,0:T(8,128)}, f32[64,50304]{1,0:T(8,128)}, f32[64,50304]{1,0:T(8,128)}, f32[64,50304]{1,0:T(8,128)}) custom-call(f32[1,1]{1,0:T(1,128)} %bitcast.128.factor_ref, f32[64,50304]{1,0:T(8,128)} %table_ref.3, f32[64,50304]{1,0:T(8,128)} %moment_ref.1, f32[64,50304]{1,0:T(8,128)} %second_ref.1, f32[64,50304]{1,0:T(8,128)} %average_ref.1, ...), custom_call_target="tpu_custom_call" | custom-call | tf_op jit(solution)/shard_map/table_update/pallas_call | solution.py:654
  (940 shorter events, 481.8 us)
Async XLA Ops:
  7.2 176.2 %all-gather.6.cloned.1.call-start = ((), (), s32[]{:S(2)}) async-start(), calls=%async_computation.1 | async-start | bytes 15138816 | tf_op jit(solution)/shard_map/all_gather | solution.py:714
  11.9 315.5 %all-gather.10.cloned.1.call-start = ((), (), s32[]{:S(2)}) async-start(), calls=%async_computation.3 | async-start | bytes 8650752 | tf_op jit(solution)/shard_map/all_gather | solution.py:715
  12.7 319.8 %all-gather.8.cloned.1.call-start = ((), (), s32[]{:S(2)}) async-start(), calls=%async_computation.2 | async-start | bytes 10813440 | tf_op jit(solution)/shard_map/all_gather | solution.py:716
  25.2 639.0 %all-gather.12.cloned.1.call-start = ((), (), s32[]{:S(2)}) async-start(), calls=%async_computation.5 | async-start | bytes 3514368 | tf_op jit(solution)/shard_map/all_gather | solution.py:846
  29.6 18.3 %collective-permute-start.4 = (f32[1472]{0:T(1024)}, f32[1472]{0:T(1024)S(1)}, u32[]{:S(2)}, u32[]{:S(2)}) collective-permute-start(f32[1472]{0:T(1024)} %behind.59), channel_id=1, source_target_pairs={{0,4},{1,5},{2,6},{3,7},{4,8},{5,9},{6,10},{7,11},{8,12},{9,13},{1... | collective-permute-start | bytes 17672 | tf_op jit(solution)/shard_map/ppermute | solution.py:155
  83.9 19.4 %collective-permute-start.10 = (bf16[160,1024]{1,0:T(8,128)(2,1)}, bf16[160,1024]{1,0:T(8,128)(2,1)S(1)}, u32[]{:S(2)}, u32[]{:S(2)}) collective-permute-start(bf16[160,1024]{1,0:T(8,128)(2,1)} %behind.66), channel_id=1, source_target_pairs={{0,4},{1,5},{2,6},{3,7},{4,8},{5,9},{6,10},{7,11},{8,12},{9,13},{1... | collective-permute-start | bytes 983048 | tf_op jit(solution)/shard_map/ppermute | solution.py:155
  107.1 23.4 %collective-permute-start.12 = (bf16[160,1024]{1,0:T(8,128)(2,1)}, bf16[160,1024]{1,0:T(8,128)(2,1)S(1)}, u32[]{:S(2)}, u32[]{:S(2)}) collective-permute-start(bf16[160,1024]{1,0:T(8,128)(2,1)} %behind.68), channel_id=1, source_target_pairs={{0,4},{1,5},{2,6},{3,7},{4,8},{5,9},{6,10},{7,11},{8,12},{9,13},{1... | collective-permute-start | bytes 983048 | tf_op jit(solution)/shard_map/ppermute | solution.py:155
  161.4 56.0 %collective-permute-start.17 = (bf16[4,160,1024]{2,1,0:T(8,128)(2,1)}, bf16[4,160,1024]{2,1,0:T(8,128)(2,1)}, u32[]{:S(2)}, u32[]{:S(2)}) collective-permute-start(bf16[4,160,1024]{2,1,0:T(8,128)(2,1)} %behind.71.refs_0_), channel_id=1, source_target_pairs={{0,16},{16,0},{1,17},{17,1},{2,18},{18,2},{3,19},{19,3},{4,20},{20... | collective-permute-start | bytes 3932168 | tf_op jit(solution)/shard_map/ppermute | solution.py:161
  161.4 56.0 %collective-permute-start.18 = (bf16[4,160,1024]{2,1,0:T(8,128)(2,1)}, bf16[4,160,1024]{2,1,0:T(8,128)(2,1)S(1)}, u32[]{:S(2)}, u32[]{:S(2)}) collective-permute-start(bf16[4,160,1024]{2,1,0:T(8,128)(2,1)} %behind.71.refs_0_), channel_id=1, source_target_pairs={{0,2},{1,3},{2,0},{3,1},{4,6},{5,7},{6,4},{7,5},{8,10},{9,11},{10,... | collective-permute-start | bytes 3932168 | tf_op jit(solution)/shard_map/ppermute | solution.py:155
  163.2 54.2 %collective-permute-start.19 = (bf16[4,160,1024]{2,1,0:T(8,128)(2,1)}, bf16[4,160,1024]{2,1,0:T(8,128)(2,1)S(1)}, u32[]{:S(2)}, u32[]{:S(2)}) collective-permute-start(bf16[4,160,1024]{2,1,0:T(8,128)(2,1)} %behind.71.refs_0_), channel_id=1, source_target_pairs={{0,1},{1,0},{2,3},{3,2},{4,5},{5,4},{6,7},{7,6},{8,9},{9,8},{10,11... | collective-permute-start | bytes 3932168 | tf_op jit(solution)/shard_map/ppermute | solution.py:155
  252.9 27.9 %collective-permute-start.27 = (bf16[4,32,3072]{2,1,0:T(8,128)(2,1)}, bf16[4,32,3072]{2,1,0:T(8,128)(2,1)}, u32[]{:S(2)}, u32[]{:S(2)}) collective-permute-start(bf16[4,32,3072]{2,1,0:T(8,128)(2,1)} %behind.80.refs_0_), channel_id=1, source_target_pairs={{0,1},{1,0},{2,3},{3,2},{4,5},{5,4},{6,7},{7,6},{8,9},{9,8},{10,11... | collective-permute-start | bytes 2359304 | tf_op jit(solution)/shard_map/ppermute | solution.py:155
  254.8 26.0 %collective-permute-start.28 = (bf16[4,32,3072]{2,1,0:T(8,128)(2,1)}, bf16[4,32,3072]{2,1,0:T(8,128)(2,1)}, u32[]{:S(2)}, u32[]{:S(2)}) collective-permute-start(bf16[4,32,3072]{2,1,0:T(8,128)(2,1)} %behind.80.refs_0_), channel_id=1, source_target_pairs={{0,16},{16,0},{1,17},{17,1},{2,18},{18,2},{3,19},{19,3},{4,20},{20... | collective-permute-start | bytes 2359304 | tf_op jit(solution)/shard_map/ppermute | solution.py:161
  254.8 26.0 %collective-permute-start.29 = (bf16[4,32,3072]{2,1,0:T(8,128)(2,1)}, bf16[4,32,3072]{2,1,0:T(8,128)(2,1)S(1)}, u32[]{:S(2)}, u32[]{:S(2)}) collective-permute-start(bf16[4,32,3072]{2,1,0:T(8,128)(2,1)} %behind.80.refs_0_), channel_id=1, source_target_pairs={{0,2},{1,3},{2,0},{3,1},{4,6},{5,7},{6,4},{7,5},{8,10},{9,11},{10,... | collective-permute-start | bytes 2359304 | tf_op jit(solution)/shard_map/ppermute | solution.py:155
  350.3 25.3 %collective-permute-start.35 = (bf16[224,2048]{1,0:T(8,128)(2,1)S(1)}, bf16[224,2048]{1,0:T(8,128)(2,1)}, u32[]{:S(2)}, u32[]{:S(2)}) collective-permute-start(bf16[224,2048]{1,0:T(8,128)(2,1)S(1)} %pad_maximum_fusion.3), channel_id=1, source_target_pairs={{0,16},{16,0},{1,17},{17,1},{2,18},{18,2},{3,19},{19,3},{4,20},{20... | collective-permute-start | bytes 2752520 | tf_op jit(solution)/shard_map/ppermute | solution.py:161
  357.6 352.6 %reduce-scatter.2.cloned.1.call-start = ((), (), s32[]{:S(2)}) async-start(), calls=%async_computation.4 | async-start | bytes 10813440 | tf_op jit(solution)/shard_map/reduce_scatter | solution.py:856
  379.4 23.6 %collective-permute-start.36 = (bf16[2,4,32,2048]{3,2,1,0:T(8,128)(2,1)}, bf16[2,4,32,2048]{3,2,1,0:T(8,128)(2,1)}, u32[]{:S(2)}, u32[]{:S(2)}) collective-permute-start(bf16[2,4,32,2048]{3,2,1,0:T(8,128)(2,1)} %behind.86), channel_id=1, source_target_pairs={{0,2},{1,3},{2,0},{3,1},{4,6},{5,7},{6,4},{7,5},{8,10},{9,11},{10,... | collective-permute-start | bytes 3145736 | tf_op jit(solution)/shard_map/ppermute | solution.py:155
  391.3 36.9 %collective-permute-start.39 = (bf16[224,4096]{1,0:T(8,128)(2,1)}, bf16[224,4096]{1,0:T(8,128)(2,1)}, u32[]{:S(2)}, u32[]{:S(2)}) collective-permute-start(bf16[224,4096]{1,0:T(8,128)(2,1)} %get-tuple-element.224), channel_id=1, source_target_pairs={{0,16},{16,0},{1,17},{17,1},{2,18},{18,2},{3,19},{19,3},{4,20},{20... | collective-permute-start | bytes 5505032 | tf_op jit(solution)/shard_map/ppermute | solution.py:161
  443.0 20.4 %collective-permute-start.45 = (bf16[224,3072]{1,0:T(8,128)(2,1)}, bf16[224,3072]{1,0:T(8,128)(2,1)}, u32[]{:S(2)}, u32[]{:S(2)}) collective-permute-start(bf16[224,3072]{1,0:T(8,128)(2,1)} %behind.90), channel_id=1, source_target_pairs={{0,16},{16,0},{1,17},{17,1},{2,18},{18,2},{3,19},{19,3},{4,20},{20... | collective-permute-start | bytes 4128776 | tf_op jit(solution)/shard_map/ppermute | solution.py:161
  443.3 38.7 %collective-permute-start.41 = (bf16[2,4,32,4096]{3,2,1,0:T(8,128)(2,1)}, bf16[2,4,32,4096]{3,2,1,0:T(8,128)(2,1)}, u32[]{:S(2)}, u32[]{:S(2)}) collective-permute-start(bf16[2,4,32,4096]{3,2,1,0:T(8,128)(2,1)} %behind.92), channel_id=1, source_target_pairs={{0,2},{1,3},{2,0},{3,1},{4,6},{5,7},{6,4},{7,5},{8,10},{9,11},{10,... | collective-permute-start | bytes 6291464 | tf_op jit(solution)/shard_map/ppermute | solution.py:155
  522.7 51.9 %collective-permute-start.49 = (bf16[4,32,4096]{2,1,0:T(8,128)(2,1)}, bf16[4,32,4096]{2,1,0:T(8,128)(2,1)}, u32[]{:S(2)}, u32[]{:S(2)}) collective-permute-start(bf16[4,32,4096]{2,1,0:T(8,128)(2,1)} %behind.101), channel_id=1, source_target_pairs={{0,1},{1,0},{2,3},{3,2},{4,5},{5,4},{6,7},{7,6},{8,9},{9,8},{10,11... | collective-permute-start | bytes 3145736 | tf_op jit(solution)/shard_map/ppermute | solution.py:155
  524.5 36.0 %collective-permute-start.50 = (bf16[1,2,2,64,224]{4,3,2,1,0:T(8,128)(2,1)S(1)}, bf16[1,2,2,64,224]{4,3,2,1,0:T(8,128)(2,1)S(1)}, u32[]{:S(2)}, u32[]{:S(2)}) collective-permute-start(bf16[1,2,2,64,224]{4,3,2,1,0:T(8,128)(2,1)S(1)} %constant_dynamic-slice_fusion.2), channel_id=1, source_target_pairs={{0,4},{1,5},{2,6},{3,7},{4,8},{5,9},{6,10},{7,11},{8,12},{9,13},{1... | collective-permute-start | bytes 344072 | tf_op jit(solution)/shard_map/ppermute | solution.py:155
  524.6 41.0 %collective-permute-start.48 = (f32[233,128]{1,0:T(8,128)}, f32[233,128]{1,0:T(8,128)S(1)}, u32[]{:S(2)}, u32[]{:S(2)}) collective-permute-start(f32[233,128]{1,0:T(8,128)} %behind.100), channel_id=1, source_target_pairs={{0,16},{16,0},{1,17},{17,1},{2,18},{18,2},{3,19},{19,3},{4,20},{20... | collective-permute-start | bytes 357896 | tf_op jit(solution)/shard_map/ppermute | solution.py:161
  587.2 54.3 %collective-permute-start.54 = (bf16[2,4,32,3072]{3,2,1,0:T(8,128)(2,1)}, bf16[2,4,32,3072]{3,2,1,0:T(8,128)(2,1)}, u32[]{:S(2)}, u32[]{:S(2)}) collective-permute-start(bf16[2,4,32,3072]{3,2,1,0:T(8,128)(2,1)} %behind.104), channel_id=1, source_target_pairs={{0,2},{1,3},{2,0},{3,1},{4,6},{5,7},{6,4},{7,5},{8,10},{9,11},{10,... | collective-permute-start | bytes 4718600 | tf_op jit(solution)/shard_map/ppermute | solution.py:155
  664.2 50.1 %collective-permute-start.67 = (f32[32,2048]{1,0:T(8,128)}, f32[32,2048]{1,0:T(8,128)}, u32[]{:S(2)}, u32[]{:S(2)}) collective-permute-start(f32[32,2048]{1,0:T(8,128)} %convert_add_fusion.13), channel_id=1, source_target_pairs={{0,16},{16,0},{1,17},{17,1},{2,18},{18,2},{3,19},{19,3},{4,20},{20... | collective-permute-start | bytes 786440 | tf_op jit(solution)/shard_map/ppermute | solution.py:161
  (231 other events, 1931.0 us)
Sparse Core Ops, SparseCore 0:
  12.1 127.3 all-gather.5
  142.3 86.1 all-gather.9
  231.4 99.4 all-gather.7
  357.7 61.0 all-gather.11
  421.5 161.0 reduce-scatter.1

commit v3 on v2

--- a/solution.py
+++ b/solution.py
@@ -591,7 +591,7 @@
 
 def sum_rows(ids, rows, count):
     tokens, features = rows.shape
-    unroll, block = 32, 64
+    unroll, block = 32, 384
 
     def kernel(ids_ref, rows_ref, out_ref, squares_ref):
         def clear(at, carry):
@@ -639,7 +639,7 @@
 
 def table_update(table, moment, second, average, grad_rows, factor):
     features, vocabulary = table.shape
-    block = 2048
+    block = 7296
 
     def kernel(factor_ref, table_ref, moment_ref, second_ref, average_ref, grad_ref, *outs):
         grad = grad_ref[...].T * factor_ref[0, 0]
@@ -659,7 +659,7 @@
             + [wide] * 4
             + [pl.BlockSpec((block, features), lambda at: (at, 0))],
             out_specs=[wide] * 4,
-            compiler_params=pltpu.CompilerParams(vmem_limit_bytes=48 * 1024 * 1024),
+            compiler_params=pltpu.CompilerParams(vmem_limit_bytes=56 * 1024 * 1024),
             name="table_update",
         )(factor.reshape(1, 1), table, moment, second, average, grad_rows)
     )
@@ -869,7 +869,6 @@
         1,
     ).astype(jnp.bfloat16)
     pace.close(*map(peek, pair_sum.ring(pace)), peek(up_sum), peek(grad_joined))
-    up_sum = Reduce(links, up_sum, "baz")
     grad_joined = pace.tie(grad_joined)
     back_left = dot_cols(grad_joined, w_in_0[:, : 3 * D])
     back_right = dot_cols(grad_upper, w_in_0[:, 3 * D :])
@@ -878,11 +877,11 @@
     )
     joined_both = jnp.concatenate([grad_joined, links.swap(grad_joined)])
     blocks = grad_embedded.astype(jnp.bfloat16).T.reshape(links.sizes + (features, width))
-    pace.close(*map(peek, up_sum.ring(pace) + pair_sum.step(pace)), peek(joined_both), peek(blocks))
+    pace.close(*map(peek, pair_sum.step(pace)), peek(joined_both), peek(blocks))
     blocks = exchange_along(links, pace.tie(blocks), 2)
     qkv_sum = halves_total(left_both, pace.tie(joined_both))
     pace.close(*map(peek, pair_sum.step(pace)), peek(blocks), peek(qkv_sum))
-    qkv_sum = Reduce(links, qkv_sum, "baz")
+    rest_sum = Reduce(links, jnp.concatenate([qkv_sum, up_sum], 4), "baz")
     blocks = exchange_along(links, pace.tie(blocks), 1)
     back_left, back_right = pace.tie(back_left), pace.tie(back_right)
     sum_state = total_rows(low_state)
@@ -902,7 +901,7 @@
     packed = Total(links, packed.reshape(-1, 128))
     pace.close(*map(peek, pair_sum.step(pace)), peek(blocks), packed.value)
     blocks = exchange_along(links, pace.tie(blocks), 0)
-    pace.close(*map(peek, up_sum.ring(pace)), peek(blocks), *packed.step(pace))
+    pace.close(peek(blocks), *packed.step(pace))
     blocks = pace.tie(blocks)
     spread_mine = blocks.reshape(count, features, width).transpose(0, 2, 1)
     spread_other = links.swap(spread_mine)
@@ -910,12 +909,13 @@
         [jnp.where(mine_first, spread_mine, spread_other), jnp.where(mine_first, spread_other, spread_mine)], 1
     ).reshape(count * micro * width, features)
     table_grad, table_squares = sum_rows(every_ids.reshape(-1), spread.astype(jnp.float32), table.shape[1])
-    pace.close(*map(peek, up_sum.step(pace) + qkv_sum.ring(pace)), peek(table_grad))
-    pace.close(*map(peek, up_sum.step(pace) + qkv_sum.ring(pace)), *packed.step(pace))
-    pace.close(*map(peek, up_sum.ring(pace) + qkv_sum.step(pace)), *packed.step(pace))
-    pace.close(*map(peek, qkv_sum.step(pace)), *packed.step(pace))
-    pace.close(*map(peek, qkv_sum.ring(pace)), *packed.step(pace))
-    up_half, pair_half, qkv_half = up_sum.done(pace), pair_sum.done(pace), qkv_sum.done(pace)
+    pace.close(*map(peek, rest_sum.ring(pace)), peek(table_grad))
+    pace.close(*map(peek, rest_sum.ring(pace)))
+    pace.close(*map(peek, rest_sum.step(pace)), *packed.step(pace))
+    pace.close(*map(peek, rest_sum.step(pace)), *packed.step(pace))
+    pace.close(*map(peek, rest_sum.ring(pace)), *packed.step(pace))
+    in_half, pair_half = rest_sum.done(pace), pair_sum.done(pace)
+
     def factor_part(begin, size):
         return every_factor[:, begin : begin + size]
 
@@ -936,7 +936,6 @@
     shard_fin = lax.dynamic_slice_in_dim(packed, 2 * vec_size + place * final_part, final_part, 0)
     loss_sum = packed[2 * vec_size + 3 * D]
 
-    in_half = jnp.concatenate([qkv_half, up_half], 1)
     in_other, out_other, pair_other = links.swap(in_half), links.swap(out_half), links.swap(pair_half)
     grad_in_0 = jnp.concatenate([in_half, in_other], 0)
     out_half = out_half.astype(jnp.float32)

time: 822 us -> 793 us (0.965)
  starting transfers between devices: 111 us -> 68.9 us
  waiting for transfers between devices: 133 us -> 170 us
  Pallas kernels: 134 us -> 123 us
  local copies, waits for them, and re-layouts: 177 us -> 168 us
    ppermute x23, starting transfers between devices: 44.8 us -> 15.7 us  [swap(): return lax.ppermute(value, 'section', [(0, 1), (1, 0)])]
    ppermute x43 -> x38, waiting for transfers between devices: 111 us -> 133 us  [shift(): return lax.ppermute(value, ('section', 'dp'), pairs)]
    ppermute x43 -> x38, starting transfers between devices: 63.2 us -> 49.2 us  [shift(): return lax.ppermute(value, ('section', 'dp'), pairs)]
    ppermute x8, waiting for transfers between devices: 20 us -> 33.7 us  [flip(): lax.ppermute(value, ('section', 'dp'), self.pairs(kind, lambda place, siz...]
    slice x37 -> x33, local copies, waits for them, and re-layouts: 29.2 us -> 27.2 us  [peek(): lax.slice(value, (0,) * value.ndim, (1,) * (value.ndim - 2) + tuple(ends))]
    unnamed x348 -> x352, local copies, waits for them, and re-layouts: 42.1 us -> 43.4 us
  transfers between devices with their start and end apart: 79 -> 74, of which waited for: 33 -> 36; matrix products, arithmetic and copies ran while one was open for 42% -> 42% of each run, Pallas kernels for 10% -> 10%
where the time goes in v3:
time: 793 us; the launch traced here: 782 us
  waiting for transfers between devices  170 us (21%)
  local copies, waits for them, and re-layouts  168 us (21%)
  matrix products  125 us (16%)
  Pallas kernels  123 us (16%)
  other arithmetic  106 us (13%)
  starting transfers between devices  68.9 us (9%)
  between operations  22.1 us (3%)
    ppermute x38, waiting for transfers between devices, shift(): return lax.ppermute(value, ('section', 'dp'), pairs)  133 us
    dot_general x12, matrix products, matmul(): jnp.dot(left_operand, right_operand, preferred_element_type=jnp.float32)  50.8 us
    ppermute x38, starting transfers between devices, shift(): return lax.ppermute(value, ('section', 'dp'), pairs)  49.2 us
    pallas_call x1, Pallas kernels, table_update(): pl.pallas_call(kernel, grid=(pl.cdiv(vocabulary, block),), out_shape=[jax...  45.2 us
    unnamed x352, local copies, waits for them, and re-layouts  43.4 us
    dot_general x9, matrix products, dot_cols(): lax.dot_general(left_operand, right_operand, (((1,), (1,)), ((), ())), pr...  43.4 us
    pallas_call x1, Pallas kernels, sum_rows(): pl.pallas_call(kernel, out_shape=(jax.ShapeDtypeStruct((count, features),...  37.6 us
    ppermute x8, waiting for transfers between devices, flip(): lax.ppermute(value, ('section', 'dp'), self.pairs(kind, lambda place, siz...  33.7 us
  transfers between devices with their start and end apart: 74, of which 36 were waited for; matrix products, arithmetic and copies ran while one was open for 42% of the time, Pallas kernels for 10%

profile of v3, /device:TPU:0, one launch (start us, length us, event | category | flops | bytes accessed | tf_op | source)
XLA Modules:
  0.0 781.9 jit_solution(10266491405988741050)
XLA Ops:
  30.9 15.6 %low_rows.1 = bf16[50304,64]{1,0:T(8,128)(2,1)} custom-call(f32[64,50304]{1,0:T(8,128)} %table_ref.3, f32[8,128]{1,0:T(8,128)S(1)} %copy-done.25), custom_call_target="tpu_custom_call" | custom-call | tf_op jit(solution)/shard_map/low_rows/pallas_call | solution.py:578
  65.8 12.2 %gather_fusion = bf16[3584,64]{1,0:T(8,128)(2,1)S(1)} fusion(bf16[50304,64]{1,0:T(8,128)(2,1)} %low_rows.1, s32[4096]{0:T(1024)S(1)} %pad_clamp_fusion), kind=kCustom, calls=%fused_computation | custom fusion | bytes 931840 | tf_op jit(solution)/shard_map/jit(_take)/gather | solution.py:733
  85.0 11.1 %collective-permute-done.9 = bf16[4,2,1,64,224]{4,3,2,1,0:T(8,128)(2,1)S(1)} collective-permute-done((bf16[4,2,1,64,224]{4,3,2,1,0:T(8,128)(2,1)S(1)}, bf16[4,2,1,64,224]{4,3,2,1,0:T(8,128)(2,1)S(1)}, u32[]{:S(2)}, u32[]{:S(2)}) %collective-permute-start.9) | collective-permute-done | bytes 229408 | tf_op jit(solution)/shard_map/ppermute | solution.py:155
  98.0 5.4 collective-permute-done.10.refs_1_.refs_0_
  107.2 7.0 collective-permute-start.12
  116.2 14.5 %collective-permute-done.12.refs_1_ = bf16[160,1024]{1,0:T(8,128)(2,1)S(1)} collective-permute-done((bf16[160,1024]{1,0:T(8,128)(2,1)}, bf16[160,1024]{1,0:T(8,128)(2,1)S(1)}, u32[]{:S(2)}, u32[]{:S(2)}) %collective-permute-start.12) | collective-permute-done | bytes 327712 | tf_op jit(solution)/shard_map/ppermute | solution.py:155
  138.2 5.7 collective-permute-done.13
  221.2 13.1 %fusion.43 = (bf16[224,4096]{1,0:T(8,128)(2,1)S(1)}, f32[224,4096]{1,0:T(8,128)}) fusion(f32[4096]{0:T(1024)S(1)} %slice-done.3, bf16[224,1024]{1,0:T(8,128)(2,1)} %behind.71, bf16[1024,7168]{1,0:T(8,128)(2,1)} %all-gather.6.cloned.1.call-done), kind=kOutput, calls=%fused_computation.48 | convolution fusion | flops 1939603456 | bytes 14368768 | tf_op jit(solution)/shard_map/dot_general | solution.py:29
  259.5 5.7 place.2
  265.2 5.6 fusion.108
  273.8 7.7 collective-permute-done.27.refs_2_.refs_0_
  351.1 6.3 convert_reduce_fusion.5
  361.4 6.4 fusion.237
  380.0 8.2 %convert_reduce_fusion = (f32[4096]{0:T(1024)}, bf16[224,4096]{1,0:T(8,128)(2,1)}) fusion(f32[224,4096]{1,0:T(8,128)} %get-tuple-element.211, bf16[224,1024]{1,0:T(8,128)(2,1)} %behind.80, bf16[5120,1024]{1,0:T(8,128)(2,1)} %bitcast.300), kind=kOutput, calls=%fused_computation.60 | convolution fusion | flops 1890054144 | bytes 14368768 | tf_op jit(solution)/shard_map/dot_general | solution.py:39
  396.1 7.4 convolution_convert_fusion
  442.3 5.3 fusion.15.refs_0_
  447.7 8.1 %fusion.236 = (f32[224]{0:T(256)S(1)}, f32[224]{0:T(256)S(1)}, f32[224,1024]{1,0:T(8,128)S(1)}, f32[224,1024]{1,0:T(8,128)}) fusion(f32[224]{0:T(256)S(1)} %copy-done.122, f32[224]{0:T(256)S(1)} %copy-done.116, f32[1024,224]{0,1:T(8,128)S(1)} %copy-done.27, f32[1024]{0:T(1024)S(1)} %copy-done.132, f32[224,1024]{1,0:T(8,128)S(1)} %fusion.15.refs_0_, ...), kind=kOutput, calls=%fused_computation.543 | convolution fusion | flops 1880882688 | bytes 13905408 | tf_op jit(solution)/shard_map/dot_general | solution.py:39
  472.8 8.5 %collective-permute-done.42 = bf16[4,2,1,64,224]{4,3,2,1,0:T(8,128)(2,1)S(1)} collective-permute-done((bf16[4,2,1,64,224]{4,3,2,1,0:T(8,128)(2,1)S(1)}, bf16[4,2,1,64,224]{4,3,2,1,0:T(8,128)(2,1)S(1)}, u32[]{:S(2)}, u32[]{:S(2)}) %collective-permute-start.42) | collective-permute-done | bytes 229408 | tf_op jit(solution)/shard_map/ppermute | solution.py:155
  544.2 37.6 %sum_rows.1 = (f32[50304,64]{1,0:T(8,128)}, f32[1,1]{1,0:T(1,128)}) custom-call(s32[7168]{0:T(1024)} %reshape_reshape.3.ids_ref, f32[7168,64]{1,0:T(8,128)} %bitcast.302), custom_call_target="tpu_custom_call" | custom-call | tf_op jit(solution)/shard_map/sum_rows/pallas_call | solution.py:619
  583.1 9.8 %collective-permute-done.51 = bf16[2,4,32,7168]{3,2,1,0:T(8,128)(2,1)} collective-permute-done((bf16[2,4,32,7168]{3,2,1,0:T(8,128)(2,1)}, bf16[2,4,32,7168]{3,2,1,0:T(8,128)(2,1)}, u32[]{:S(2)}, u32[]{:S(2)}) %collective-permute-start.51) | collective-permute-done | bytes 3670048 | tf_op jit(solution)/shard_map/ppermute | solution.py:155
  601.9 23.4 %collective-permute-done.53 = bf16[4,32,7168]{2,1,0:T(8,128)(2,1)S(1)} collective-permute-done((bf16[4,32,7168]{2,1,0:T(8,128)(2,1)}, bf16[4,32,7168]{2,1,0:T(8,128)(2,1)S(1)}, u32[]{:S(2)}, u32[]{:S(2)}) %collective-permute-start.53) | collective-permute-done | bytes 1835040 | tf_op jit(solution)/shard_map/ppermute | solution.py:155
  641.4 6.2 collective-permute-start.62
  660.8 11.1 %collective-permute-done.58 = f32[233,128]{1,0:T(8,128)S(1)} collective-permute-done((f32[233,128]{1,0:T(8,128)}, f32[233,128]{1,0:T(8,128)S(1)}, u32[]{:S(2)}, u32[]{:S(2)}) %collective-permute-start.58) | collective-permute-done | bytes 119328 | tf_op jit(solution)/shard_map/ppermute | solution.py:158
  719.0 45.2 %table_update.1 = (f32[64,50304]{1,0:T(8,128)}, f32[64,50304]{1,0:T(8,128)}, f32[64,50304]{1,0:T(8,128)}, f32[64,50304]{1,0:T(8,128)}) custom-call(f32[1,1]{1,0:T(1,128)} %bitcast.120.factor_ref, f32[64,50304]{1,0:T(8,128)} %table_ref.3, f32[64,50304]{1,0:T(8,128)} %moment_ref.1, f32[64,50304]{1,0:T(8,128)} %second_ref.1, f32[64,50304]{1,0:T(8,128)} %average_ref.1, ...), custom_call_target="tpu_custom_call" | custom-call | tf_op jit(solution)/shard_map/table_update/pallas_call | solution.py:654
  (917 shorter events, 472.9 us)
Async XLA Ops:
  7.2 176.2 %all-gather.6.cloned.1.call-start = ((), (), s32[]{:S(2)}) async-start(), calls=%async_computation.1 | async-start | bytes 15138816 | tf_op jit(solution)/shard_map/all_gather | solution.py:714
  11.9 316.0 %all-gather.10.cloned.1.call-start = ((), (), s32[]{:S(2)}) async-start(), calls=%async_computation.3 | async-start | bytes 8650752 | tf_op jit(solution)/shard_map/all_gather | solution.py:715
  12.7 320.3 %all-gather.8.cloned.1.call-start = ((), (), s32[]{:S(2)}) async-start(), calls=%async_computation.2 | async-start | bytes 10813440 | tf_op jit(solution)/shard_map/all_gather | solution.py:716
  25.2 622.4 %all-gather.12.cloned.1.call-start = ((), (), s32[]{:S(2)}) async-start(), calls=%async_computation.5 | async-start | bytes 3514368 | tf_op jit(solution)/shard_map/all_gather | solution.py:846
  29.5 18.3 %collective-permute-start.4 = (f32[1472]{0:T(1024)}, f32[1472]{0:T(1024)S(1)}, u32[]{:S(2)}, u32[]{:S(2)}) collective-permute-start(f32[1472]{0:T(1024)} %behind.54), channel_id=1, source_target_pairs={{0,4},{1,5},{2,6},{3,7},{4,8},{5,9},{6,10},{7,11},{8,12},{9,13},{1... | collective-permute-start | bytes 17672 | tf_op jit(solution)/shard_map/ppermute | solution.py:155
  84.0 19.4 %collective-permute-start.10 = (bf16[160,1024]{1,0:T(8,128)(2,1)}, bf16[160,1024]{1,0:T(8,128)(2,1)S(1)}, u32[]{:S(2)}, u32[]{:S(2)}) collective-permute-start(bf16[160,1024]{1,0:T(8,128)(2,1)} %behind.61), channel_id=1, source_target_pairs={{0,4},{1,5},{2,6},{3,7},{4,8},{5,9},{6,10},{7,11},{8,12},{9,13},{1... | collective-permute-start | bytes 983048 | tf_op jit(solution)/shard_map/ppermute | solution.py:155
  107.2 23.5 %collective-permute-start.12 = (bf16[160,1024]{1,0:T(8,128)(2,1)}, bf16[160,1024]{1,0:T(8,128)(2,1)S(1)}, u32[]{:S(2)}, u32[]{:S(2)}) collective-permute-start(bf16[160,1024]{1,0:T(8,128)(2,1)} %behind.63), channel_id=1, source_target_pairs={{0,4},{1,5},{2,6},{3,7},{4,8},{5,9},{6,10},{7,11},{8,12},{9,13},{1... | collective-permute-start | bytes 983048 | tf_op jit(solution)/shard_map/ppermute | solution.py:155
  162.6 54.8 %collective-permute-start.17 = (bf16[4,160,1024]{2,1,0:T(8,128)(2,1)}, bf16[4,160,1024]{2,1,0:T(8,128)(2,1)}, u32[]{:S(2)}, u32[]{:S(2)}) collective-permute-start(bf16[4,160,1024]{2,1,0:T(8,128)(2,1)} %behind.66.refs_0_), channel_id=1, source_target_pairs={{0,16},{16,0},{1,17},{17,1},{2,18},{18,2},{3,19},{19,3},{4,20},{20... | collective-permute-start | bytes 3932168 | tf_op jit(solution)/shard_map/ppermute | solution.py:161
  162.6 54.8 %collective-permute-start.18 = (bf16[4,160,1024]{2,1,0:T(8,128)(2,1)}, bf16[4,160,1024]{2,1,0:T(8,128)(2,1)S(1)}, u32[]{:S(2)}, u32[]{:S(2)}) collective-permute-start(bf16[4,160,1024]{2,1,0:T(8,128)(2,1)} %behind.66.refs_0_), channel_id=1, source_target_pairs={{0,2},{1,3},{2,0},{3,1},{4,6},{5,7},{6,4},{7,5},{8,10},{9,11},{10,... | collective-permute-start | bytes 3932168 | tf_op jit(solution)/shard_map/ppermute | solution.py:155
  163.1 54.3 %collective-permute-start.19 = (bf16[4,160,1024]{2,1,0:T(8,128)(2,1)}, bf16[4,160,1024]{2,1,0:T(8,128)(2,1)S(1)}, u32[]{:S(2)}, u32[]{:S(2)}) collective-permute-start(bf16[4,160,1024]{2,1,0:T(8,128)(2,1)} %behind.66.refs_0_), channel_id=1, source_target_pairs={{0,1},{1,0},{2,3},{3,2},{4,5},{5,4},{6,7},{7,6},{8,9},{9,8},{10,11... | collective-permute-start | bytes 3932168 | tf_op jit(solution)/shard_map/ppermute | solution.py:155
  220.1 17.8 %collective-permute-start.23 = (bf16[4,160,1024]{2,1,0:T(8,128)(2,1)}, bf16[4,160,1024]{2,1,0:T(8,128)(2,1)S(1)}, u32[]{:S(2)}, u32[]{:S(2)}) collective-permute-start(bf16[4,160,1024]{2,1,0:T(8,128)(2,1)} %behind.69.refs_4_), channel_id=1, source_target_pairs={{0,2},{1,3},{2,0},{3,1},{4,6},{5,7},{6,4},{7,5},{8,10},{9,11},{10,... | collective-permute-start | bytes 3932168 | tf_op jit(solution)/shard_map/ppermute | solution.py:155
  220.2 17.7 %collective-permute-start.22 = (bf16[4,160,1024]{2,1,0:T(8,128)(2,1)}, bf16[4,160,1024]{2,1,0:T(8,128)(2,1)S(1)}, u32[]{:S(2)}, u32[]{:S(2)}) collective-permute-start(bf16[4,160,1024]{2,1,0:T(8,128)(2,1)} %behind.69.refs_4_), channel_id=1, source_target_pairs={{0,16},{16,0},{1,17},{17,1},{2,18},{18,2},{3,19},{19,3},{4,20},{20... | collective-permute-start | bytes 3932168 | tf_op jit(solution)/shard_map/ppermute | solution.py:161
  253.1 28.3 %collective-permute-start.27 = (bf16[4,32,3072]{2,1,0:T(8,128)(2,1)}, bf16[4,32,3072]{2,1,0:T(8,128)(2,1)}, u32[]{:S(2)}, u32[]{:S(2)}) collective-permute-start(bf16[4,32,3072]{2,1,0:T(8,128)(2,1)} %behind.75.refs_0_), channel_id=1, source_target_pairs={{0,1},{1,0},{2,3},{3,2},{4,5},{5,4},{6,7},{7,6},{8,9},{9,8},{10,11... | collective-permute-start | bytes 2359304 | tf_op jit(solution)/shard_map/ppermute | solution.py:155
  255.5 26.0 %collective-permute-start.28 = (bf16[4,32,3072]{2,1,0:T(8,128)(2,1)}, bf16[4,32,3072]{2,1,0:T(8,128)(2,1)}, u32[]{:S(2)}, u32[]{:S(2)}) collective-permute-start(bf16[4,32,3072]{2,1,0:T(8,128)(2,1)} %behind.75.refs_0_), channel_id=1, source_target_pairs={{0,16},{16,0},{1,17},{17,1},{2,18},{18,2},{3,19},{19,3},{4,20},{20... | collective-permute-start | bytes 2359304 | tf_op jit(solution)/shard_map/ppermute | solution.py:161
  255.5 26.0 %collective-permute-start.29 = (bf16[4,32,3072]{2,1,0:T(8,128)(2,1)}, bf16[4,32,3072]{2,1,0:T(8,128)(2,1)S(1)}, u32[]{:S(2)}, u32[]{:S(2)}) collective-permute-start(bf16[4,32,3072]{2,1,0:T(8,128)(2,1)} %behind.75.refs_0_), channel_id=1, source_target_pairs={{0,2},{1,3},{2,0},{3,1},{4,6},{5,7},{6,4},{7,5},{8,10},{9,11},{10,... | collective-permute-start | bytes 2359304 | tf_op jit(solution)/shard_map/ppermute | solution.py:155
  350.8 25.3 %collective-permute-start.35 = (bf16[224,2048]{1,0:T(8,128)(2,1)S(1)}, bf16[224,2048]{1,0:T(8,128)(2,1)}, u32[]{:S(2)}, u32[]{:S(2)}) collective-permute-start(bf16[224,2048]{1,0:T(8,128)(2,1)S(1)} %pad_maximum_fusion.4), channel_id=1, source_target_pairs={{0,16},{16,0},{1,17},{17,1},{2,18},{18,2},{3,19},{19,3},{4,20},{20... | collective-permute-start | bytes 2752520 | tf_op jit(solution)/shard_map/ppermute | solution.py:161
  358.0 325.2 %reduce-scatter.2.cloned.1.call-start = ((), (), s32[]{:S(2)}) async-start(), calls=%async_computation.4 | async-start | bytes 10813440 | tf_op jit(solution)/shard_map/reduce_scatter | solution.py:856
  380.0 23.6 %collective-permute-start.36 = (bf16[2,4,32,2048]{3,2,1,0:T(8,128)(2,1)}, bf16[2,4,32,2048]{3,2,1,0:T(8,128)(2,1)}, u32[]{:S(2)}, u32[]{:S(2)}) collective-permute-start(bf16[2,4,32,2048]{3,2,1,0:T(8,128)(2,1)} %behind.81), channel_id=1, source_target_pairs={{0,2},{1,3},{2,0},{3,1},{4,6},{5,7},{6,4},{7,5},{8,10},{9,11},{10,... | collective-permute-start | bytes 3145736 | tf_op jit(solution)/shard_map/ppermute | solution.py:155
  391.8 36.9 %collective-permute-start.39 = (bf16[224,4096]{1,0:T(8,128)(2,1)}, bf16[224,4096]{1,0:T(8,128)(2,1)}, u32[]{:S(2)}, u32[]{:S(2)}) collective-permute-start(bf16[224,4096]{1,0:T(8,128)(2,1)} %get-tuple-element.220), channel_id=1, source_target_pairs={{0,16},{16,0},{1,17},{17,1},{2,18},{18,2},{3,19},{19,3},{4,20},{20... | collective-permute-start | bytes 5505032 | tf_op jit(solution)/shard_map/ppermute | solution.py:161
  441.7 17.7 %collective-permute-start.40 = (bf16[32,2048]{1,0:T(8,128)(2,1)}, bf16[32,2048]{1,0:T(8,128)(2,1)}, u32[]{:S(2)}, u32[]{:S(2)}) collective-permute-start(bf16[32,2048]{1,0:T(8,128)(2,1)} %behind.86), channel_id=1, source_target_pairs={{0,4},{1,5},{2,6},{3,7},{4,8},{5,9},{6,10},{7,11},{8,12},{9,13},{1... | collective-permute-start | bytes 393224 | tf_op jit(solution)/shard_map/ppermute | solution.py:155
  442.2 41.1 %collective-permute-start.44 = (bf16[224,3072]{1,0:T(8,128)(2,1)}, bf16[224,3072]{1,0:T(8,128)(2,1)}, u32[]{:S(2)}, u32[]{:S(2)}) collective-permute-start(bf16[224,3072]{1,0:T(8,128)(2,1)} %behind.85), channel_id=1, source_target_pairs={{0,16},{16,0},{1,17},{17,1},{2,18},{18,2},{3,19},{19,3},{4,20},{20... | collective-permute-start | bytes 4128776 | tf_op jit(solution)/shard_map/ppermute | solution.py:161
  535.7 57.2 %collective-permute-start.51 = (bf16[2,4,32,7168]{3,2,1,0:T(8,128)(2,1)}, bf16[2,4,32,7168]{3,2,1,0:T(8,128)(2,1)}, u32[]{:S(2)}, u32[]{:S(2)}) collective-permute-start(bf16[2,4,32,7168]{3,2,1,0:T(8,128)(2,1)} %behind.96), channel_id=1, source_target_pairs={{0,2},{1,3},{2,0},{3,1},{4,6},{5,7},{6,4},{7,5},{8,10},{9,11},{10,... | collective-permute-start | bytes 11010056 | tf_op jit(solution)/shard_map/ppermute | solution.py:155
  601.9 23.4 %collective-permute-start.53 = (bf16[4,32,7168]{2,1,0:T(8,128)(2,1)}, bf16[4,32,7168]{2,1,0:T(8,128)(2,1)S(1)}, u32[]{:S(2)}, u32[]{:S(2)}) collective-permute-start(bf16[4,32,7168]{2,1,0:T(8,128)(2,1)} %behind.98), channel_id=1, source_target_pairs={{0,1},{1,0},{2,3},{3,2},{4,5},{5,4},{6,7},{7,6},{8,9},{9,8},{10,11... | collective-permute-start | bytes 5505032 | tf_op jit(solution)/shard_map/ppermute | solution.py:155
  641.4 50.9 %collective-permute-start.62 = (f32[32,2048]{1,0:T(8,128)}, f32[32,2048]{1,0:T(8,128)}, u32[]{:S(2)}, u32[]{:S(2)}) collective-permute-start(f32[32,2048]{1,0:T(8,128)} %convert_add_fusion.8), channel_id=1, source_target_pairs={{0,16},{16,0},{1,17},{17,1},{2,18},{18,2},{3,19},{19,3},{4,20},{20... | collective-permute-start | bytes 786440 | tf_op jit(solution)/shard_map/ppermute | solution.py:161
  (228 other events, 1974.9 us)
Sparse Core Ops, SparseCore 0:
  12.1 127.4 all-gather.5
  142.4 86.8 all-gather.9
  232.1 98.9 all-gather.7
  358.2 60.5 all-gather.11
  421.5 155.8 reduce-scatter.1

commit v4 on v3

--- a/solution.py
+++ b/solution.py
@@ -512,6 +512,101 @@
     top_score = jnp.max(scores, -1, keepdims=True)
     powers = jnp.exp(scores - top_score)
     return powers / jnp.sum(powers, -1, keepdims=True)
+
+
+def spin_tables(cosine, sine):
+    rows, _, half = cosine.shape
+    cosine, sine = cosine[:, 0], sine[:, 0]
+    rest = HEAD_DIM - 2 * half
+    none = jnp.zeros((rows, half), jnp.float32)
+    own = jnp.concatenate([cosine, cosine, jnp.ones((rows, rest), jnp.float32)], 1)
+    above = jnp.concatenate([-sine, none, jnp.zeros((rows, rest), jnp.float32)], 1)
+    below = jnp.concatenate([none, sine, jnp.zeros((rows, rest), jnp.float32)], 1)
+    return tuple(jnp.concatenate([part, part], 1) for part in (own, above, below))
+
+
+def spin(value, own, above, below, sign):
+    half, lanes = ROT // 2, 2 * HEAD_DIM
+    turned = pltpu.roll(value, lanes - half, 1) * above + pltpu.roll(value, half, 1) * below
+    return value * own + sign * turned
+
+
+def head_weights(query, keys, seen):
+    scores = jnp.where(seen, dot_cols(query, keys) * HEAD_DIM ** (-0.5), MASKED)
+    powers = jnp.exp(scores - jnp.max(scores, -1, keepdims=True))
+    return powers / jnp.sum(powers, -1, keepdims=True)
+
+
+def attend(joined, tables, allowed):
+    rows, lanes = joined.shape[0], 2 * HEAD_DIM
+
+    def kernel(joined_ref, own_ref, above_ref, below_ref, seen_ref, query_ref, keys_ref, values_ref, mixed_ref):
+        own, above, below = own_ref[...], above_ref[...], below_ref[...]
+        seen = seen_ref[...] > 0.5
+        lower = lax.broadcasted_iota(jnp.int32, (rows, lanes), 1) < HEAD_DIM
+        for pair in range(D // lanes):
+            at = slice(pair * lanes, (pair + 1) * lanes)
+            query = spin(joined_ref[:, pair * lanes : (pair + 1) * lanes], own, above, below, 1.0)
+            keys = spin(joined_ref[:, D + pair * lanes : D + (pair + 1) * lanes], own, above, below, 1.0)
+            keys = keys.astype(jnp.bfloat16)
+            values = joined_ref[:, 2 * D + pair * lanes : 2 * D + (pair + 1) * lanes].astype(jnp.bfloat16)
+            query_ref[:, at], keys_ref[:, at], values_ref[:, at] = query.astype(jnp.bfloat16), keys, values
+            parts = []
+            for head in range(2):
+                mine = lower if head == 0 else jnp.logical_not(lower)
+                weights = head_weights(jnp.where(mine, query, 0.0).astype(jnp.bfloat16), keys, seen)
+                parts.append(matmul(weights.astype(jnp.bfloat16), values))
+            mixed_ref[:, at] = jnp.where(lower, parts[0], parts[1]).astype(jnp.bfloat16)
+
+    return pl.pallas_call(
+        kernel,
+        out_shape=[jax.ShapeDtypeStruct((rows, D), jnp.bfloat16)] * 4,
+        compiler_params=pltpu.CompilerParams(vmem_limit_bytes=40 * 1024 * 1024),
+        name="attend",
+    )(joined, *tables, allowed)
+
+
+def attend_back(query, keys, values, grad_mixed, tables, allowed):
+    rows, lanes = query.shape[0], 2 * HEAD_DIM
+
+    def kernel(
+        query_ref, keys_ref, values_ref, grad_ref, own_ref, above_ref, below_ref, seen_ref, joined_ref
+    ):
+        own, above, below = own_ref[...], above_ref[...], below_ref[...]
+        seen = seen_ref[...] > 0.5
+        lower = lax.broadcasted_iota(jnp.int32, (rows, lanes), 1) < HEAD_DIM
+        factor = HEAD_DIM ** (-0.5)
+        for pair in range(D // lanes):
+            at = slice(pair * lanes, (pair + 1) * lanes)
+            query, keys, values, grad = query_ref[:, at], keys_ref[:, at], values_ref[:, at], grad_ref[:, at]
+            wide_query, wide_grad = query.astype(jnp.float32), grad.astype(jnp.float32)
+            parts = []
+            for head in range(2):
+                mine = lower if head == 0 else jnp.logical_not(lower)
+                weights = head_weights(jnp.where(mine, wide_query, 0.0).astype(jnp.bfloat16), keys, seen)
+                pulled = dot_cols(jnp.where(mine, wide_grad, 0.0).astype(jnp.bfloat16), values)
+                pulled = weights * (pulled - jnp.sum(weights * pulled, -1, keepdims=True))
+                pulled = pulled.astype(jnp.bfloat16)
+                parts.append(
+                    (
+                        matmul(pulled, keys) * factor,
+                        dot_rows(pulled, query) * factor,
+                        dot_rows(weights.astype(jnp.bfloat16), grad),
+                    )
+                )
+            grads = [jnp.where(lower, first, second) for first, second in zip(*parts)]
+            for third in range(2):
+                grads[third] = spin(grads[third], own, above, below, -1.0)
+            for third in range(3):
+                start = third * D + pair * lanes
+                joined_ref[:, start : start + lanes] = grads[third].astype(jnp.bfloat16)
+
+    return pl.pallas_call(
+        kernel,
+        out_shape=jax.ShapeDtypeStruct((rows, 3 * D), jnp.bfloat16),
+        compiler_params=pltpu.CompilerParams(vmem_limit_bytes=40 * 1024 * 1024),
+        name="attend_back",
+    )(query, keys, values, grad_mixed, *tables, allowed)
 
 
 def attention_backward(query, keys, values, weights, grad_mixed):
@@ -751,15 +846,8 @@
     left = (normal * first_gain + first_bias).astype(jnp.bfloat16)
     right = (normal * second_gain + second_bias).astype(jnp.bfloat16)
     joined = matmul(pace.tie(left), w_in_0[:, : 3 * D]) + bias_qkv
-    query = turn(joined[:, :D].reshape(width, HEADS, HEAD_DIM), cosine, sine, 1.0).astype(jnp.bfloat16)
-    keys = turn(joined[:, D : 2 * D].reshape(width, HEADS, HEAD_DIM), cosine, sine, 1.0).astype(jnp.bfloat16)
-    values = joined[:, 2 * D :].reshape(width, HEADS, HEAD_DIM).astype(jnp.bfloat16)
-    weights = softmax_parts(scores_of(query, keys, allowed))
-    mixed = (
-        jnp.einsum("hqk,khe->qhe", weights.astype(jnp.bfloat16), values, preferred_element_type=jnp.float32)
-        .reshape(width, D)
-        .astype(jnp.bfloat16)
-    )
+    tables, seen = spin_tables(cosine, sine), allowed.astype(jnp.float32)
+    query, keys, values, mixed = attend(joined, tables, seen)
     pace.close(*out_0.wave(pace), *qkv_1.along(pace, 1), peek(mixed))
     upper = matmul(pace.tie(right), w_in_0[:, 3 * D :]) + bias_up
     active = jax.nn.gelu(upper, approximate=False).astype(jnp.bfloat16)
@@ -773,7 +861,7 @@
         state + matmul(mixed, w_out_0[:D]) + bias_attn + (matmul(pace.tie(active), w_out_0[D:]) + bias_down)
     )
     state_1 = lax.reduce_precision(state_1, 8, 7)
-    kept = (normal, scale, left, right, upper, query, keys, values, weights, acts)
+    kept = (normal, scale, left, right, upper, query, keys, values, acts)
     pace.close(*qkv_1.wave(pace), peek(state_1))
     pace.close(*qkv_1.wave(pace))
     pace.close(*qkv_1.last(pace))
@@ -846,7 +934,7 @@
     every_factor = lax.all_gather(factors, ("dp", "section"), axis=0, tiled=True)
     in_rows, out_rows = in_w.shape[1], out_w.shape[1]
 
-    normal, scale, left, right, upper, query, keys, values, weights, acts = kept
+    normal, scale, left, right, upper, query, keys, values, acts = kept
     first_gain, first_bias, second_gain, second_bias = pieces(vector_0)[:4]
     low_state = grad_state
     pair_sum = Reduce(links, halves_total(pairs_both, pairs_grad), "baz")
@@ -854,20 +942,12 @@
     low_state = pace.tie(low_state)
     out_half = dot_rows(acts, low_state).astype(jnp.bfloat16)
     out_half = lax.psum_scatter(out_half, ("dp", "section"), scatter_dimension=0, tiled=True)
-    grad_mixed = dot_cols(low_state, w_out_0[:D]).astype(jnp.bfloat16).reshape(width, HEADS, HEAD_DIM)
+    grad_mixed = dot_cols(low_state, w_out_0[:D]).astype(jnp.bfloat16)
     grad_upper = (dot_cols(low_state, w_out_0[D:]) * gelu_slope(upper)).astype(jnp.bfloat16)
     upper_both = jnp.concatenate([grad_upper, links.swap(grad_upper)])
     pace.close(*map(peek, pair_sum.ring(pace)), peek(grad_mixed), peek(upper_both))
     up_sum = halves_total(right_both, pace.tie(upper_both))
-    grad_query, grad_keys, grad_values = attention_backward(query, keys, values, weights, pace.tie(grad_mixed))
-    grad_joined = jnp.concatenate(
-        [
-            turn(grad_query, cosine, sine, -1.0).reshape(width, D),
-            turn(grad_keys, cosine, sine, -1.0).reshape(width, D),
-            grad_values.reshape(width, D),
-        ],
-        1,
-    ).astype(jnp.bfloat16)
+    grad_joined = attend_back(query, keys, values, pace.tie(grad_mixed), tables, seen)
     pace.close(*map(peek, pair_sum.ring(pace)), peek(up_sum), peek(grad_joined))
     grad_joined = pace.tie(grad_joined)
     back_left = dot_cols(grad_joined, w_in_0[:, : 3 * D])
@@ -901,6 +981,7 @@
     packed = Total(links, packed.reshape(-1, 128))
     pace.close(*map(peek, pair_sum.step(pace)), peek(blocks), packed.value)
     blocks = exchange_along(links, pace.tie(blocks), 0)
+    first = rest_sum.ring(pace)
     pace.close(peek(blocks), *packed.step(pace))
     blocks = pace.tie(blocks)
     spread_mine = blocks.reshape(count, features, width).transpose(0, 2, 1)
@@ -909,8 +990,8 @@
         [jnp.where(mine_first, spread_mine, spread_other), jnp.where(mine_first, spread_other, spread_mine)], 1
     ).reshape(count * micro * width, features)
     table_grad, table_squares = sum_rows(every_ids.reshape(-1), spread.astype(jnp.float32), table.shape[1])
-    pace.close(*map(peek, rest_sum.ring(pace)), peek(table_grad))
-    pace.close(*map(peek, rest_sum.ring(pace)))
+    pace.close(*map(peek, first), peek(table_grad), *packed.step(pace))
+    pace.close(*map(peek, rest_sum.ring(pace)), *packed.step(pace))
     pace.close(*map(peek, rest_sum.step(pace)), *packed.step(pace))
     pace.close(*map(peek, rest_sum.step(pace)), *packed.step(pace))
     pace.close(*map(peek, rest_sum.ring(pace)), *packed.step(pace))

time: 793 us -> 835 us (1.053)
  starting transfers between devices: 68.9 us -> 126 us
  local copies, waits for them, and re-layouts: 168 us -> 151 us
  Pallas kernels: 123 us -> 136 us
  matrix products: 125 us -> 113 us
    ppermute x23, starting transfers between devices: 15.7 us -> 62.3 us  [swap(): return lax.ppermute(value, 'section', [(0, 1), (1, 0)])]
    pallas_call x0 -> x2, Pallas kernels: none -> 14 us  [the longest x1 9.21 us: attend_back(): pl.pallas_call(kernel, out_shape=jax.ShapeDtypeStruct((rows, 3 * D), jnp....]
    slice x5 -> x0, local copies, waits for them, and re-layouts: 10.7 us -> none  [the longest x2 5.38 us: body(): joined[:, D:2 * D].reshape(width, HEADS, HEAD_DIM)]
    ppermute x8, waiting for transfers between devices: 33.7 us -> 42.9 us  [flip(): lax.ppermute(value, ('section', 'dp'), self.pairs(kind, lambda place, siz...]
    ppermute x38, starting transfers between devices: 49.2 us -> 57.6 us  [shift(): return lax.ppermute(value, ('section', 'dp'), pairs)]
    unnamed x352 -> x372, local copies, waits for them, and re-layouts: 43.4 us -> 44.9 us
    slice x33 -> x32, local copies, waits for them, and re-layouts: 27.2 us -> 26 us  [peek(): lax.slice(value, (0,) * value.ndim, (1,) * (value.ndim - 2) + tuple(ends))]
  transfers between devices with their start and end apart: 74 -> 74, of which waited for: 36 -> 36; matrix products, arithmetic and copies ran while one was open for 42% -> 35% of each run, Pallas kernels for 10% -> 11%
where the time goes in v4:
time: 835 us; the launch traced here: 825 us
  waiting for transfers between devices  177 us (21%)
  local copies, waits for them, and re-layouts  151 us (18%)
  Pallas kernels  136 us (16%)
  starting transfers between devices  126 us (15%)
  matrix products  113 us (14%)
  other arithmetic  99.6 us (12%)
  between operations  22.1 us (3%)
    ppermute x38, waiting for transfers between devices, shift(): return lax.ppermute(value, ('section', 'dp'), pairs)  128 us
    ppermute x23, starting transfers between devices, swap(): return lax.ppermute(value, 'section', [(0, 1), (1, 0)])  62.3 us
    ppermute x38, starting transfers between devices, shift(): return lax.ppermute(value, ('section', 'dp'), pairs)  57.6 us
    dot_general x12, matrix products, matmul(): jnp.dot(left_operand, right_operand, preferred_element_type=jnp.float32)  50.6 us
    dot_general x9, matrix products, dot_cols(): lax.dot_general(left_operand, right_operand, (((1,), (1,)), ((), ())), pr...  46.1 us
    pallas_call x1, Pallas kernels, table_update(): pl.pallas_call(kernel, grid=(pl.cdiv(vocabulary, block),), out_shape=[jax...  45.2 us
    unnamed x372, local copies, waits for them, and re-layouts  44.9 us
    ppermute x8, waiting for transfers between devices, flip(): lax.ppermute(value, ('section', 'dp'), self.pairs(kind, lambda place, siz...  42.9 us
  transfers between devices with their start and end apart: 74, of which 36 were waited for; matrix products, arithmetic and copies ran while one was open for 35% of the time, Pallas kernels for 11%

profile of v4, /device:TPU:0, one launch (start us, length us, event | category | flops | bytes accessed | tf_op | source)
XLA Modules:
  0.0 824.9 jit_solution(8121188953504592283)
XLA Ops:
  34.0 15.6 %low_rows.1 = bf16[50304,64]{1,0:T(8,128)(2,1)} custom-call(f32[64,50304]{1,0:T(8,128)} %table_ref.3, f32[8,128]{1,0:T(8,128)S(1)} %copy-done.44), custom_call_target="tpu_custom_call" | custom-call | tf_op jit(solution)/shard_map/low_rows/pallas_call | solution.py:673
  69.2 12.2 %gather_fusion = bf16[3584,64]{1,0:T(8,128)(2,1)S(1)} fusion(bf16[50304,64]{1,0:T(8,128)(2,1)} %low_rows.1, s32[4096]{0:T(1024)S(1)} %pad_clamp_fusion), kind=kCustom, calls=%fused_computation | custom fusion | bytes 931840 | tf_op jit(solution)/shard_map/jit(_take)/gather | solution.py:828
  88.7 10.6 %collective-permute-done.9 = bf16[4,2,1,64,224]{4,3,2,1,0:T(8,128)(2,1)S(1)} collective-permute-done((bf16[4,2,1,64,224]{4,3,2,1,0:T(8,128)(2,1)S(1)}, bf16[4,2,1,64,224]{4,3,2,1,0:T(8,128)(2,1)S(1)}, u32[]{:S(2)}, u32[]{:S(2)}) %collective-permute-start.9) | collective-permute-done | bytes 229408 | tf_op jit(solution)/shard_map/ppermute | solution.py:155
  118.5 15.7 %collective-permute-done.12.refs_1_ = bf16[160,1024]{1,0:T(8,128)(2,1)S(1)} collective-permute-done((bf16[160,1024]{1,0:T(8,128)(2,1)}, bf16[160,1024]{1,0:T(8,128)(2,1)S(1)}, u32[]{:S(2)}, u32[]{:S(2)}) %collective-permute-start.12) | collective-permute-done | bytes 327712 | tf_op jit(solution)/shard_map/ppermute | solution.py:155
  146.6 7.4 collective-permute-done.14
  195.2 6.5 collective-permute-done.19.refs_2_.refs_0_
  208.9 13.0 %fusion.42 = (bf16[224,4096]{1,0:T(8,128)(2,1)S(1)}, f32[224,4096]{1,0:T(8,128)}) fusion(f32[4096]{0:T(1024)S(1)} %slice-done.1, bf16[224,1024]{1,0:T(8,128)(2,1)} %behind.71, bf16[1024,7168]{1,0:T(8,128)(2,1)} %all-gather.6.cloned.1.call-done), kind=kOutput, calls=%fused_computation.47 | convolution fusion | flops 1939603456 | bytes 14368768 | tf_op jit(solution)/shard_map/dot_general | solution.py:29
  351.2 6.3 convert_reduce_fusion.5
  358.9 6.3 fusion.227
  380.7 8.2 convert_reduce_fusion
  399.5 7.6 convolution_convert_fusion
  409.7 9.2 %attend_back.1.refs_0_ = bf16[224,3072]{1,0:T(8,128)(2,1)S(1)} custom-call(bf16[224,1024]{1,0:T(8,128)(2,1)S(1)} %copy-done.39, bf16[224,1024]{1,0:T(8,128)(2,1)S(1)} %copy-done.41, bf16[224,1024]{1,0:T(8,128)(2,1)S(1)} %copy-done.43, bf16[224,1024]{1,0:T(8,128)(2,1)S(1)} %copy-done.30, f32[224,128]{1,0:T(8,128)S(1)} %copy-done.34, ...), custom_call_target="tpu_custom_call" | custom-call | tf_op jit(solution)/shard_map/attend_back/pallas_call | solution.py:604
  442.4 8.1 fusion.226
  459.1 6.5 collective-permute-done.41
  466.3 7.4 collective-permute-done.42
  507.5 6.2 collective-permute-done.48
  528.8 8.1 collective-permute-done.51
  544.9 37.6 %sum_rows.1 = (f32[50304,64]{1,0:T(8,128)}, f32[1,1]{1,0:T(1,128)}) custom-call(s32[7168]{0:T(1024)} %reshape_reshape.3.ids_ref, f32[7168,64]{1,0:T(8,128)} %bitcast.277), custom_call_target="tpu_custom_call" | custom-call | tf_op jit(solution)/shard_map/sum_rows/pallas_call | solution.py:714
  600.7 15.6 %collective-permute-done.55 = bf16[4,32,7168]{2,1,0:T(8,128)(2,1)} collective-permute-done((bf16[4,32,7168]{2,1,0:T(8,128)(2,1)}, bf16[4,32,7168]{2,1,0:T(8,128)(2,1)}, u32[]{:S(2)}, u32[]{:S(2)}) %collective-permute-start.55) | collective-permute-done | bytes 1835040 | tf_op jit(solution)/shard_map/ppermute | solution.py:155
  626.2 10.0 %collective-permute-done.56 = f32[233,128]{1,0:T(8,128)S(1)} collective-permute-done((f32[233,128]{1,0:T(8,128)}, f32[233,128]{1,0:T(8,128)S(1)}, u32[]{:S(2)}, u32[]{:S(2)}) %collective-permute-start.56) | collective-permute-done | bytes 119328 | tf_op jit(solution)/shard_map/ppermute | solution.py:158
  642.1 9.5 %collective-permute-done.58 = f32[233,128]{1,0:T(8,128)S(1)} collective-permute-done((f32[233,128]{1,0:T(8,128)}, f32[233,128]{1,0:T(8,128)S(1)}, u32[]{:S(2)}, u32[]{:S(2)}) %collective-permute-start.58) | collective-permute-done | bytes 119328 | tf_op jit(solution)/shard_map/ppermute | solution.py:158
  654.7 10.3 %collective-permute-done.60 = bf16[32,7168]{1,0:T(8,128)(2,1)S(1)} collective-permute-done((bf16[32,7168]{1,0:T(8,128)(2,1)}, bf16[32,7168]{1,0:T(8,128)(2,1)S(1)}, u32[]{:S(2)}, u32[]{:S(2)}) %collective-permute-start.60) | collective-permute-done | bytes 458784 | tf_op jit(solution)/shard_map/ppermute | solution.py:155
  666.3 53.1 %collective-permute-start.61 = (f32[32,7168]{1,0:T(8,128)}, f32[32,7168]{1,0:T(8,128)}, u32[]{:S(2)}, u32[]{:S(2)}) collective-permute-start(f32[32,7168]{1,0:T(8,128)} %get-tuple-element.113), channel_id=1, source_target_pairs={{0,16},{16,0},{1,17},{17,1},{2,18},{18,2},{3,19},{19,3},{4,20},{20... | collective-permute-start | bytes 2752520 | tf_op jit(solution)/shard_map/ppermute | solution.py:161
  761.9 45.2 %table_update.1 = (f32[64,50304]{1,0:T(8,128)}, f32[64,50304]{1,0:T(8,128)}, f32[64,50304]{1,0:T(8,128)}, f32[64,50304]{1,0:T(8,128)}) custom-call(f32[1,1]{1,0:T(1,128)} %bitcast.107.factor_ref, f32[64,50304]{1,0:T(8,128)} %table_ref.3, f32[64,50304]{1,0:T(8,128)} %moment_ref.1, f32[64,50304]{1,0:T(8,128)} %second_ref.1, f32[64,50304]{1,0:T(8,128)} %average_ref.1, ...), custom_call_target="tpu_custom_call" | custom-call | tf_op jit(solution)/shard_map/table_update/pallas_call | solution.py:749
  (915 shorter events, 466.4 us)
Async XLA Ops:
  7.2 173.5 %all-gather.6.cloned.1.call-start = ((), (), s32[]{:S(2)}) async-start(), calls=%async_computation.1 | async-start | bytes 15138816 | tf_op jit(solution)/shard_map/all_gather | solution.py:809
  11.9 305.6 %all-gather.10.cloned.1.call-start = ((), (), s32[]{:S(2)}) async-start(), calls=%async_computation.3 | async-start | bytes 8650752 | tf_op jit(solution)/shard_map/all_gather | solution.py:810
  12.7 314.0 %all-gather.8.cloned.1.call-start = ((), (), s32[]{:S(2)}) async-start(), calls=%async_computation.2 | async-start | bytes 10813440 | tf_op jit(solution)/shard_map/all_gather | solution.py:811
  20.4 699.1 %all-gather.12.cloned.1.call-start = ((), (), s32[]{:S(2)}) async-start(), calls=%async_computation.5 | async-start | bytes 3514368 | tf_op jit(solution)/shard_map/all_gather | solution.py:934
  86.8 19.4 %collective-permute-start.10 = (bf16[160,1024]{1,0:T(8,128)(2,1)}, bf16[160,1024]{1,0:T(8,128)(2,1)S(1)}, u32[]{:S(2)}, u32[]{:S(2)}) collective-permute-start(bf16[160,1024]{1,0:T(8,128)(2,1)} %behind.61), channel_id=1, source_target_pairs={{0,4},{1,5},{2,6},{3,7},{4,8},{5,9},{6,10},{7,11},{8,12},{9,13},{1... | collective-permute-start | bytes 983048 | tf_op jit(solution)/shard_map/ppermute | solution.py:155
  110.6 23.7 %collective-permute-start.12 = (bf16[160,1024]{1,0:T(8,128)(2,1)}, bf16[160,1024]{1,0:T(8,128)(2,1)S(1)}, u32[]{:S(2)}, u32[]{:S(2)}) collective-permute-start(bf16[160,1024]{1,0:T(8,128)(2,1)} %behind.63), channel_id=1, source_target_pairs={{0,4},{1,5},{2,6},{3,7},{4,8},{5,9},{6,10},{7,11},{8,12},{9,13},{1... | collective-permute-start | bytes 983048 | tf_op jit(solution)/shard_map/ppermute | solution.py:155
  160.0 33.1 %collective-permute-start.17 = (bf16[4,160,1024]{2,1,0:T(8,128)(2,1)}, bf16[4,160,1024]{2,1,0:T(8,128)(2,1)}, u32[]{:S(2)}, u32[]{:S(2)}) collective-permute-start(bf16[4,160,1024]{2,1,0:T(8,128)(2,1)} %behind.66.refs_0_), channel_id=1, source_target_pairs={{0,16},{16,0},{1,17},{17,1},{2,18},{18,2},{3,19},{19,3},{4,20},{20... | collective-permute-start | bytes 3932168 | tf_op jit(solution)/shard_map/ppermute | solution.py:161
  160.0 35.2 %collective-permute-start.18 = (bf16[4,160,1024]{2,1,0:T(8,128)(2,1)}, bf16[4,160,1024]{2,1,0:T(8,128)(2,1)S(1)}, u32[]{:S(2)}, u32[]{:S(2)}) collective-permute-start(bf16[4,160,1024]{2,1,0:T(8,128)(2,1)} %behind.66.refs_0_), channel_id=1, source_target_pairs={{0,2},{1,3},{2,0},{3,1},{4,6},{5,7},{6,4},{7,5},{8,10},{9,11},{10,... | collective-permute-start | bytes 3932168 | tf_op jit(solution)/shard_map/ppermute | solution.py:155
  160.6 41.2 %collective-permute-start.19 = (bf16[4,160,1024]{2,1,0:T(8,128)(2,1)}, bf16[4,160,1024]{2,1,0:T(8,128)(2,1)S(1)}, u32[]{:S(2)}, u32[]{:S(2)}) collective-permute-start(bf16[4,160,1024]{2,1,0:T(8,128)(2,1)} %behind.66.refs_0_), channel_id=1, source_target_pairs={{0,1},{1,0},{2,3},{3,2},{4,5},{5,4},{6,7},{7,6},{8,9},{9,8},{10,11... | collective-permute-start | bytes 3932168 | tf_op jit(solution)/shard_map/ppermute | solution.py:155
  203.4 22.5 %collective-permute-start.23 = (bf16[4,160,1024]{2,1,0:T(8,128)(2,1)}, bf16[4,160,1024]{2,1,0:T(8,128)(2,1)S(1)}, u32[]{:S(2)}, u32[]{:S(2)}) collective-permute-start(bf16[4,160,1024]{2,1,0:T(8,128)(2,1)} %behind.69.refs_4_), channel_id=1, source_target_pairs={{0,2},{1,3},{2,0},{3,1},{4,6},{5,7},{6,4},{7,5},{8,10},{9,11},{10,... | collective-permute-start | bytes 3932168 | tf_op jit(solution)/shard_map/ppermute | solution.py:155
  203.4 22.5 %collective-permute-start.22 = (bf16[4,160,1024]{2,1,0:T(8,128)(2,1)}, bf16[4,160,1024]{2,1,0:T(8,128)(2,1)S(1)}, u32[]{:S(2)}, u32[]{:S(2)}) collective-permute-start(bf16[4,160,1024]{2,1,0:T(8,128)(2,1)} %behind.69.refs_4_), channel_id=1, source_target_pairs={{0,16},{16,0},{1,17},{17,1},{2,18},{18,2},{3,19},{19,3},{4,20},{20... | collective-permute-start | bytes 3932168 | tf_op jit(solution)/shard_map/ppermute | solution.py:161
  203.4 22.5 %collective-permute-start.21 = (bf16[4,160,1024]{2,1,0:T(8,128)(2,1)}, bf16[4,160,1024]{2,1,0:T(8,128)(2,1)}, u32[]{:S(2)}, u32[]{:S(2)}) collective-permute-start(bf16[4,160,1024]{2,1,0:T(8,128)(2,1)} %behind.68.refs_2_), channel_id=1, source_target_pairs={{0,16},{16,0},{1,17},{17,1},{2,18},{18,2},{3,19},{19,3},{4,20},{20... | collective-permute-start | bytes 3932168 | tf_op jit(solution)/shard_map/ppermute | solution.py:161
  244.3 21.4 %collective-permute-start.27 = (bf16[4,32,3072]{2,1,0:T(8,128)(2,1)}, bf16[4,32,3072]{2,1,0:T(8,128)(2,1)}, u32[]{:S(2)}, u32[]{:S(2)}) collective-permute-start(bf16[4,32,3072]{2,1,0:T(8,128)(2,1)} %behind.75.refs_0_), channel_id=1, source_target_pairs={{0,1},{1,0},{2,3},{3,2},{4,5},{5,4},{6,7},{7,6},{8,9},{9,8},{10,11... | collective-permute-start | bytes 2359304 | tf_op jit(solution)/shard_map/ppermute | solution.py:155
  244.6 21.1 %collective-permute-start.28 = (bf16[4,32,3072]{2,1,0:T(8,128)(2,1)}, bf16[4,32,3072]{2,1,0:T(8,128)(2,1)}, u32[]{:S(2)}, u32[]{:S(2)}) collective-permute-start(bf16[4,32,3072]{2,1,0:T(8,128)(2,1)} %behind.75.refs_0_), channel_id=1, source_target_pairs={{0,16},{16,0},{1,17},{17,1},{2,18},{18,2},{3,19},{19,3},{4,20},{20... | collective-permute-start | bytes 2359304 | tf_op jit(solution)/shard_map/ppermute | solution.py:161
  245.2 20.4 %collective-permute-start.29 = (bf16[4,32,3072]{2,1,0:T(8,128)(2,1)}, bf16[4,32,3072]{2,1,0:T(8,128)(2,1)S(1)}, u32[]{:S(2)}, u32[]{:S(2)}) collective-permute-start(bf16[4,32,3072]{2,1,0:T(8,128)(2,1)} %behind.75.refs_0_), channel_id=1, source_target_pairs={{0,2},{1,3},{2,0},{3,1},{4,6},{5,7},{6,4},{7,5},{8,10},{9,11},{10,... | collective-permute-start | bytes 2359304 | tf_op jit(solution)/shard_map/ppermute | solution.py:155
  350.4 24.1 %collective-permute-start.35 = (bf16[224,2048]{1,0:T(8,128)(2,1)}, bf16[224,2048]{1,0:T(8,128)(2,1)}, u32[]{:S(2)}, u32[]{:S(2)}) collective-permute-start(bf16[224,2048]{1,0:T(8,128)(2,1)} %pad_maximum_fusion.3), channel_id=1, source_target_pairs={{0,16},{16,0},{1,17},{17,1},{2,18},{18,2},{3,19},{19,3},{4,20},{20... | collective-permute-start | bytes 2752520 | tf_op jit(solution)/shard_map/ppermute | solution.py:161
  358.8 368.5 %reduce-scatter.2.cloned.1.call-start = ((), (), s32[]{:S(2)}) async-start(), calls=%async_computation.4 | async-start | bytes 10813440 | tf_op jit(solution)/shard_map/reduce_scatter | solution.py:944
  390.3 31.8 %collective-permute-start.39 = (bf16[224,4096]{1,0:T(8,128)(2,1)}, bf16[224,4096]{1,0:T(8,128)(2,1)}, u32[]{:S(2)}, u32[]{:S(2)}) collective-permute-start(bf16[224,4096]{1,0:T(8,128)(2,1)} %get-tuple-element.213), channel_id=1, source_target_pairs={{0,16},{16,0},{1,17},{17,1},{2,18},{18,2},{3,19},{19,3},{4,20},{20... | collective-permute-start | bytes 5505032 | tf_op jit(solution)/shard_map/ppermute | solution.py:161
  398.3 21.3 %collective-permute-start.37 = (bf16[4,32,2048]{2,1,0:T(8,128)(2,1)}, bf16[4,32,2048]{2,1,0:T(8,128)(2,1)}, u32[]{:S(2)}, u32[]{:S(2)}) collective-permute-start(bf16[4,32,2048]{2,1,0:T(8,128)(2,1)} %behind.83), channel_id=1, source_target_pairs={{0,1},{1,0},{2,3},{3,2},{4,5},{5,4},{6,7},{7,6},{8,9},{9,8},{10,11... | collective-permute-start | bytes 1572872 | tf_op jit(solution)/shard_map/ppermute | solution.py:155
  435.2 19.0 %collective-permute-start.40 = (bf16[32,2048]{1,0:T(8,128)(2,1)}, bf16[32,2048]{1,0:T(8,128)(2,1)}, u32[]{:S(2)}, u32[]{:S(2)}) collective-permute-start(bf16[32,2048]{1,0:T(8,128)(2,1)} %behind.86), channel_id=1, source_target_pairs={{0,4},{1,5},{2,6},{3,7},{4,8},{5,9},{6,10},{7,11},{8,12},{9,13},{1... | collective-permute-start | bytes 393224 | tf_op jit(solution)/shard_map/ppermute | solution.py:155
  436.9 38.8 %collective-permute-start.44 = (bf16[224,3072]{1,0:T(8,128)(2,1)}, bf16[224,3072]{1,0:T(8,128)(2,1)}, u32[]{:S(2)}, u32[]{:S(2)}) collective-permute-start(bf16[224,3072]{1,0:T(8,128)(2,1)} %behind.85), channel_id=1, source_target_pairs={{0,16},{16,0},{1,17},{17,1},{2,18},{18,2},{3,19},{19,3},{4,20},{20... | collective-permute-start | bytes 4128776 | tf_op jit(solution)/shard_map/ppermute | solution.py:161
  500.7 83.2 %collective-permute-start.52 = (bf16[2,4,32,7168]{3,2,1,0:T(8,128)(2,1)}, bf16[2,4,32,7168]{3,2,1,0:T(8,128)(2,1)}, u32[]{:S(2)}, u32[]{:S(2)}) collective-permute-start(bf16[2,4,32,7168]{3,2,1,0:T(8,128)(2,1)} %behind.97), channel_id=1, source_target_pairs={{0,2},{1,3},{2,0},{3,1},{4,6},{5,7},{6,4},{7,5},{8,10},{9,11},{10,... | collective-permute-start | bytes 11010056 | tf_op jit(solution)/shard_map/ppermute | solution.py:155
  592.8 23.5 %collective-permute-start.55 = (bf16[4,32,7168]{2,1,0:T(8,128)(2,1)}, bf16[4,32,7168]{2,1,0:T(8,128)(2,1)}, u32[]{:S(2)}, u32[]{:S(2)}) collective-permute-start(bf16[4,32,7168]{2,1,0:T(8,128)(2,1)} %behind.100), channel_id=1, source_target_pairs={{0,1},{1,0},{2,3},{3,2},{4,5},{5,4},{6,7},{7,6},{8,9},{9,8},{10,11... | collective-permute-start | bytes 5505032 | tf_op jit(solution)/shard_map/ppermute | solution.py:155
  666.3 67.4 %collective-permute-start.61 = (f32[32,7168]{1,0:T(8,128)}, f32[32,7168]{1,0:T(8,128)}, u32[]{:S(2)}, u32[]{:S(2)}) collective-permute-start(f32[32,7168]{1,0:T(8,128)} %get-tuple-element.113), channel_id=1, source_target_pairs={{0,16},{16,0},{1,17},{17,1},{2,18},{18,2},{3,19},{19,3},{4,20},{20... | collective-permute-start | bytes 2752520 | tf_op jit(solution)/shard_map/ppermute | solution.py:161
  (237 other events, 1855.3 us)
Sparse Core Ops, SparseCore 0:
  12.1 124.4 all-gather.5
  139.4 91.8 all-gather.9
  234.2 92.5 all-gather.7
  358.9 61.6 all-gather.11
  423.3 158.3 reduce-scatter.1
